TPU v7x, 128 devices: a whole 4x4x4 slice. The times are simulated.
128 devices in a mesh: dp: 8 (over z, y_lo), expert: 16 (over x, y_hi, core).
Axes of the slice: x: 4, y: 4 (y_hi: 2, y_lo: 2; y = y_hi * 2 + y_lo), z: 4, core: 2. Of those that a mesh axis runs over, the one named last changes fastest.
Arguments:
- tokens: bfloat16 [32768, 2048], P(('dp', 'expert')), may hold values from -6 to 6
- out_grad: bfloat16 [32768, 2048], P(('dp', 'expert')), may hold values from -6 to 6
- expert_ids: int32 [32768, 2], P(('dp', 'expert')), may hold values from 0 to 15, all different within a row; in each aligned block of 256 rows (0 to 255, 256 to 511, ...) at most 48 rows name the same one
- gate_values: bfloat16 [32768, 2], P(('dp', 'expert')), may hold values from 0.049804688 to 0.59765625
- master_gate_up: float32 [16, 2048, 1536], P('expert', 'dp'), may hold values from -4 to 4
- master_down: float32 [16, 768, 2048], P('expert', 'dp'), may hold values from -4 to 4
- moment_gate_up: float32 [16, 2048, 1536], P('expert', 'dp'), may hold values from -4 to 4
- moment_down: float32 [16, 768, 2048], P('expert', 'dp'), may hold values from -4 to 4
- second_gate_up: float32 [16, 2048, 1536], P('expert', 'dp'), may hold values from 0.003 to 0.006
- second_down: float32 [16, 768, 2048], P('expert', 'dp'), may hold values from 0.003 to 0.006
Outputs:
- input_grad: bfloat16 [32768, 2048], P(('dp', 'expert'))
- gate_grad: bfloat16 [32768, 2], P(('dp', 'expert'))
- new_gate_up: bfloat16 [16, 2048, 1536], P('expert')
- new_down: bfloat16 [16, 768, 2048], P('expert')
- master_gate_up_next: float32 [16, 2048, 1536], P('expert', 'dp')
- master_down_next: float32 [16, 768, 2048], P('expert', 'dp')
- moment_gate_up_next: float32 [16, 2048, 1536], P('expert', 'dp')
- moment_down_next: float32 [16, 768, 2048], P('expert', 'dp')
- second_gate_up_next: float32 [16, 2048, 1536], P('expert', 'dp')
- second_down_next: float32 [16, 768, 2048], P('expert', 'dp')
Inputs may be any that keep to these rules, and one draw needn't show every extreme that they name: `expert_ids`: each token names 2 different experts. Among the rows of one device at most 48 routes name one expert, and in every draw some expert receives exactly 48 routes from some device.
All inputs are finite; a program needn't handle non-finite values.
Results may differ from a plain program's by a relative error of at most 0.028.
Values may be sent and summed in bfloat16 or wider, within the bound.
No kernel may reach another device: no remote copies, remote signals or barrier semaphores. Data moves between devices by JAX's collectives and lax.ppermute only.
A program may use at most 128 MiB of HBM per device.

v0:
```python
import jax
import jax.numpy as jnp
from jax import lax
from jax.sharding import PartitionSpec as P

beta_first = 0.9
beta_second = 0.95
learn_rate = 0.01
weight_decay = 0.1
adam_epsilon = 1e-08
bias_first = 0.9999734386
bias_second = 0.9940794708


def expert_rows(in_rows, grad_rows, gate_rows, w_gate_up, w_down):
    hidden = w_down.shape[0]
    scale_in = in_rows.shape[1] ** (-0.5)
    scale_out = hidden ** (-0.5)
    projected = scale_in * jnp.dot(in_rows, w_gate_up, preferred_element_type=jnp.float32)
    gate_part = projected[:, :hidden]
    up_part = projected[:, hidden:]
    sig_gate = jax.nn.sigmoid(gate_part)
    swish_gate = gate_part * sig_gate
    hidden_act = (swish_gate * up_part).astype(jnp.bfloat16)
    expert_out = scale_out * jnp.dot(hidden_act, w_down, preferred_element_type=jnp.float32)
    gate_score = jnp.sum(grad_rows.astype(jnp.float32) * expert_out, axis=1).astype(jnp.bfloat16)
    scaled = (gate_rows.astype(jnp.float32)[:, None] * grad_rows.astype(jnp.float32)).astype(
        jnp.bfloat16
    )
    grad_act = scale_out * lax.dot_general(
        scaled, w_down, (((1,), (1,)), ((), ())), preferred_element_type=jnp.float32
    )
    grad_gate = grad_act * up_part * sig_gate * (1.0 + gate_part * (1.0 - sig_gate))
    grad_up = grad_act * swish_gate
    grad_proj = jnp.concatenate([grad_gate, grad_up], axis=1).astype(jnp.bfloat16)
    grad_route = (
        scale_in
        * lax.dot_general(
            grad_proj, w_gate_up, (((1,), (1,)), ((), ())), preferred_element_type=jnp.float32
        )
    ).astype(jnp.bfloat16)
    return (hidden_act, scaled, grad_proj, grad_route, gate_score)


def adam_update(master, moment, second, grad):
    moment_next = beta_first * moment + (1.0 - beta_first) * grad
    second_next = beta_second * second + (1.0 - beta_second) * grad * grad
    step_size = moment_next / bias_first / (jnp.sqrt(second_next / bias_second) + adam_epsilon)
    master_next = master - learn_rate * (step_size + weight_decay * master)
    return (master_next, moment_next, second_next)


def local(
    tokens,
    out_grad,
    expert_ids,
    gate_values,
    master_gate_up,
    master_down,
    moment_gate_up,
    moment_down,
    second_gate_up,
    second_down,
):
    experts = lax.axis_size("expert")
    replicas = lax.axis_size("dp")
    tok_count, model_width = tokens.shape
    top_count = expert_ids.shape[1]
    hidden = master_down.shape[1] * replicas
    capacity = 3 * tok_count * top_count // (2 * experts)
    route_count = tok_count * top_count
    scale_in = model_width ** (-0.5)
    scale_out = hidden ** (-0.5)
    w_gate_up, w_down = (
        lax.all_gather(master_gate_up[0].astype(jnp.bfloat16), "dp", axis=0, tiled=True),
        lax.all_gather(master_down[0].astype(jnp.bfloat16), "dp", axis=0, tiled=True),
    )
    route_ids = expert_ids.reshape(route_count)
    onehot = (route_ids[:, None] == jnp.arange(experts, dtype=jnp.int32)[None, :]).astype(jnp.int32)
    before = jnp.cumsum(onehot, axis=0) - onehot
    slot_index = jnp.sum(before * onehot, axis=1)
    position = route_ids * capacity + slot_index
    anchor = (
        jnp.full((experts * capacity,), route_count, jnp.int32)
        .at[position]
        .set(jnp.arange(route_count, dtype=jnp.int32))
    )
    source_tok = anchor // top_count
    padded_in = jnp.concatenate([tokens, jnp.zeros((1, model_width), tokens.dtype)], axis=0)
    padded_grad = jnp.concatenate([out_grad, jnp.zeros((1, model_width), out_grad.dtype)], axis=0)
    padded_gate = jnp.concatenate(
        [gate_values.reshape(route_count), jnp.zeros((1,), gate_values.dtype)], axis=0
    )
    send_in = padded_in[source_tok].reshape(experts, capacity, model_width)
    send_grad = padded_grad[source_tok].reshape(experts, capacity, model_width)
    send_gate = padded_gate[anchor].reshape(experts, capacity)
    in_block = lax.all_to_all(send_in, "expert", split_axis=0, concat_axis=0, tiled=True)
    grad_block = lax.all_to_all(send_grad, "expert", split_axis=0, concat_axis=0, tiled=True)
    gate_block = lax.all_to_all(send_gate, "expert", split_axis=0, concat_axis=0, tiled=True)
    sources, item_count = gate_block.shape
    flat_rows = sources * item_count
    hidden_act, scaled, grad_proj, grad_route, gate_score = expert_rows(
        in_block.reshape(flat_rows, model_width),
        grad_block.reshape(flat_rows, model_width),
        gate_block.reshape(flat_rows),
        w_gate_up,
        w_down,
    )
    returned = (
        grad_route.reshape(sources, item_count, model_width),
        gate_score.reshape(sources, item_count),
    )
    in_recv, act_recv, scaled_recv, proj_recv, grad_back, score_back = (
        in_block,
        hidden_act.reshape(sources, item_count, hidden),
        scaled.reshape(sources, item_count, model_width),
        grad_proj.reshape(sources, item_count, 2 * hidden),
    ) + returned
    grad_back, score_back = (
        lax.all_to_all(grad_back, "expert", split_axis=0, concat_axis=0, tiled=True),
        lax.all_to_all(score_back, "expert", split_axis=0, concat_axis=0, tiled=True),
    )
    route_grads = grad_back.reshape(experts * capacity, model_width)[position].reshape(
        tok_count, top_count, model_width
    )
    input_grad = jnp.sum(route_grads.astype(jnp.float32), axis=1).astype(jnp.bfloat16)
    gate_grad = score_back.reshape(experts * capacity)[position].reshape(tok_count, top_count)
    rows_in = in_recv.reshape(-1, model_width)
    rows_act = act_recv.reshape(-1, hidden)
    rows_scaled = scaled_recv.reshape(-1, model_width)
    rows_proj = proj_recv.reshape(-1, 2 * hidden)
    contract_rows = (((0,), (0,)), ((), ()))
    full_down = scale_out * lax.dot_general(
        rows_act, rows_scaled, contract_rows, preferred_element_type=jnp.float32
    )
    full_gate_up = scale_in * lax.dot_general(
        rows_in, rows_proj, contract_rows, preferred_element_type=jnp.float32
    )
    grad_gate_up, grad_down = (
        lax.psum_scatter(
            full_gate_up.astype(jnp.bfloat16), "dp", scatter_dimension=0, tiled=True
        ).astype(jnp.float32),
        lax.psum_scatter(
            full_down.astype(jnp.bfloat16), "dp", scatter_dimension=0, tiled=True
        ).astype(jnp.float32),
    )
    master_gu_next, moment_gu_next, second_gu_next = adam_update(
        master_gate_up[0], moment_gate_up[0], second_gate_up[0], grad_gate_up
    )
    master_dn_next, moment_dn_next, second_dn_next = adam_update(
        master_down[0], moment_down[0], second_down[0], grad_down
    )
    new_gate_up, new_down = (
        lax.all_gather(master_gu_next.astype(jnp.bfloat16), "dp", axis=0, tiled=True),
        lax.all_gather(master_dn_next.astype(jnp.bfloat16), "dp", axis=0, tiled=True),
    )
    return (
        input_grad,
        gate_grad,
        new_gate_up[None],
        new_down[None],
        master_gu_next[None],
        master_dn_next[None],
        moment_gu_next[None],
        moment_dn_next[None],
        second_gu_next[None],
        second_dn_next[None],
    )


def solution(mesh):
    placed = (
        P(("dp", "expert"), None),
        P(("dp", "expert"), None),
        P(("dp", "expert"), None),
        P(("dp", "expert"), None),
        P("expert", "dp", None),
        P("expert", "dp", None),
        P("expert", "dp", None),
        P("expert", "dp", None),
        P("expert", "dp", None),
        P("expert", "dp", None),
    )
    return jax.shard_map(
        local,
        mesh=mesh,
        in_specs=placed,
        out_specs=(
            P(("dp", "expert"), None),
            P(("dp", "expert"), None),
            P("expert", None, None),
            P("expert", None, None),
            P("expert", "dp", None),
            P("expert", "dp", None),
            P("expert", "dp", None),
            P("expert", "dp", None),
            P("expert", "dp", None),
            P("expert", "dp", None),
        ),
        check_vma=False,
    )
```

profile of v0, /device:TPU:4, one launch (start us, length us, event | category | flops | bytes accessed | tf_op | source)
XLA Modules:
  0.0 755.8 jit_solution(6685142565843695377)
XLA Ops:
  7.2 0.0 all-gather.7.cloned.1.call-start
  7.2 2.4 bitcast_convert_fusion
  9.6 0.0 all-gather.7.cloned.1.call-update
  9.6 0.1 copy.30
  9.8 0.1 eq.25
  9.9 0.1 eq.29
  10.1 0.1 copy.29
  10.2 0.1 mul.161
  10.4 1.2 reduce-window.6
  11.5 0.2 slice_reduce_fusion
  11.8 0.1 copy.28
  12.0 0.2 reshape.134
  12.1 0.1 fusion.17
  12.2 2.4 scatter_custom_fusion
  14.7 5.0 gather_fusion
  19.7 0.7 all_to_all.25
  20.4 7.5 all-to-all-start
  27.9 0.1 concatenate.14
  28.0 4.2 gather_fusion.1
  32.2 0.9 all-to-all-done
  33.1 6.8 all-to-all-start.1
  39.9 0.0 all-gather.5.cloned.1.call-start
  39.9 0.8 bitcast_convert_fusion.1
  40.7 0.1 concatenate.15
  40.9 4.2 gather_fusion.2
  45.1 41.0 %all-to-all-done.1 = bf16[16,48,2048]{2,1,0:T(8,128)(2,1)} async-done(((bf16[16,48,2048]{2,1,0:T(8,128)(2,1)}), bf16[16,48,2048]{2,1,0:T(8,128)(2,1)}, u32[]{:S(2)}, u32[]{:S(2)}) %all-to-all-start.1) | async-done | bytes 3145760 | tf_op jit(solution)/shard_map/all_to_all | solution.py:98
  86.1 5.3 all-to-all-start.2
  91.4 0.2 reduce-scatter.5.cloned.1.call-start
  91.7 0.1 reshape.144
  91.8 4.2 fusion
  96.0 41.5 %all-to-all-done.2 = bf16[16,48,2048]{2,1,0:T(8,128)(2,1)S(1)} async-done(((bf16[16,48,2048]{2,1,0:T(8,128)(2,1)}), bf16[16,48,2048]{2,1,0:T(8,128)(2,1)S(1)}, u32[]{:S(2)}, u32[]{:S(2)}) %all-to-all-start.2) | async-done | bytes 3145760 | tf_op jit(solution)/shard_map/all_to_all | solution.py:97
  137.5 72.2 %all-gather.7.cloned.1.call-done = bf16[2048,1536]{1,0:T(8,128)(2,1)} async-done(((bf16[256,1536]{1,0:T(8,128)(2,1)}), bf16[2048,1536]{1,0:T(8,128)(2,1)}) %all-gather.7.cloned.1.call-update) | async-done | bytes 6291472 | tf_op jit(solution)/shard_map/all_gather | solution.py:75
  209.7 8.6 %convolution_multiply_fusion = f32[768,1536]{0,1:T(8,128)} fusion(bf16[768,2048]{1,0:T(8,128)(2,1)S(1)} %bitcast.106, bf16[2048,1536]{1,0:T(8,128)(2,1)} %all-gather.7.cloned.1.call-done), kind=kOutput, calls=%fused_computation.13 | convolution fusion | flops 4833017856 | bytes 14155776 | tf_op jit(solution)/shard_map/dot_general | solution.py:19
  218.3 65.8 %all-gather.5.cloned.1.call-done = bf16[768,2048]{1,0:T(8,128)(2,1)} async-done(((bf16[96,2048]{1,0:T(8,128)(2,1)}), bf16[768,2048]{1,0:T(8,128)(2,1)}) %all-gather.5.cloned.1.call-update) | async-done | bytes 3145744 | tf_op jit(solution)/shard_map/all_gather | solution.py:76
  284.1 9.2 %multiply_convert_fusion.5 = (bf16[768,768]{0,1:T(8,128)(2,1)}, bf16[768,768]{0,1:T(8,128)(2,1)}, bf16[768,768]{0,1:T(8,128)(2,1)S(1)}) fusion(f32[768,1536]{0,1:T(8,128)} %convolution_multiply_fusion, bf16[768,2048]{1,0:T(8,128)(2,1)} %fusion, bf16[768,2048]{1,0:T(8,128)(2,1)} %all-gather.5.cloned.1.call-done), kind=kOutput, calls=%fused_computation.18 | convolution fusion | flops 2425356288 | bytes 14548992 | tf_op jit(solution)/shard_map/dot_general | solution.py:30
  293.3 1.1 copy-done.10
  294.4 3.9 multiply_convert_fusion.1
  298.4 0.0 reduce-scatter.3.cloned.1.call-start
  298.4 8.7 %multiply_convert_fusion = bf16[2048,1536]{1,0:T(8,128)(2,1)} fusion(bf16[768,2048]{1,0:T(8,128)(2,1)S(1)} %bitcast.107, bf16[768,768]{0,1:T(8,128)(2,1)} %get-tuple-element.35, bf16[768,768]{0,1:T(8,128)(2,1)} %get-tuple-element.34), kind=kOutput, calls=%fused_computation.6 | convolution fusion | flops 4842848256 | bytes 11796480 | tf_op jit(solution)/shard_map/dot_general | solution.py:136
  307.1 0.0 all-gather.11.cloned.1.call-start
  307.2 62.8 %reduce-scatter.5.cloned.1.call-done = bf16[96,2048]{1,0:T(8,128)(2,1)} async-done(((bf16[768,2048]{1,0:T(8,128)(2,1)}), bf16[96,2048]{1,0:T(8,128)(2,1)}) %reduce-scatter.5.cloned.1.call-update) | async-done | bytes 393232 | tf_op jit(solution)/shard_map/reduce_scatter | solution.py:143
  370.1 3.4 fusion.25
  373.5 0.0 all-gather.11.cloned.1.call-update
  373.5 0.3 all-gather.9.cloned.1.call-start
  373.8 128.8 %reduce-scatter.3.cloned.1.call-done = bf16[256,1536]{1,0:T(8,128)(2,1)} async-done(((bf16[2048,1536]{1,0:T(8,128)(2,1)}), bf16[256,1536]{1,0:T(8,128)(2,1)}) %reduce-scatter.3.cloned.1.call-update) | async-done | bytes 786448 | tf_op jit(solution)/shard_map/reduce_scatter | solution.py:140
  502.6 5.8 fusion.26
  508.4 0.0 all-gather.9.cloned.1.call-update
  508.4 5.8 fusion.1
  514.2 0.7 convert_element_type.95
  514.9 7.0 all-to-all-start.4
  521.9 8.7 %multiply_convert_fusion.2 = bf16[768,2048]{1,0:T(8,128)(2,1)} fusion(bf16[2048,1536]{1,0:T(8,128)(2,1)} %all-gather.7.cloned.1.call-done, bf16[768,768]{0,1:T(8,128)(2,1)} %get-tuple-element.35, bf16[768,768]{0,1:T(8,128)(2,1)S(1)} %copy-done.12), kind=kOutput, calls=%fused_computation.12 | convolution fusion | flops 4839702528 | bytes 11796480 | tf_op jit(solution)/shard_map/dot_general | solution.py:38
  530.6 7.2 all-to-all-start.3
  537.9 0.1 reshape.142
  538.0 3.5 gather_fusion.4
  541.5 0.2 reshape.143
  541.7 0.7 copy.36
  542.3 41.6 %all-to-all-done.3 = bf16[16,48,2048]{2,1,0:T(8,128)(2,1)S(1)} async-done(((bf16[16,48,2048]{2,1,0:T(8,128)(2,1)}), bf16[16,48,2048]{2,1,0:T(8,128)(2,1)S(1)}, u32[]{:S(2)}, u32[]{:S(2)}) %all-to-all-start.3) | async-done | bytes 3145760 | tf_op jit(solution)/shard_map/all_to_all | solution.py:120
  583.9 3.3 gather_fusion.3
  587.2 3.2 reshape.141
  590.4 6.7 reduce_sum.34
  597.1 13.0 %all-gather.11.cloned.1.call-done = bf16[768,2048]{1,0:T(8,128)(2,1)} async-done(((bf16[96,2048]{1,0:T(8,128)(2,1)}), bf16[768,2048]{1,0:T(8,128)(2,1)}) %all-gather.11.cloned.1.call-update) | async-done | bytes 3145744 | tf_op jit(solution)/shard_map/all_gather | solution.py:155
  610.1 131.1 %all-gather.9.cloned.1.call-done = bf16[2048,1536]{1,0:T(8,128)(2,1)} async-done(((bf16[256,1536]{1,0:T(8,128)(2,1)}), bf16[2048,1536]{1,0:T(8,128)(2,1)}) %all-gather.9.cloned.1.call-update) | async-done | bytes 6291472 | tf_op jit(solution)/shard_map/all_gather | solution.py:154
  741.2 6.0 copy.42
  747.3 1.7 copy.43
  (41 shorter events, 0.3 us)
Async XLA Ops:
  7.2 2.5 copy-start.8
  7.2 4.6 copy-start.9
  7.2 202.5 %all-gather.7.cloned.1.call-start = ((), (), s32[]{:S(2)}) async-start(), calls=%async_computation.8 | async-start | bytes 7077888 | tf_op jit(solution)/shard_map/all_gather | solution.py:75
  9.6 18.3 %copy-start.5 = (bf16[256,2048]{1,0:T(8,128)(2,1)S(1)}, bf16[256,2048]{1,0:T(8,128)(2,1)}, u32[]{:S(2)}) copy-start(bf16[256,2048]{1,0:T(8,128)(2,1)} %param.11) | copy-start | bytes 3145732
  20.4 12.7 %all-to-all-start = ((bf16[16,1,48]{2,1,0:T(2,128)(2,1)}), bf16[16,1,48]{2,1,0:T(2,128)(2,1)S(1)}, u32[]{:S(2)}, u32[]{:S(2)}) async-start(bf16[16,1,48]{2,1,0:T(2,128)(2,1)} %all_to_all.25), calls=%async_computation | async-start | bytes 16384 | tf_op jit(solution)/shard_map/all_to_all | solution.py:99
  33.1 6.8 copy-start.3
  33.1 7.6 %copy-start.6 = (bf16[256,2048]{1,0:T(8,128)(2,1)S(1)}, bf16[256,2048]{1,0:T(8,128)(2,1)}, u32[]{:S(2)}) copy-start(bf16[256,2048]{1,0:T(8,128)(2,1)} %param.10) | copy-start | bytes 3145732
  33.1 53.0 %all-to-all-start.1 = ((bf16[16,48,2048]{2,1,0:T(8,128)(2,1)}), bf16[16,48,2048]{2,1,0:T(8,128)(2,1)}, u32[]{:S(2)}, u32[]{:S(2)}) async-start(bf16[16,48,2048]{2,1,0:T(8,128)(2,1)} %bitcast.102), calls=%async_computation.1 | async-start | bytes 6291456 | tf_op jit(solution)/shard_map/all_to_all | solution.py:98
  39.9 244.2 %all-gather.5.cloned.1.call-start = ((), (), s32[]{:S(2)}) async-start(), calls=%async_computation.7 | async-start | bytes 3538944 | tf_op jit(solution)/shard_map/all_gather | solution.py:76
  86.1 51.4 %all-to-all-start.2 = ((bf16[16,48,2048]{2,1,0:T(8,128)(2,1)}), bf16[16,48,2048]{2,1,0:T(8,128)(2,1)S(1)}, u32[]{:S(2)}, u32[]{:S(2)}) async-start(bf16[16,48,2048]{2,1,0:T(8,128)(2,1)} %bitcast.103), calls=%async_computation.2 | async-start | bytes 6291456 | tf_op jit(solution)/shard_map/all_to_all | solution.py:97
  91.4 278.6 %reduce-scatter.5.cloned.1.call-start = ((), (), s32[]{:S(2)}) async-start(), calls=%async_computation.11 | async-start | bytes 3538944 | tf_op jit(solution)/shard_map/reduce_scatter | solution.py:143
  284.1 10.3 %copy-start.2 = (bf16[768,2048]{1,0:T(8,128)(2,1)S(1)}, bf16[768,2048]{1,0:T(8,128)(2,1)}, u32[]{:S(2)}) copy-start(bf16[768,2048]{1,0:T(8,128)(2,1)} %fusion) | copy-start | bytes 9437188
  293.3 1.1 copy-start.10
  298.4 204.2 %reduce-scatter.3.cloned.1.call-start = ((), (), s32[]{:S(2)}) async-start(), calls=%async_computation.9 | async-start | bytes 7077888 | tf_op jit(solution)/shard_map/reduce_scatter | solution.py:140
  307.1 62.9 %copy-start.4 = (f32[1,96,2048]{2,1,0:T(8,128)S(1)}, f32[1,96,2048]{2,1,0:T(8,128)}, u32[]{:S(2)}) copy-start(f32[1,96,2048]{2,1,0:T(8,128)} %param.15) | copy-start | bytes 2359300
  307.1 62.9 %copy-start.7 = (f32[1,96,2048]{2,1,0:T(8,128)S(1)}, f32[1,96,2048]{2,1,0:T(8,128)}, u32[]{:S(2)}) copy-start(f32[1,96,2048]{2,1,0:T(8,128)} %param.19) | copy-start | bytes 2359300
  307.1 195.5 %copy-start = (f32[1,256,1536]{2,1,0:T(8,128)S(1)}, f32[1,256,1536]{2,1,0:T(8,128)}, u32[]{:S(2)}) copy-start(f32[1,256,1536]{2,1,0:T(8,128)} %param.14) | copy-start | bytes 4718596
  307.1 303.0 %all-gather.11.cloned.1.call-start = ((), (), s32[]{:S(2)}) async-start(), calls=%async_computation.12 | async-start | bytes 3538944 | tf_op jit(solution)/shard_map/all_gather | solution.py:155
  373.5 134.9 %copy-start.11 = (bf16[768,768]{0,1:T(8,128)(2,1)S(1)}, bf16[768,768]{0,1:T(8,128)(2,1)}, u32[]{:S(2)}) copy-start(bf16[768,768]{0,1:T(8,128)(2,1)} %copy-done.10) | copy-start | bytes 3538948
  373.5 367.7 %all-gather.9.cloned.1.call-start = ((), (), s32[]{:S(2)}) async-start(), calls=%async_computation.10 | async-start | bytes 7077888 | tf_op jit(solution)/shard_map/all_gather | solution.py:154
  508.4 13.5 %copy-start.12 = (bf16[768,768]{0,1:T(8,128)(2,1)S(1)}, bf16[768,768]{0,1:T(8,128)(2,1)}, u32[]{:S(2)}) copy-start(bf16[768,768]{0,1:T(8,128)(2,1)} %get-tuple-element.34) | copy-start | bytes 3538948
  514.9 15.7 %all-to-all-start.4 = ((bf16[16,1,48]{2,1,0:T(2,128)(2,1)}), bf16[16,1,48]{2,1,0:T(2,128)(2,1)S(1)}, u32[]{:S(2)}, u32[]{:S(2)}) async-start(bf16[16,1,48]{2,1,0:T(2,128)(2,1)} %convert_element_type.95), calls=%async_computation.4 | async-start | bytes 16384 | tf_op jit(solution)/shard_map/all_to_all | solution.py:121
  530.6 53.3 %all-to-all-start.3 = ((bf16[16,48,2048]{2,1,0:T(8,128)(2,1)}), bf16[16,48,2048]{2,1,0:T(8,128)(2,1)S(1)}, u32[]{:S(2)}, u32[]{:S(2)}) async-start(bf16[16,48,2048]{2,1,0:T(8,128)(2,1)} %bitcast.108), calls=%async_computation.3 | async-start | bytes 6291456 | tf_op jit(solution)/shard_map/all_to_all | solution.py:120
  741.2 6.1 copy-start.1
Sparse Core Ops, SparseCore 0:
  10.2 199.4 all-gather.6
  211.9 72.1 all-gather.4
  298.5 71.4 reduce-scatter.4
  372.9 129.6 reduce-scatter.2
  504.1 105.9 all-gather.10
  612.2 129.0 all-gather.8
where the time goes:
time: 757 us; the launch traced here: 756 us
  waiting for transfers between devices  599 us (79%)
  matrix products  44.9 us (6%)
  local copies, waits for them, and re-layouts  38.6 us (5%)
  starting transfers between devices  34.4 us (5%)
  other arithmetic  24.7 us (3%)
  between operations  14.4 us (2%)
    all_gather x1, waiting for transfers between devices, local(): lax.all_gather(master_gu_next.astype(jnp.bfloat16), 'dp', axis=0, tiled=T...  131 us
    reduce_scatter x1, waiting for transfers between devices, local(): lax.psum_scatter(full_gate_up.astype(jnp.bfloat16), 'dp', scatter_dimensi...  129 us
    all_gather x1, waiting for transfers between devices, local(): lax.all_gather(master_gate_up[0].astype(jnp.bfloat16), 'dp', axis=0, tile...  72.2 us
    all_gather x1, waiting for transfers between devices, local(): lax.all_gather(master_down[0].astype(jnp.bfloat16), 'dp', axis=0, tiled=T...  65.8 us
    reduce_scatter x1, waiting for transfers between devices, local(): lax.psum_scatter(full_down.astype(jnp.bfloat16), 'dp', scatter_dimension=...  62.8 us
    all_to_all x1, waiting for transfers between devices, local(): lax.all_to_all(grad_back, 'expert', split_axis=0, concat_axis=0, tiled=True)  41.6 us
    all_to_all x1, waiting for transfers between devices, local(): lax.all_to_all(send_in, 'expert', split_axis=0, concat_axis=0, tiled=True)  41.5 us
    all_to_all x1, waiting for transfers between devices, local(): lax.all_to_all(send_grad, 'expert', split_axis=0, concat_axis=0, tiled=True)  41 us
  transfers between devices with their start and end apart: 11, of which 10 were waited for; matrix products, arithmetic and copies ran while one was open for 11% of the time, Pallas kernels for 0%

commit v1 on v0

v1 whole, which is shorter than its diff:
```python
import jax
import jax.numpy as jnp
from jax import lax
from jax.sharding import PartitionSpec as P

beta_first = 0.9
beta_second = 0.95
learn_rate = 0.01
weight_decay = 0.1
adam_epsilon = 1e-08
bias_first = 0.9999734386
bias_second = 0.9940794708

F32 = jnp.float32
BF16 = jnp.bfloat16

Z_UP = [(i, (i + 2) % 8) for i in range(8)]
Z_DOWN = [(i, (i - 2) % 8) for i in range(8)]
Y_SWAP = [(i, i ^ 1) for i in range(8)]
X_UP = [(i, (i + 4) % 16) for i in range(16)]
X_DOWN = [(i, (i - 4) % 16) for i in range(16)]
X_FAR = [(i, (i + 8) % 16) for i in range(16)]
YH_SWAP = [(i, i ^ 2) for i in range(16)]
CORE_SWAP = [(i, i ^ 1) for i in range(16)]


def z_up(a):
    return lax.ppermute(a, "dp", Z_UP)


def z_down(a):
    return lax.ppermute(a, "dp", Z_DOWN)


def y_swap(a):
    return lax.ppermute(a, "dp", Y_SWAP)


def x_up(a):
    return lax.ppermute(a, "expert", X_UP)


def x_down(a):
    return lax.ppermute(a, "expert", X_DOWN)


def x_far(a):
    return lax.ppermute(a, "expert", X_FAR)


def yh_swap(a):
    return lax.ppermute(a, "expert", YH_SWAP)


def core_swap(a):
    return lax.ppermute(a, "expert", CORE_SWAP)


def place(full, block, shard):
    return lax.dynamic_update_slice(full, block, (shard * block.shape[0], 0))


def gather_shards(own, z, y):
    rows = own.shape[0]
    half = rows // 2
    full = jnp.zeros((8 * rows, own.shape[1]), own.dtype)
    for dy, block in ((0, own), (1, y_swap(own))):
        below = z_up(block)
        above = z_down(block)
        far_first = z_up(below[:half])
        far_last = z_down(above[half:])
        column = y ^ dy
        full = place(full, block, z * 2 + column)
        full = place(full, below, ((z + 3) % 4) * 2 + column)
        full = place(full, above, ((z + 1) % 4) * 2 + column)
        far = (((z + 2) % 4) * 2 + column) * 2
        full = place(full, far_first, far)
        full = place(full, far_last, far + 1)
    return full


def scatter_sum(block_of):
    sums = []
    for dy in (1, 0):
        far = block_of(2, dy)
        half = far.shape[0] // 2
        up_first = z_up(far[:half])
        down_last = z_down(far[half:])
        up_block = block_of(1, dy)
        down_block = block_of(-1, dy)
        up_sum = (up_block[:half].astype(F32) + up_first.astype(F32)).astype(BF16)
        down_sum = (down_block[half:].astype(F32) + down_last.astype(F32)).astype(BF16)
        from_below = z_up(jnp.concatenate([up_sum, up_block[half:]], axis=0))
        from_above = z_down(jnp.concatenate([down_block[:half], down_sum], axis=0))
        sums.append(
            block_of(0, dy).astype(F32) + from_below.astype(F32) + from_above.astype(F32)
        )
    other, own = sums
    return own + y_swap(other.astype(BF16)).astype(F32)


def adam_update(master, moment, second, grad):
    moment_next = beta_first * moment + (1.0 - beta_first) * grad
    second_next = beta_second * second + (1.0 - beta_second) * grad * grad
    step_size = moment_next / bias_first / (jnp.sqrt(second_next / bias_second) + adam_epsilon)
    master_next = master - learn_rate * (step_size + weight_decay * master)
    return (master_next, moment_next, second_next)


def local(
    tokens,
    out_grad,
    expert_ids,
    gate_values,
    master_gate_up,
    master_down,
    moment_gate_up,
    moment_down,
    second_gate_up,
    second_down,
):
    experts = 16
    tok_count, width = tokens.shape
    hidden = 768
    cap = 48
    route_count = 2 * tok_count
    scale_in = width ** (-0.5)
    scale_out = hidden ** (-0.5)
    r = lax.axis_index("dp")
    e = lax.axis_index("expert")
    z, y = r // 2, r % 2
    x, hc = e // 4, e % 4

    w_gate_up = gather_shards(master_gate_up[0].astype(BF16), z, y)
    w_down = gather_shards(master_down[0].astype(BF16), z, y)

    route_ids = expert_ids.reshape(route_count)
    onehot = (route_ids[:, None] == jnp.arange(experts, dtype=jnp.int32)[None, :]).astype(jnp.int32)
    before = jnp.cumsum(onehot, axis=0) - onehot
    position = route_ids * cap + jnp.sum(before * onehot, axis=1)
    pos_own = position.reshape(tok_count, 2).T
    pos_core = core_swap(pos_own)
    pos_yh = yh_swap(pos_own)
    pos_yhc = core_swap(pos_yh)

    slots = jnp.arange(experts * cap, dtype=jnp.int32)
    send_gate = jnp.sum(
        jnp.where(
            slots[:, None] == position[None, :],
            gate_values.reshape(1, route_count).astype(F32),
            0.0,
        ),
        axis=1,
    ).astype(BF16)
    gate_block = lax.all_to_all(
        send_gate.reshape(experts, cap), "expert", split_axis=0, concat_axis=0, tiled=True
    )

    dx = jnp.array([0, 1, 3, 2], jnp.int32)
    target = ((((x + dx) % 4) * 4 + hc) * cap)[:, None] + jnp.arange(cap, dtype=jnp.int32)[None, :]

    def pick(pos_pair):
        pos = jnp.stack(pos_pair)
        hit = (pos[:, 0][None, None] == target[:, :, None, None]) | (
            pos[:, 1][None, None] == target[:, :, None, None]
        )
        same = jnp.arange(2)[:, None] == jnp.arange(2)[None, :]
        full = hit[:, None] & same[None, :, None, :, None]
        return full.astype(BF16).reshape(8 * cap, 2 * tok_count)

    pick_near = pick((pos_own, pos_core))
    pick_far = pick((pos_yh, pos_yhc))

    def spread(rows):
        near = jnp.concatenate([rows, core_swap(rows)], axis=0)
        other = yh_swap(rows)
        far = jnp.concatenate([other, core_swap(other)], axis=0)
        got = []
        for chosen, block in ((pick_near, near), (pick_far, far)):
            sent = jnp.dot(chosen, block, preferred_element_type=F32).astype(BF16)
            sent = sent.reshape(4, 2 * cap, width)
            got.append((sent[0], x_up(sent[1]), x_down(sent[2]), x_far(sent[3])))
        return jnp.concatenate([got[s][j] for j in range(4) for s in range(2)], axis=0)

    in_rows = spread(tokens)
    grad_rows = spread(out_grad)
    offsets = jnp.array([0, 3, 1, 2], jnp.int32)
    source = (
        (((x + offsets) % 4) * 4)[:, None] + (hc ^ jnp.arange(4, dtype=jnp.int32))[None, :]
    ).reshape(16)
    gate_rows = gate_block[source].reshape(experts * cap)

    projected = scale_in * jnp.dot(in_rows, w_gate_up, preferred_element_type=F32)
    gate_part = projected[:, :hidden]
    up_part = projected[:, hidden:]
    sig_gate = jax.nn.sigmoid(gate_part)
    swish_gate = gate_part * sig_gate
    hidden_act = (swish_gate * up_part).astype(BF16)
    scaled = (gate_rows.astype(F32)[:, None] * grad_rows.astype(F32)).astype(BF16)

    contract_rows = (((0,), (0,)), ((), ()))
    part_down = (
        scale_out
        * lax.dot_general(hidden_act, scaled, contract_rows, preferred_element_type=F32)
    ).astype(BF16)

    def down_block(dz, dy):
        shard = ((z + dz) % 4) * 2 + (y ^ dy)
        return lax.dynamic_slice(part_down, (shard * 96, 0), (96, width))

    grad_down = scatter_sum(down_block)

    grad_act = scale_out * lax.dot_general(
        scaled, w_down, (((1,), (1,)), ((), ())), preferred_element_type=F32
    )
    grad_gate = grad_act * up_part * sig_gate * (1.0 + gate_part * (1.0 - sig_gate))
    grad_up = grad_act * swish_gate
    grad_proj = jnp.concatenate([grad_gate, grad_up], axis=1).astype(BF16)

    parts = {}
    for dz in (2, 1, -1, 0):
        plane = (z + dz) % 4
        columns = lax.dynamic_slice(in_rows, (0, plane * 512), (experts * cap, 512))
        parts[dz] = (
            scale_in
            * lax.dot_general(columns, grad_proj, contract_rows, preferred_element_type=F32)
        ).astype(BF16)

    def gate_up_block(dz, dy):
        return lax.dynamic_slice(parts[dz], ((y ^ dy) * 256, 0), (256, 2 * hidden))

    grad_gate_up = scatter_sum(gate_up_block)

    grad_route = (
        scale_in
        * lax.dot_general(
            grad_proj, w_gate_up, (((1,), (1,)), ((), ())), preferred_element_type=F32
        )
    ).astype(BF16)
    expert_out = scale_out * jnp.dot(hidden_act, w_down, preferred_element_type=F32)
    gate_score = jnp.sum(grad_rows.astype(F32) * expert_out, axis=1).astype(BF16)

    back = grad_route.reshape(4, 4 * cap, width)
    returned = jnp.concatenate(
        [back[0], x_down(back[1]), x_up(back[2]), x_far(back[3])], axis=0
    )
    pos_all = jnp.stack([pos_own, pos_core, pos_yh, pos_yhc])
    hit_back = (pos_all[:, 0, :, None, None] == target) | (pos_all[:, 1, :, None, None] == target)
    same_back = jnp.arange(4)[:, None] == jnp.arange(4)[None, :]
    choose = (hit_back[:, :, :, None, :] & same_back[:, None, None, :, None]).astype(BF16)
    partial = jnp.dot(
        choose.reshape(4 * tok_count, 16 * cap), returned, preferred_element_type=F32
    ).reshape(4, tok_count, width)
    swapped = core_swap(jnp.concatenate([partial[1], partial[3]], axis=0).astype(BF16)).astype(F32)
    own_sum = partial[0] + swapped[:tok_count]
    far_sum = partial[2] + swapped[tok_count:]
    input_grad = (own_sum + yh_swap(far_sum.astype(BF16)).astype(F32)).astype(BF16)

    home = jnp.zeros((16,), jnp.int32).at[source].set(jnp.arange(16, dtype=jnp.int32))
    score_back = lax.all_to_all(
        gate_score.reshape(experts, cap)[home], "expert", split_axis=0, concat_axis=0, tiled=True
    )
    gate_grad = score_back.reshape(experts * cap)[position].reshape(tok_count, 2)

    master_dn_next, moment_dn_next, second_dn_next = adam_update(
        master_down[0], moment_down[0], second_down[0], grad_down
    )
    new_down = gather_shards(master_dn_next.astype(BF16), z, y)
    master_gu_next, moment_gu_next, second_gu_next = adam_update(
        master_gate_up[0], moment_gate_up[0], second_gate_up[0], grad_gate_up
    )
    new_gate_up = gather_shards(master_gu_next.astype(BF16), z, y)
    return (
        input_grad,
        gate_grad,
        new_gate_up[None],
        new_down[None],
        master_gu_next[None],
        master_dn_next[None],
        moment_gu_next[None],
        moment_dn_next[None],
        second_gu_next[None],
        second_dn_next[None],
    )


def solution(mesh):
    rows = P(("dp", "expert"), None)
    state = P("expert", "dp", None)
    whole = P("expert", None, None)
    return jax.shard_map(
        local,
        mesh=mesh,
        in_specs=(rows,) * 4 + (state,) * 6,
        out_specs=(rows, rows, whole, whole) + (state,) * 6,
        check_vma=False,
    )
```

time: 757 us -> 470 us (0.62)
  the two profiles are of different devices: /device:TPU:4 before, /device:TPU:16 now
where the time goes in v1:
time: 470 us; the launch traced here: 460 us
  waiting for transfers between devices  197 us (42%)
  starting transfers between devices  116 us (25%)
  local copies, waits for them, and re-layouts  63.8 us (14%)
  matrix products  50.6 us (11%)
  other arithmetic  30.9 us (7%)
    ppermute x24, waiting for transfers between devices, z_up(): return lax.ppermute(a, 'dp', Z_UP)  113 us
    ppermute x24, starting transfers between devices, z_down(): return lax.ppermute(a, 'dp', Z_DOWN)  52.1 us
    ppermute x24, waiting for transfers between devices, z_down(): return lax.ppermute(a, 'dp', Z_DOWN)  39.1 us
    dynamic_update_slice x36, local copies, waits for them, and re-layouts, place(): return lax.dynamic_update_slice(full, block, (shard * block.shape[0], 0))  18.4 us
    ppermute x5, waiting for transfers between devices, x_up(): return lax.ppermute(a, 'expert', X_UP)  18.1 us
    ppermute x5, starting transfers between devices, x_far(): return lax.ppermute(a, 'expert', X_FAR)  14.4 us
    unnamed x90, local copies, waits for them, and re-layouts  11.5 us
    all_to_all x1, starting transfers between devices, local(): lax.all_to_all(gate_score.reshape(experts, cap)[home], 'expert', split_ax...  9.64 us
  transfers between devices with their start and end apart: 82, of which 34 were waited for; matrix products, arithmetic and copies ran while one was open for 24% of the time, Pallas kernels for 0%

profile of v1, /device:TPU:16, one launch (start us, length us, event | category | flops | bytes accessed | tf_op | source)
XLA Modules:
  0.0 460.3 jit_solution(5919219127373749634)
XLA Ops:
  4.4 3.1 broadcast.228
  17.8 7.3 %all-to-all-start = ((bf16[16,1,48]{2,1,0:T(2,128)(2,1)}), bf16[16,1,48]{2,1,0:T(2,128)(2,1)S(1)}, u32[]{:S(2)}, u32[]{:S(2)}) async-start(bf16[16,1,48]{2,1,0:T(2,128)(2,1)} %convert_element_type.311), calls=%async_computation | async-start | bytes 16384 | tf_op jit(solution)/shard_map/all_to_all | solution.py:155
  41.1 3.2 collective-permute-start.13
  60.4 4.2 collective-permute-done.14
  65.3 5.0 %collective-permute-done.15 = bf16[48,2048]{1,0:T(8,128)(2,1)S(1)} collective-permute-done((bf16[48,2048]{1,0:T(8,128)(2,1)S(1)}, bf16[48,2048]{1,0:T(8,128)(2,1)S(1)}, u32[]{:S(2)}, u32[]{:S(2)}) %collective-permute-start.15) | collective-permute-done | bytes 196640 | tf_op jit(solution)/shard_map/ppermute | solution.py:32
  72.9 3.2 collective-permute-start.18
  78.2 6.5 %collective-permute-done.17 = bf16[96,2048]{1,0:T(8,128)(2,1)S(1)} collective-permute-done((bf16[96,2048]{1,0:T(8,128)(2,1)S(1)}, bf16[96,2048]{1,0:T(8,128)(2,1)S(1)}, u32[]{:S(2)}, u32[]{:S(2)}) %collective-permute-start.17) | collective-permute-done | bytes 393248 | tf_op jit(solution)/shard_map/ppermute | solution.py:28
  87.8 7.7 %collective-permute-done.19 = bf16[48,2048]{1,0:T(8,128)(2,1)S(1)} collective-permute-done((bf16[48,2048]{1,0:T(8,128)(2,1)S(1)}, bf16[48,2048]{1,0:T(8,128)(2,1)S(1)}, u32[]{:S(2)}, u32[]{:S(2)}) %collective-permute-start.19) | collective-permute-done | bytes 196640 | tf_op jit(solution)/shard_map/ppermute | solution.py:28
  96.2 5.8 %collective-permute-done.20 = bf16[48,2048]{1,0:T(8,128)(2,1)S(1)} collective-permute-done((bf16[48,2048]{1,0:T(8,128)(2,1)S(1)}, bf16[48,2048]{1,0:T(8,128)(2,1)S(1)}, u32[]{:S(2)}, u32[]{:S(2)}) %collective-permute-start.20) | collective-permute-done | bytes 196640 | tf_op jit(solution)/shard_map/ppermute | solution.py:32
  102.7 3.2 collective-permute-start.33
  107.1 3.3 collective-permute-start.36
  111.5 3.7 collective-permute-done.32
  115.2 3.3 collective-permute-start.4
  123.7 6.2 %collective-permute-done.35 = bf16[256,1536]{1,0:T(8,128)(2,1)S(1)} collective-permute-done((bf16[256,1536]{1,0:T(8,128)(2,1)}, bf16[256,1536]{1,0:T(8,128)(2,1)S(1)}, u32[]{:S(2)}, u32[]{:S(2)}) %collective-permute-start.35) | collective-permute-done | bytes 786464 | tf_op jit(solution)/shard_map/ppermute | solution.py:28
  130.0 3.6 collective-permute-start.38
  137.6 2.8 collective-permute-start.26
  141.1 2.8 collective-permute-start.28
  146.5 2.7 collective-permute-start.8
  150.4 12.2 %collective-permute-done.6 = bf16[96,2048]{1,0:T(8,128)(2,1)S(1)} collective-permute-done((bf16[96,2048]{1,0:T(8,128)(2,1)S(1)}, bf16[96,2048]{1,0:T(8,128)(2,1)S(1)}, u32[]{:S(2)}, u32[]{:S(2)}) %collective-permute-start.6) | collective-permute-done | bytes 393248 | tf_op jit(solution)/shard_map/ppermute | solution.py:40
  162.7 2.8 collective-permute-start.10
  165.5 5.9 %collective-permute-done.25 = bf16[96,2048]{1,0:T(8,128)(2,1)S(1)} collective-permute-done((bf16[96,2048]{1,0:T(8,128)(2,1)S(1)}, bf16[96,2048]{1,0:T(8,128)(2,1)S(1)}, u32[]{:S(2)}, u32[]{:S(2)}) %collective-permute-start.25) | collective-permute-done | bytes 393248 | tf_op jit(solution)/shard_map/ppermute | solution.py:40
  172.1 2.9 collective-permute-start.29
  174.9 8.4 %collective-permute-done.27 = bf16[96,2048]{1,0:T(8,128)(2,1)S(1)} collective-permute-done((bf16[96,2048]{1,0:T(8,128)(2,1)S(1)}, bf16[96,2048]{1,0:T(8,128)(2,1)S(1)}, u32[]{:S(2)}, u32[]{:S(2)}) %collective-permute-start.27) | collective-permute-done | bytes 393248 | tf_op jit(solution)/shard_map/ppermute | solution.py:44
  188.3 2.8 collective-permute-start.11
  191.2 8.8 %convolution_multiply_fusion = f32[768,1536]{0,1:T(8,128)S(1)} fusion(bf16[768,2048]{1,0:T(8,128)(2,1)S(1)} %constant_dynamic-update-slice_fusion.6, bf16[2048,1536]{1,0:T(8,128)(2,1)} %constant_dynamic-update-slice_fusion.12), kind=kOutput, calls=%fused_computation.10 | convolution fusion | flops 4833017856 | bytes 14155776 | tf_op jit(solution)/shard_map/dot_general | solution.py:193
  200.3 4.5 collective-permute-done.11
  204.9 5.5 %multiply_convert_fusion.4 = (bf16[768,768]{0,1:T(8,128)(2,1)S(1)}, bf16[768,768]{0,1:T(8,128)(2,1)S(1)}, bf16[768,768]{0,1:T(8,128)(2,1)S(1)}) fusion(f32[768,1536]{0,1:T(8,128)S(1)} %convolution_multiply_fusion, bf16[768,2048]{1,0:T(8,128)(2,1)} %constant_dynamic-update-slice_fusion.22, bf16[768,2048]{1,0:T(8,128)(2,1)S(1)} %constant_dynamic-update-slice_fusion, ...), kind=kOutput, calls=%fused_computation.35 | convolution fusion | flops 2430074880 | bytes 14552064 | tf_op jit(solution)/shard_map/dot_general | solution.py:213
  210.4 6.2 %fusion.1 = bf16[768]{0:T(1024)(128)(2,1)S(1)} fusion(bf16[768,2048]{1,0:T(8,128)(2,1)S(1)} %constant_dynamic-update-slice_fusion, bf16[768,768]{0,1:T(8,128)(2,1)S(1)} %get-tuple-element.76, bf16[768,2048]{1,0:T(8,128)(2,1)} %constant_dynamic-update-slice_fusion.22), kind=kOutput, calls=%fused_computation.7 | convolution fusion | flops 2422209792 | bytes 7472640 | tf_op jit(solution)/shard_map/dot_general | solution.py:240
  216.6 4.2 multiply_convert_fusion
  220.7 8.2 %multiply_convert_fusion.1 = bf16[768,2048]{1,0:T(8,128)(2,1)S(1)} fusion(bf16[2048,1536]{1,0:T(8,128)(2,1)} %constant_dynamic-update-slice_fusion.12, bf16[768,768]{0,1:T(8,128)(2,1)S(1)} %get-tuple-element.75, bf16[768,768]{0,1:T(8,128)(2,1)S(1)} %get-tuple-element.74), kind=kOutput, calls=%fused_computation.9 | convolution fusion | flops 4839702528 | bytes 11796480 | tf_op jit(solution)/shard_map/dot_general | solution.py:236
  230.7 3.2 collective-permute-start.41
  235.3 9.6 %all-to-all-start.1 = ((bf16[16,1,48]{2,1,0:T(2,128)(2,1)}), bf16[16,1,48]{2,1,0:T(2,128)(2,1)S(1)}, u32[]{:S(2)}, u32[]{:S(2)}) async-start(bf16[16,1,48]{2,1,0:T(2,128)(2,1)} %copy.85), calls=%async_computation.1 | async-start | bytes 16384 | tf_op jit(solution)/shard_map/all_to_all | solution.py:260
  244.9 3.5 fusion.12
  258.7 2.2 collective-permute-start.68
  262.8 2.6 fusion.10
  265.5 3.5 gather_fusion.2
  279.1 7.9 %collective-permute-done.46 = bf16[128,1536]{1,0:T(8,128)(2,1)S(1)} collective-permute-done((bf16[128,1536]{1,0:T(8,128)(2,1)}, bf16[128,1536]{1,0:T(8,128)(2,1)S(1)}, u32[]{:S(2)}, u32[]{:S(2)}) %collective-permute-start.46) | collective-permute-done | bytes 393248 | tf_op jit(solution)/shard_map/ppermute | solution.py:32
  287.0 5.8 %collective-permute-done.50 = bf16[128,1536]{1,0:T(8,128)(2,1)S(1)} collective-permute-done((bf16[128,1536]{1,0:T(8,128)(2,1)}, bf16[128,1536]{1,0:T(8,128)(2,1)S(1)}, u32[]{:S(2)}, u32[]{:S(2)}) %collective-permute-start.50) | collective-permute-done | bytes 393248 | tf_op jit(solution)/shard_map/ppermute | solution.py:32
  293.5 4.2 collective-permute-done.44
  299.2 5.1 %collective-permute-done.48 = bf16[128,1536]{1,0:T(8,128)(2,1)S(1)} collective-permute-done((bf16[128,1536]{1,0:T(8,128)(2,1)S(1)}, bf16[128,1536]{1,0:T(8,128)(2,1)S(1)}, u32[]{:S(2)}, u32[]{:S(2)}) %collective-permute-start.48) | collective-permute-done | bytes 393248 | tf_op jit(solution)/shard_map/ppermute | solution.py:28
  305.6 2.6 collective-permute-start.65
  308.2 6.8 %collective-permute-done.67 = bf16[96,2048]{1,0:T(8,128)(2,1)S(1)} collective-permute-done((bf16[96,2048]{1,0:T(8,128)(2,1)S(1)}, bf16[96,2048]{1,0:T(8,128)(2,1)S(1)}, u32[]{:S(2)}, u32[]{:S(2)}) %collective-permute-start.67) | collective-permute-done | bytes 393248 | tf_op jit(solution)/shard_map/ppermute | solution.py:28
  316.2 3.3 collective-permute-start.51
  321.5 4.8 %fusion.77 = (bf16[1024,2048]{1,0:T(8,128)(2,1)S(1)}, f32[1024,2048]{1,0:T(8,128)S(1)}) fusion(pred[1024,768]{0,1:T(8,128)(4,1)S(1)} %bitcast.181, bf16[192,2048]{1,0:T(8,128)(2,1)} %collective-permute-done.41, bf16[192,2048]{1,0:T(8,128)(2,1)S(1)} %collective-permute-done.40, bf16[192,2048]{1,0:T(8,128)(2,1)S(1)} %collective-permute-done.39, ...), kind=kOutput, calls=%fused_computation.250 | convolution fusion | flops 3235905536 | bytes 16515072 | tf_op jit(solution)/shard_map/dot_general | solution.py:251
  326.8 3.2 collective-permute-start.47
  337.5 7.7 %collective-permute-done.49 = bf16[256,1536]{1,0:T(8,128)(2,1)S(1)} collective-permute-done((bf16[256,1536]{1,0:T(8,128)(2,1)S(1)}, bf16[256,1536]{1,0:T(8,128)(2,1)S(1)}, u32[]{:S(2)}, u32[]{:S(2)}) %collective-permute-start.49) | collective-permute-done | bytes 786464 | tf_op jit(solution)/shard_map/ppermute | solution.py:28
  345.5 21.4 %collective-permute-done.71 = bf16[96,2048]{1,0:T(8,128)(2,1)S(1)} collective-permute-done((bf16[96,2048]{1,0:T(8,128)(2,1)S(1)}, bf16[96,2048]{1,0:T(8,128)(2,1)S(1)}, u32[]{:S(2)}, u32[]{:S(2)}) %collective-permute-start.71) | collective-permute-done | bytes 393248 | tf_op jit(solution)/shard_map/ppermute | solution.py:28
  369.0 5.6 %collective-permute-done.75 = bf16[96,2048]{1,0:T(8,128)(2,1)S(1)} collective-permute-done((bf16[96,2048]{1,0:T(8,128)(2,1)S(1)}, bf16[96,2048]{1,0:T(8,128)(2,1)S(1)}, u32[]{:S(2)}, u32[]{:S(2)}) %collective-permute-start.75) | collective-permute-done | bytes 393248 | tf_op jit(solution)/shard_map/ppermute | solution.py:36
  374.7 2.2 collective-permute-done.73
  376.9 5.4 %collective-permute-done.74 = bf16[48,2048]{1,0:T(8,128)(2,1)S(1)} collective-permute-done((bf16[48,2048]{1,0:T(8,128)(2,1)S(1)}, bf16[48,2048]{1,0:T(8,128)(2,1)S(1)}, u32[]{:S(2)}, u32[]{:S(2)}) %collective-permute-start.74) | collective-permute-done | bytes 196640 | tf_op jit(solution)/shard_map/ppermute | solution.py:32
  383.1 2.8 collective-permute-done.76
  386.1 6.1 %collective-permute-done.77 = bf16[96,2048]{1,0:T(8,128)(2,1)S(1)} collective-permute-done((bf16[96,2048]{1,0:T(8,128)(2,1)S(1)}, bf16[96,2048]{1,0:T(8,128)(2,1)S(1)}, u32[]{:S(2)}, u32[]{:S(2)}) %collective-permute-start.77) | collective-permute-done | bytes 393248 | tf_op jit(solution)/shard_map/ppermute | solution.py:32
  392.4 3.3 collective-permute-start.79
  395.7 3.8 collective-permute-done.52
  402.6 2.4 bitcast_dynamic-update-slice_fusion.5
  405.0 3.2 collective-permute-start.54
  410.1 12.6 %collective-permute-done.53 = bf16[256,1536]{1,0:T(8,128)(2,1)S(1)} collective-permute-done((bf16[256,1536]{1,0:T(8,128)(2,1)S(1)}, bf16[256,1536]{1,0:T(8,128)(2,1)S(1)}, u32[]{:S(2)}, u32[]{:S(2)}) %collective-permute-start.53) | collective-permute-done | bytes 786464 | tf_op jit(solution)/shard_map/ppermute | solution.py:28
  422.8 3.3 collective-permute-start.56
  426.1 3.2 collective-permute-start.59
  430.4 5.2 %collective-permute-done.55 = bf16[128,1536]{1,0:T(8,128)(2,1)S(1)} collective-permute-done((bf16[128,1536]{1,0:T(8,128)(2,1)S(1)}, bf16[128,1536]{1,0:T(8,128)(2,1)S(1)}, u32[]{:S(2)}, u32[]{:S(2)}) %collective-permute-start.55) | collective-permute-done | bytes 393248 | tf_op jit(solution)/shard_map/ppermute | solution.py:28
  435.8 12.5 %collective-permute-done.58 = bf16[256,1536]{1,0:T(8,128)(2,1)S(1)} collective-permute-done((bf16[256,1536]{1,0:T(8,128)(2,1)S(1)}, bf16[256,1536]{1,0:T(8,128)(2,1)S(1)}, u32[]{:S(2)}, u32[]{:S(2)}) %collective-permute-start.58) | collective-permute-done | bytes 786464 | tf_op jit(solution)/shard_map/ppermute | solution.py:28
  448.4 3.3 collective-permute-start.61
  453.3 4.0 collective-permute-done.60
  457.4 2.7 copy-done
  (352 shorter events, 129.0 us)
Async XLA Ops:
  4.1 29.3 %collective-permute-start.1 = (s32[2,256]{0,1:T(8,128)}, s32[2,256]{0,1:T(8,128)}, u32[]{:S(2)}, u32[]{:S(2)}) collective-permute-start(s32[2,256]{0,1:T(8,128)} %get-tuple-element.124), channel_id=1, source_target_pairs={{0,2},{1,3},{2,0},{3,1},{4,6},{5,7},{6,4},{7,5},{8,10},{9,11},{10,... | collective-permute-start | bytes 6152 | tf_op jit(solution)/shard_map/ppermute | solution.py:52
  4.4 33.5 %collective-permute-start = (s32[2,256]{0,1:T(8,128)}, s32[2,256]{0,1:T(8,128)S(1)}, u32[]{:S(2)}, u32[]{:S(2)}) collective-permute-start(s32[2,256]{0,1:T(8,128)} %get-tuple-element.124), channel_id=1, source_target_pairs={{0,1},{1,0},{2,3},{3,2},{4,5},{5,4},{6,7},{7,6},{8,9},{9,8},{10,11... | collective-permute-start | bytes 6152 | tf_op jit(solution)/shard_map/ppermute | solution.py:56
  8.7 63.2 %collective-permute-start.30 = (bf16[256,1536]{1,0:T(8,128)(2,1)}, bf16[256,1536]{1,0:T(8,128)(2,1)S(1)}, u32[]{:S(2)}, u32[]{:S(2)}) collective-permute-start(bf16[256,1536]{1,0:T(8,128)(2,1)} %get-tuple-element.73), channel_id=1, source_target_pairs={{0,32},{16,48},{32,64},{48,80},{64,96},{80,112},{96,0},{112,16},{1... | collective-permute-start | bytes 2359304 | tf_op jit(solution)/shard_map/ppermute | solution.py:28
  10.7 62.1 %collective-permute-start.31 = (bf16[256,1536]{1,0:T(8,128)(2,1)}, bf16[256,1536]{1,0:T(8,128)(2,1)}, u32[]{:S(2)}, u32[]{:S(2)}) collective-permute-start(bf16[256,1536]{1,0:T(8,128)(2,1)} %get-tuple-element.73), channel_id=1, source_target_pairs={{0,96},{16,112},{32,0},{48,16},{64,32},{80,48},{96,64},{112,80},{1... | collective-permute-start | bytes 2359304 | tf_op jit(solution)/shard_map/ppermute | solution.py:32
  12.9 89.8 %collective-permute-start.34 = (bf16[256,1536]{1,0:T(8,128)(2,1)}, bf16[256,1536]{1,0:T(8,128)(2,1)}, u32[]{:S(2)}, u32[]{:S(2)}) collective-permute-start(bf16[256,1536]{1,0:T(8,128)(2,1)} %get-tuple-element.73), channel_id=1, source_target_pairs={{0,16},{16,0},{32,48},{48,32},{64,80},{80,64},{96,112},{112,96},{1... | collective-permute-start | bytes 2359304 | tf_op jit(solution)/shard_map/ppermute | solution.py:36
  17.8 16.8 %all-to-all-start = ((bf16[16,1,48]{2,1,0:T(2,128)(2,1)}), bf16[16,1,48]{2,1,0:T(2,128)(2,1)S(1)}, u32[]{:S(2)}, u32[]{:S(2)}) async-start(bf16[16,1,48]{2,1,0:T(2,128)(2,1)} %convert_element_type.311), calls=%async_computation | async-start | bytes 16384 | tf_op jit(solution)/shard_map/all_to_all | solution.py:155
  38.5 16.2 %collective-permute-start.12 = (bf16[96,2048]{1,0:T(8,128)(2,1)}, bf16[96,2048]{1,0:T(8,128)(2,1)S(1)}, u32[]{:S(2)}, u32[]{:S(2)}) collective-permute-start(bf16[96,2048]{1,0:T(8,128)(2,1)} %get-tuple-element.71), channel_id=1, source_target_pairs={{0,32},{16,48},{32,64},{48,80},{64,96},{80,112},{96,0},{112,16},{1... | collective-permute-start | bytes 1179656 | tf_op jit(solution)/shard_map/ppermute | solution.py:28
  41.1 16.5 %collective-permute-start.13 = (bf16[96,2048]{1,0:T(8,128)(2,1)}, bf16[96,2048]{1,0:T(8,128)(2,1)}, u32[]{:S(2)}, u32[]{:S(2)}) collective-permute-start(bf16[96,2048]{1,0:T(8,128)(2,1)} %get-tuple-element.71), channel_id=1, source_target_pairs={{0,96},{16,112},{32,0},{48,16},{64,32},{80,48},{96,64},{112,80},{1... | collective-permute-start | bytes 1179656 | tf_op jit(solution)/shard_map/ppermute | solution.py:32
  54.8 16.4 %collective-permute-start.16 = (bf16[96,2048]{1,0:T(8,128)(2,1)S(1)}, bf16[96,2048]{1,0:T(8,128)(2,1)S(1)}, u32[]{:S(2)}, u32[]{:S(2)}) collective-permute-start(bf16[96,2048]{1,0:T(8,128)(2,1)S(1)} %copy-done.21), channel_id=1, source_target_pairs={{0,16},{16,0},{32,48},{48,32},{64,80},{80,64},{96,112},{112,96},{1... | collective-permute-start | bytes 1179656 | tf_op jit(solution)/shard_map/ppermute | solution.py:36
  70.3 49.1 %collective-permute-start.22 = (bf16[256,2048]{1,0:T(8,128)(2,1)S(1)}, bf16[256,2048]{1,0:T(8,128)(2,1)S(1)}, u32[]{:S(2)}, u32[]{:S(2)}) collective-permute-start(bf16[256,2048]{1,0:T(8,128)(2,1)S(1)} %copy-done.29), channel_id=1, source_target_pairs={{0,2},{1,3},{2,0},{3,1},{4,6},{5,7},{6,4},{7,5},{8,10},{9,11},{10,... | collective-permute-start | bytes 3145736 | tf_op jit(solution)/shard_map/ppermute | solution.py:52
  71.2 34.8 %collective-permute-start.21 = (bf16[256,2048]{1,0:T(8,128)(2,1)S(1)}, bf16[256,2048]{1,0:T(8,128)(2,1)S(1)}, u32[]{:S(2)}, u32[]{:S(2)}) collective-permute-start(bf16[256,2048]{1,0:T(8,128)(2,1)S(1)} %copy-done.29), channel_id=1, source_target_pairs={{0,1},{1,0},{2,3},{3,2},{4,5},{5,4},{6,7},{7,6},{8,9},{9,8},{10,11... | collective-permute-start | bytes 3145736 | tf_op jit(solution)/shard_map/ppermute | solution.py:56
  71.9 12.7 %collective-permute-start.17 = (bf16[96,2048]{1,0:T(8,128)(2,1)S(1)}, bf16[96,2048]{1,0:T(8,128)(2,1)S(1)}, u32[]{:S(2)}, u32[]{:S(2)}) collective-permute-start(bf16[96,2048]{1,0:T(8,128)(2,1)S(1)} %collective-permute-done.16), channel_id=1, source_target_pairs={{0,32},{16,48},{32,64},{48,80},{64,96},{80,112},{96,0},{112,16},{1... | collective-permute-start | bytes 1179656 | tf_op jit(solution)/shard_map/ppermute | solution.py:28
  72.9 14.0 %collective-permute-start.18 = (bf16[96,2048]{1,0:T(8,128)(2,1)S(1)}, bf16[96,2048]{1,0:T(8,128)(2,1)S(1)}, u32[]{:S(2)}, u32[]{:S(2)}) collective-permute-start(bf16[96,2048]{1,0:T(8,128)(2,1)S(1)} %collective-permute-done.16), channel_id=1, source_target_pairs={{0,96},{16,112},{32,0},{48,16},{64,32},{80,48},{96,64},{112,80},{1... | collective-permute-start | bytes 1179656 | tf_op jit(solution)/shard_map/ppermute | solution.py:32
  84.7 22.4 %collective-permute-start.3 = (bf16[256,2048]{1,0:T(8,128)(2,1)S(1)}, bf16[256,2048]{1,0:T(8,128)(2,1)S(1)}, u32[]{:S(2)}, u32[]{:S(2)}) collective-permute-start(bf16[256,2048]{1,0:T(8,128)(2,1)S(1)} %copy-done.30), channel_id=1, source_target_pairs={{0,1},{1,0},{2,3},{3,2},{4,5},{5,4},{6,7},{7,6},{8,9},{9,8},{10,11... | collective-permute-start | bytes 3145736 | tf_op jit(solution)/shard_map/ppermute | solution.py:56
  102.0 13.3 %collective-permute-start.32 = (bf16[128,1536]{1,0:T(8,128)(2,1)S(1)}, bf16[128,1536]{1,0:T(8,128)(2,1)S(1)}, u32[]{:S(2)}, u32[]{:S(2)}) collective-permute-start(bf16[128,1536]{1,0:T(8,128)(2,1)S(1)} %slice.363), channel_id=1, source_target_pairs={{0,32},{16,48},{32,64},{48,80},{64,96},{80,112},{96,0},{112,16},{1... | collective-permute-start | bytes 1179656 | tf_op jit(solution)/shard_map/ppermute | solution.py:28
  102.7 18.2 %collective-permute-start.33 = (bf16[128,1536]{1,0:T(8,128)(2,1)S(1)}, bf16[128,1536]{1,0:T(8,128)(2,1)S(1)}, u32[]{:S(2)}, u32[]{:S(2)}) collective-permute-start(bf16[128,1536]{1,0:T(8,128)(2,1)S(1)} %slice.364), channel_id=1, source_target_pairs={{0,96},{16,112},{32,0},{48,16},{64,32},{80,48},{96,64},{112,80},{1... | collective-permute-start | bytes 1179656 | tf_op jit(solution)/shard_map/ppermute | solution.py:32
  105.9 24.0 %collective-permute-start.35 = (bf16[256,1536]{1,0:T(8,128)(2,1)}, bf16[256,1536]{1,0:T(8,128)(2,1)S(1)}, u32[]{:S(2)}, u32[]{:S(2)}) collective-permute-start(bf16[256,1536]{1,0:T(8,128)(2,1)} %collective-permute-done.34), channel_id=1, source_target_pairs={{0,32},{16,48},{32,64},{48,80},{64,96},{80,112},{96,0},{112,16},{1... | collective-permute-start | bytes 2359304 | tf_op jit(solution)/shard_map/ppermute | solution.py:28
  107.1 22.9 %collective-permute-start.36 = (bf16[256,1536]{1,0:T(8,128)(2,1)}, bf16[256,1536]{1,0:T(8,128)(2,1)S(1)}, u32[]{:S(2)}, u32[]{:S(2)}) collective-permute-start(bf16[256,1536]{1,0:T(8,128)(2,1)} %collective-permute-done.34), channel_id=1, source_target_pairs={{0,96},{16,112},{32,0},{48,16},{64,32},{80,48},{96,64},{112,80},{1... | collective-permute-start | bytes 2359304 | tf_op jit(solution)/shard_map/ppermute | solution.py:32
  115.2 22.3 %collective-permute-start.4 = (bf16[256,2048]{1,0:T(8,128)(2,1)S(1)}, bf16[256,2048]{1,0:T(8,128)(2,1)S(1)}, u32[]{:S(2)}, u32[]{:S(2)}) collective-permute-start(bf16[256,2048]{1,0:T(8,128)(2,1)S(1)} %copy-done.30), channel_id=1, source_target_pairs={{0,2},{1,3},{2,0},{3,1},{4,6},{5,7},{6,4},{7,5},{8,10},{9,11},{10,... | collective-permute-start | bytes 3145736 | tf_op jit(solution)/shard_map/ppermute | solution.py:52
  119.4 30.9 %collective-permute-start.24 = (bf16[96,2048]{1,0:T(8,128)(2,1)S(1)}, bf16[96,2048]{1,0:T(8,128)(2,1)S(1)}, u32[]{:S(2)}, u32[]{:S(2)}) collective-permute-start(bf16[96,2048]{1,0:T(8,128)(2,1)S(1)} %get-tuple-element.113), channel_id=1, source_target_pairs={{0,4},{1,5},{2,6},{3,7},{4,8},{5,9},{6,10},{7,11},{8,12},{9,13},{1... | collective-permute-start | bytes 1179656 | tf_op jit(solution)/shard_map/ppermute | solution.py:40
  120.9 23.8 %collective-permute-start.23 = (bf16[256,2048]{1,0:T(8,128)(2,1)S(1)}, bf16[256,2048]{1,0:T(8,128)(2,1)S(1)}, u32[]{:S(2)}, u32[]{:S(2)}) collective-permute-start(bf16[256,2048]{1,0:T(8,128)(2,1)S(1)} %collective-permute-done.22), channel_id=1, source_target_pairs={{0,1},{1,0},{2,3},{3,2},{4,5},{5,4},{6,7},{7,6},{8,9},{9,8},{10,11... | collective-permute-start | bytes 3145736 | tf_op jit(solution)/shard_map/ppermute | solution.py:56
  130.0 11.1 %collective-permute-start.38 = (bf16[128,1536]{1,0:T(8,128)(2,1)S(1)}, bf16[128,1536]{1,0:T(8,128)(2,1)S(1)}, u32[]{:S(2)}, u32[]{:S(2)}) collective-permute-start(bf16[128,1536]{1,0:T(8,128)(2,1)S(1)} %slice.366), channel_id=1, source_target_pairs={{0,96},{16,112},{32,0},{48,16},{64,32},{80,48},{96,64},{112,80},{1... | collective-permute-start | bytes 1179656 | tf_op jit(solution)/shard_map/ppermute | solution.py:32
  137.6 34.4 %collective-permute-start.26 = (bf16[96,2048]{1,0:T(8,128)(2,1)S(1)}, bf16[96,2048]{1,0:T(8,128)(2,1)S(1)}, u32[]{:S(2)}, u32[]{:S(2)}) collective-permute-start(bf16[96,2048]{1,0:T(8,128)(2,1)S(1)} %get-tuple-element.112), channel_id=1, source_target_pairs={{0,12},{1,13},{2,14},{3,15},{4,0},{5,1},{6,2},{7,3},{8,4},{9,5},{1... | collective-permute-start | bytes 1179656 | tf_op jit(solution)/shard_map/ppermute | solution.py:44
  141.1 44.3 %collective-permute-start.28 = (bf16[96,2048]{1,0:T(8,128)(2,1)S(1)}, bf16[96,2048]{1,0:T(8,128)(2,1)S(1)}, u32[]{:S(2)}, u32[]{:S(2)}) collective-permute-start(bf16[96,2048]{1,0:T(8,128)(2,1)S(1)} %get-tuple-element.111), channel_id=1, source_target_pairs={{0,8},{1,9},{2,10},{3,11},{4,12},{5,13},{6,14},{7,15},{8,0},{9,1},... | collective-permute-start | bytes 1179656 | tf_op jit(solution)/shard_map/ppermute | solution.py:48
  144.7 18.0 %collective-permute-start.6 = (bf16[96,2048]{1,0:T(8,128)(2,1)S(1)}, bf16[96,2048]{1,0:T(8,128)(2,1)S(1)}, u32[]{:S(2)}, u32[]{:S(2)}) collective-permute-start(bf16[96,2048]{1,0:T(8,128)(2,1)S(1)} %get-tuple-element.121), channel_id=1, source_target_pairs={{0,4},{1,5},{2,6},{3,7},{4,8},{5,9},{6,10},{7,11},{8,12},{9,13},{1... | collective-permute-start | bytes 1179656 | tf_op jit(solution)/shard_map/ppermute | solution.py:40
  146.5 53.6 %collective-permute-start.8 = (bf16[96,2048]{1,0:T(8,128)(2,1)S(1)}, bf16[96,2048]{1,0:T(8,128)(2,1)S(1)}, u32[]{:S(2)}, u32[]{:S(2)}) collective-permute-start(bf16[96,2048]{1,0:T(8,128)(2,1)S(1)} %get-tuple-element.120), channel_id=1, source_target_pairs={{0,12},{1,13},{2,14},{3,15},{4,0},{5,1},{6,2},{7,3},{8,4},{9,5},{1... | collective-permute-start | bytes 1179656 | tf_op jit(solution)/shard_map/ppermute | solution.py:44
  150.3 21.1 %collective-permute-start.25 = (bf16[96,2048]{1,0:T(8,128)(2,1)S(1)}, bf16[96,2048]{1,0:T(8,128)(2,1)S(1)}, u32[]{:S(2)}, u32[]{:S(2)}) collective-permute-start(bf16[96,2048]{1,0:T(8,128)(2,1)S(1)} %get-tuple-element.109), channel_id=1, source_target_pairs={{0,4},{1,5},{2,6},{3,7},{4,8},{5,9},{6,10},{7,11},{8,12},{9,13},{1... | collective-permute-start | bytes 1179656 | tf_op jit(solution)/shard_map/ppermute | solution.py:40
  162.7 37.6 %collective-permute-start.10 = (bf16[96,2048]{1,0:T(8,128)(2,1)S(1)}, bf16[96,2048]{1,0:T(8,128)(2,1)S(1)}, u32[]{:S(2)}, u32[]{:S(2)}) collective-permute-start(bf16[96,2048]{1,0:T(8,128)(2,1)S(1)} %get-tuple-element.119), channel_id=1, source_target_pairs={{0,8},{1,9},{2,10},{3,11},{4,12},{5,13},{6,14},{7,15},{8,0},{9,1},... | collective-permute-start | bytes 1179656 | tf_op jit(solution)/shard_map/ppermute | solution.py:48
  171.4 12.0 %collective-permute-start.27 = (bf16[96,2048]{1,0:T(8,128)(2,1)S(1)}, bf16[96,2048]{1,0:T(8,128)(2,1)S(1)}, u32[]{:S(2)}, u32[]{:S(2)}) collective-permute-start(bf16[96,2048]{1,0:T(8,128)(2,1)S(1)} %get-tuple-element.108), channel_id=1, source_target_pairs={{0,12},{1,13},{2,14},{3,15},{4,0},{5,1},{6,2},{7,3},{8,4},{9,5},{1... | collective-permute-start | bytes 1179656 | tf_op jit(solution)/shard_map/ppermute | solution.py:44
  172.1 16.3 %collective-permute-start.29 = (bf16[96,2048]{1,0:T(8,128)(2,1)S(1)}, bf16[96,2048]{1,0:T(8,128)(2,1)S(1)}, u32[]{:S(2)}, u32[]{:S(2)}) collective-permute-start(bf16[96,2048]{1,0:T(8,128)(2,1)S(1)} %get-tuple-element.107), channel_id=1, source_target_pairs={{0,8},{1,9},{2,10},{3,11},{4,12},{5,13},{6,14},{7,15},{8,0},{9,1},... | collective-permute-start | bytes 1179656 | tf_op jit(solution)/shard_map/ppermute | solution.py:48
  183.3 16.6 %collective-permute-start.7 = (bf16[96,2048]{1,0:T(8,128)(2,1)S(1)}, bf16[96,2048]{1,0:T(8,128)(2,1)S(1)}, u32[]{:S(2)}, u32[]{:S(2)}) collective-permute-start(bf16[96,2048]{1,0:T(8,128)(2,1)S(1)} %get-tuple-element.117), channel_id=1, source_target_pairs={{0,4},{1,5},{2,6},{3,7},{4,8},{5,9},{6,10},{7,11},{8,12},{9,13},{1... | collective-permute-start | bytes 1179656 | tf_op jit(solution)/shard_map/ppermute | solution.py:40
  185.4 14.8 %collective-permute-start.9 = (bf16[96,2048]{1,0:T(8,128)(2,1)S(1)}, bf16[96,2048]{1,0:T(8,128)(2,1)S(1)}, u32[]{:S(2)}, u32[]{:S(2)}) collective-permute-start(bf16[96,2048]{1,0:T(8,128)(2,1)S(1)} %get-tuple-element.116), channel_id=1, source_target_pairs={{0,12},{1,13},{2,14},{3,15},{4,0},{5,1},{6,2},{7,3},{8,4},{9,5},{1... | collective-permute-start | bytes 1179656 | tf_op jit(solution)/shard_map/ppermute | solution.py:44
  188.3 16.5 %collective-permute-start.11 = (bf16[96,2048]{1,0:T(8,128)(2,1)S(1)}, bf16[96,2048]{1,0:T(8,128)(2,1)S(1)}, u32[]{:S(2)}, u32[]{:S(2)}) collective-permute-start(bf16[96,2048]{1,0:T(8,128)(2,1)S(1)} %get-tuple-element.115), channel_id=1, source_target_pairs={{0,8},{1,9},{2,10},{3,11},{4,12},{5,13},{6,14},{7,15},{8,0},{9,1},... | collective-permute-start | bytes 1179656 | tf_op jit(solution)/shard_map/ppermute | solution.py:48
  230.7 85.5 %collective-permute-start.41 = (bf16[192,2048]{1,0:T(8,128)(2,1)}, bf16[192,2048]{1,0:T(8,128)(2,1)}, u32[]{:S(2)}, u32[]{:S(2)}) collective-permute-start(bf16[192,2048]{1,0:T(8,128)(2,1)} %get-tuple-element.92), channel_id=1, source_target_pairs={{0,8},{1,9},{2,10},{3,11},{4,12},{5,13},{6,14},{7,15},{8,0},{9,1},... | collective-permute-start | bytes 2359304 | tf_op jit(solution)/shard_map/ppermute | solution.py:48
  235.3 30.2 %all-to-all-start.1 = ((bf16[16,1,48]{2,1,0:T(2,128)(2,1)}), bf16[16,1,48]{2,1,0:T(2,128)(2,1)S(1)}, u32[]{:S(2)}, u32[]{:S(2)}) async-start(bf16[16,1,48]{2,1,0:T(2,128)(2,1)} %copy.85), calls=%async_computation.1 | async-start | bytes 16384 | tf_op jit(solution)/shard_map/all_to_all | solution.py:260
  257.6 13.8 %collective-permute-start.62 = (bf16[48,2048]{1,0:T(8,128)(2,1)}, bf16[48,2048]{1,0:T(8,128)(2,1)}, u32[]{:S(2)}, u32[]{:S(2)}) collective-permute-start(bf16[48,2048]{1,0:T(8,128)(2,1)} %get-tuple-element.83), channel_id=1, source_target_pairs={{0,32},{16,48},{32,64},{48,80},{64,96},{80,112},{96,0},{112,16},{1... | collective-permute-start | bytes 589832 | tf_op jit(solution)/shard_map/ppermute | solution.py:28
  257.6 15.4 %collective-permute-start.66 = (bf16[48,2048]{1,0:T(8,128)(2,1)}, bf16[48,2048]{1,0:T(8,128)(2,1)}, u32[]{:S(2)}, u32[]{:S(2)}) collective-permute-start(bf16[48,2048]{1,0:T(8,128)(2,1)} %get-tuple-element.85), channel_id=1, source_target_pairs={{0,32},{16,48},{32,64},{48,80},{64,96},{80,112},{96,0},{112,16},{1... | collective-permute-start | bytes 589832 | tf_op jit(solution)/shard_map/ppermute | solution.py:28
  258.7 16.1 %collective-permute-start.68 = (bf16[48,2048]{1,0:T(8,128)(2,1)}, bf16[48,2048]{1,0:T(8,128)(2,1)}, u32[]{:S(2)}, u32[]{:S(2)}) collective-permute-start(bf16[48,2048]{1,0:T(8,128)(2,1)} %get-tuple-element.87), channel_id=1, source_target_pairs={{0,96},{16,112},{32,0},{48,16},{64,32},{80,48},{96,64},{112,80},{1... | collective-permute-start | bytes 589832 | tf_op jit(solution)/shard_map/ppermute | solution.py:32
  260.9 15.3 %collective-permute-start.64 = (bf16[48,2048]{1,0:T(8,128)(2,1)}, bf16[48,2048]{1,0:T(8,128)(2,1)}, u32[]{:S(2)}, u32[]{:S(2)}) collective-permute-start(bf16[48,2048]{1,0:T(8,128)(2,1)} %get-tuple-element.89), channel_id=1, source_target_pairs={{0,96},{16,112},{32,0},{48,16},{64,32},{80,48},{96,64},{112,80},{1... | collective-permute-start | bytes 589832 | tf_op jit(solution)/shard_map/ppermute | solution.py:32
  271.4 48.1 %collective-permute-start.40 = (bf16[192,2048]{1,0:T(8,128)(2,1)}, bf16[192,2048]{1,0:T(8,128)(2,1)S(1)}, u32[]{:S(2)}, u32[]{:S(2)}) collective-permute-start(bf16[192,2048]{1,0:T(8,128)(2,1)} %get-tuple-element.93), channel_id=1, source_target_pairs={{0,4},{1,5},{2,6},{3,7},{4,8},{5,9},{6,10},{7,11},{8,12},{9,13},{1... | collective-permute-start | bytes 2359304 | tf_op jit(solution)/shard_map/ppermute | solution.py:40
  272.9 46.6 %collective-permute-start.39 = (bf16[192,2048]{1,0:T(8,128)(2,1)}, bf16[192,2048]{1,0:T(8,128)(2,1)S(1)}, u32[]{:S(2)}, u32[]{:S(2)}) collective-permute-start(bf16[192,2048]{1,0:T(8,128)(2,1)} %get-tuple-element.94), channel_id=1, source_target_pairs={{0,12},{1,13},{2,14},{3,15},{4,0},{5,1},{6,2},{7,3},{8,4},{9,5},{1... | collective-permute-start | bytes 2359304 | tf_op jit(solution)/shard_map/ppermute | solution.py:44
  274.7 12.3 %collective-permute-start.46 = (bf16[128,1536]{1,0:T(8,128)(2,1)}, bf16[128,1536]{1,0:T(8,128)(2,1)S(1)}, u32[]{:S(2)}, u32[]{:S(2)}) collective-permute-start(bf16[128,1536]{1,0:T(8,128)(2,1)} %get-tuple-element.100), channel_id=1, source_target_pairs={{0,96},{16,112},{32,0},{48,16},{64,32},{80,48},{96,64},{112,80},{1... | collective-permute-start | bytes 1179656 | tf_op jit(solution)/shard_map/ppermute | solution.py:32
  276.1 16.7 %collective-permute-start.50 = (bf16[128,1536]{1,0:T(8,128)(2,1)}, bf16[128,1536]{1,0:T(8,128)(2,1)S(1)}, u32[]{:S(2)}, u32[]{:S(2)}) collective-permute-start(bf16[128,1536]{1,0:T(8,128)(2,1)} %get-tuple-element.99), channel_id=1, source_target_pairs={{0,96},{16,112},{32,0},{48,16},{64,32},{80,48},{96,64},{112,80},{1... | collective-permute-start | bytes 1179656 | tf_op jit(solution)/shard_map/ppermute | solution.py:32
  292.8 11.6 %collective-permute-start.48 = (bf16[128,1536]{1,0:T(8,128)(2,1)S(1)}, bf16[128,1536]{1,0:T(8,128)(2,1)S(1)}, u32[]{:S(2)}, u32[]{:S(2)}) collective-permute-start(bf16[128,1536]{1,0:T(8,128)(2,1)S(1)} %copy-done.22), channel_id=1, source_target_pairs={{0,32},{16,48},{32,64},{48,80},{64,96},{80,112},{96,0},{112,16},{1... | collective-permute-start | bytes 1179656 | tf_op jit(solution)/shard_map/ppermute | solution.py:28
  305.6 21.2 %collective-permute-start.65 = (bf16[96,2048]{1,0:T(8,128)(2,1)S(1)}, bf16[96,2048]{1,0:T(8,128)(2,1)S(1)}, u32[]{:S(2)}, u32[]{:S(2)}) collective-permute-start(bf16[96,2048]{1,0:T(8,128)(2,1)S(1)} %pad_maximum_fusion.7), channel_id=1, source_target_pairs={{0,96},{16,112},{32,0},{48,16},{64,32},{80,48},{96,64},{112,80},{1... | collective-permute-start | bytes 1179656 | tf_op jit(solution)/shard_map/ppermute | solution.py:32
  315.0 15.0 %collective-permute-start.63 = (bf16[96,2048]{1,0:T(8,128)(2,1)S(1)}, bf16[96,2048]{1,0:T(8,128)(2,1)S(1)}, u32[]{:S(2)}, u32[]{:S(2)}) collective-permute-start(bf16[96,2048]{1,0:T(8,128)(2,1)S(1)} %pad_maximum_fusion.6), channel_id=1, source_target_pairs={{0,32},{16,48},{32,64},{48,80},{64,96},{80,112},{96,0},{112,16},{1... | collective-permute-start | bytes 1179656 | tf_op jit(solution)/shard_map/ppermute | solution.py:28
  316.2 21.3 %collective-permute-start.51 = (bf16[256,1536]{1,0:T(8,128)(2,1)S(1)}, bf16[256,1536]{1,0:T(8,128)(2,1)S(1)}, u32[]{:S(2)}, u32[]{:S(2)}) collective-permute-start(bf16[256,1536]{1,0:T(8,128)(2,1)S(1)} %pad_maximum_fusion.5), channel_id=1, source_target_pairs={{0,96},{16,112},{32,0},{48,16},{64,32},{80,48},{96,64},{112,80},{1... | collective-permute-start | bytes 2359304 | tf_op jit(solution)/shard_map/ppermute | solution.py:32
  319.5 25.6 %collective-permute-start.49 = (bf16[256,1536]{1,0:T(8,128)(2,1)S(1)}, bf16[256,1536]{1,0:T(8,128)(2,1)S(1)}, u32[]{:S(2)}, u32[]{:S(2)}) collective-permute-start(bf16[256,1536]{1,0:T(8,128)(2,1)S(1)} %pad_maximum_fusion.4), channel_id=1, source_target_pairs={{0,32},{16,48},{32,64},{48,80},{64,96},{80,112},{96,0},{112,16},{1... | collective-permute-start | bytes 2359304 | tf_op jit(solution)/shard_map/ppermute | solution.py:28
  326.8 65.5 %collective-permute-start.47 = (bf16[256,1536]{1,0:T(8,128)(2,1)S(1)}, bf16[256,1536]{1,0:T(8,128)(2,1)S(1)}, u32[]{:S(2)}, u32[]{:S(2)}) collective-permute-start(bf16[256,1536]{1,0:T(8,128)(2,1)S(1)} %pad_maximum_fusion.3), channel_id=1, source_target_pairs={{0,96},{16,112},{32,0},{48,16},{64,32},{80,48},{96,64},{112,80},{1... | collective-permute-start | bytes 2359304 | tf_op jit(solution)/shard_map/ppermute | solution.py:32
  330.0 65.6 %collective-permute-start.45 = (bf16[256,1536]{1,0:T(8,128)(2,1)S(1)}, bf16[256,1536]{1,0:T(8,128)(2,1)S(1)}, u32[]{:S(2)}, u32[]{:S(2)}) collective-permute-start(bf16[256,1536]{1,0:T(8,128)(2,1)S(1)} %pad_maximum_fusion.2), channel_id=1, source_target_pairs={{0,32},{16,48},{32,64},{48,80},{64,96},{80,112},{96,0},{112,16},{1... | collective-permute-start | bytes 2359304 | tf_op jit(solution)/shard_map/ppermute | solution.py:28
  330.1 99.4 %collective-permute-start.42 = (bf16[512,2048]{1,0:T(8,128)(2,1)S(1)}, bf16[512,2048]{1,0:T(8,128)(2,1)S(1)}, u32[]{:S(2)}, u32[]{:S(2)}) collective-permute-start(bf16[512,2048]{1,0:T(8,128)(2,1)S(1)} %pad_maximum_fusion.1), channel_id=1, source_target_pairs={{0,1},{1,0},{2,3},{3,2},{4,5},{5,4},{6,7},{7,6},{8,9},{9,8},{10,11... | collective-permute-start | bytes 6291464 | tf_op jit(solution)/shard_map/ppermute | solution.py:56
  337.5 29.4 %collective-permute-start.71 = (bf16[96,2048]{1,0:T(8,128)(2,1)S(1)}, bf16[96,2048]{1,0:T(8,128)(2,1)S(1)}, u32[]{:S(2)}, u32[]{:S(2)}) collective-permute-start(bf16[96,2048]{1,0:T(8,128)(2,1)S(1)} %get-tuple-element.65), channel_id=1, source_target_pairs={{0,32},{16,48},{32,64},{48,80},{64,96},{80,112},{96,0},{112,16},{1... | collective-permute-start | bytes 1179656 | tf_op jit(solution)/shard_map/ppermute | solution.py:28
  345.1 23.7 %collective-permute-start.72 = (bf16[96,2048]{1,0:T(8,128)(2,1)S(1)}, bf16[96,2048]{1,0:T(8,128)(2,1)S(1)}, u32[]{:S(2)}, u32[]{:S(2)}) collective-permute-start(bf16[96,2048]{1,0:T(8,128)(2,1)S(1)} %get-tuple-element.65), channel_id=1, source_target_pairs={{0,96},{16,112},{32,0},{48,16},{64,32},{80,48},{96,64},{112,80},{1... | collective-permute-start | bytes 1179656 | tf_op jit(solution)/shard_map/ppermute | solution.py:32
  385.9 13.6 %collective-permute-start.52 = (bf16[256,1536]{1,0:T(8,128)(2,1)S(1)}, bf16[256,1536]{1,0:T(8,128)(2,1)S(1)}, u32[]{:S(2)}, u32[]{:S(2)}) collective-permute-start(bf16[256,1536]{1,0:T(8,128)(2,1)S(1)} %add_convert_fusion), channel_id=1, source_target_pairs={{0,16},{16,0},{32,48},{48,32},{64,80},{80,64},{96,112},{112,96},{1... | collective-permute-start | bytes 2359304 | tf_op jit(solution)/shard_map/ppermute | solution.py:36
  392.2 17.5 %collective-permute-start.78 = (bf16[48,2048]{1,0:T(8,128)(2,1)S(1)}, bf16[48,2048]{1,0:T(8,128)(2,1)S(1)}, u32[]{:S(2)}, u32[]{:S(2)}) collective-permute-start(bf16[48,2048]{1,0:T(8,128)(2,1)S(1)} %slice.385), channel_id=1, source_target_pairs={{0,32},{16,48},{32,64},{48,80},{64,96},{80,112},{96,0},{112,16},{1... | collective-permute-start | bytes 589832 | tf_op jit(solution)/shard_map/ppermute | solution.py:28
  392.4 17.7 %collective-permute-start.79 = (bf16[48,2048]{1,0:T(8,128)(2,1)S(1)}, bf16[48,2048]{1,0:T(8,128)(2,1)S(1)}, u32[]{:S(2)}, u32[]{:S(2)}) collective-permute-start(bf16[48,2048]{1,0:T(8,128)(2,1)S(1)} %slice.386), channel_id=1, source_target_pairs={{0,96},{16,112},{32,0},{48,16},{64,32},{80,48},{96,64},{112,80},{1... | collective-permute-start | bytes 589832 | tf_op jit(solution)/shard_map/ppermute | solution.py:32
  405.0 17.6 %collective-permute-start.53 = (bf16[256,1536]{1,0:T(8,128)(2,1)S(1)}, bf16[256,1536]{1,0:T(8,128)(2,1)S(1)}, u32[]{:S(2)}, u32[]{:S(2)}) collective-permute-start(bf16[256,1536]{1,0:T(8,128)(2,1)S(1)} %get-tuple-element.68), channel_id=1, source_target_pairs={{0,32},{16,48},{32,64},{48,80},{64,96},{80,112},{96,0},{112,16},{1... | collective-permute-start | bytes 2359304 | tf_op jit(solution)/shard_map/ppermute | solution.py:28
  405.0 17.7 %collective-permute-start.54 = (bf16[256,1536]{1,0:T(8,128)(2,1)S(1)}, bf16[256,1536]{1,0:T(8,128)(2,1)S(1)}, u32[]{:S(2)}, u32[]{:S(2)}) collective-permute-start(bf16[256,1536]{1,0:T(8,128)(2,1)S(1)} %get-tuple-element.68), channel_id=1, source_target_pairs={{0,96},{16,112},{32,0},{48,16},{64,32},{80,48},{96,64},{112,80},{1... | collective-permute-start | bytes 2359304 | tf_op jit(solution)/shard_map/ppermute | solution.py:32
  409.7 16.4 %collective-permute-start.57 = (bf16[256,1536]{1,0:T(8,128)(2,1)S(1)}, bf16[256,1536]{1,0:T(8,128)(2,1)S(1)}, u32[]{:S(2)}, u32[]{:S(2)}) collective-permute-start(bf16[256,1536]{1,0:T(8,128)(2,1)S(1)} %get-tuple-element.68), channel_id=1, source_target_pairs={{0,16},{16,0},{32,48},{48,32},{64,80},{80,64},{96,112},{112,96},{1... | collective-permute-start | bytes 2359304 | tf_op jit(solution)/shard_map/ppermute | solution.py:36
  422.7 12.9 %collective-permute-start.55 = (bf16[128,1536]{1,0:T(8,128)(2,1)S(1)}, bf16[128,1536]{1,0:T(8,128)(2,1)S(1)}, u32[]{:S(2)}, u32[]{:S(2)}) collective-permute-start(bf16[128,1536]{1,0:T(8,128)(2,1)S(1)} %slice.379), channel_id=1, source_target_pairs={{0,32},{16,48},{32,64},{48,80},{64,96},{80,112},{96,0},{112,16},{1... | collective-permute-start | bytes 1179656 | tf_op jit(solution)/shard_map/ppermute | solution.py:28
  422.8 12.8 %collective-permute-start.56 = (bf16[128,1536]{1,0:T(8,128)(2,1)S(1)}, bf16[128,1536]{1,0:T(8,128)(2,1)S(1)}, u32[]{:S(2)}, u32[]{:S(2)}) collective-permute-start(bf16[128,1536]{1,0:T(8,128)(2,1)S(1)} %slice.380), channel_id=1, source_target_pairs={{0,96},{16,112},{32,0},{48,16},{64,32},{80,48},{96,64},{112,80},{1... | collective-permute-start | bytes 1179656 | tf_op jit(solution)/shard_map/ppermute | solution.py:32
  426.1 22.2 %collective-permute-start.58 = (bf16[256,1536]{1,0:T(8,128)(2,1)S(1)}, bf16[256,1536]{1,0:T(8,128)(2,1)S(1)}, u32[]{:S(2)}, u32[]{:S(2)}) collective-permute-start(bf16[256,1536]{1,0:T(8,128)(2,1)S(1)} %collective-permute-done.57), channel_id=1, source_target_pairs={{0,32},{16,48},{32,64},{48,80},{64,96},{80,112},{96,0},{112,16},{1... | collective-permute-start | bytes 2359304 | tf_op jit(solution)/shard_map/ppermute | solution.py:28
  426.1 22.3 %collective-permute-start.59 = (bf16[256,1536]{1,0:T(8,128)(2,1)S(1)}, bf16[256,1536]{1,0:T(8,128)(2,1)S(1)}, u32[]{:S(2)}, u32[]{:S(2)}) collective-permute-start(bf16[256,1536]{1,0:T(8,128)(2,1)S(1)} %collective-permute-done.57), channel_id=1, source_target_pairs={{0,96},{16,112},{32,0},{48,16},{64,32},{80,48},{96,64},{112,80},{1... | collective-permute-start | bytes 2359304 | tf_op jit(solution)/shard_map/ppermute | solution.py:32
  430.3 21.5 %collective-permute-start.43 = (bf16[256,2048]{1,0:T(8,128)(2,1)S(1)}, bf16[256,2048]{1,0:T(8,128)(2,1)S(1)}, u32[]{:S(2)}, u32[]{:S(2)}) collective-permute-start(bf16[256,2048]{1,0:T(8,128)(2,1)S(1)} %fusion.15), channel_id=1, source_target_pairs={{0,2},{1,3},{2,0},{3,1},{4,6},{5,7},{6,4},{7,5},{8,10},{9,11},{10,... | collective-permute-start | bytes 3145736 | tf_op jit(solution)/shard_map/ppermute | solution.py:52
  (53 other events, 555.0 us)

commit v2 on v0

v2 whole, which is shorter than its diff:
```python
import jax
import jax.numpy as jnp
from jax import lax
from jax.experimental import pallas as pl
from jax.experimental.pallas import tpu as pltpu
from jax.sharding import PartitionSpec as P

beta_first = 0.9
beta_second = 0.95
learn_rate = 0.01
weight_decay = 0.1
adam_epsilon = 1e-08
bias_first = 0.9999734386
bias_second = 0.9940794708

F32 = jnp.float32
BF16 = jnp.bfloat16

Z_UP = [(i, (i + 2) % 8) for i in range(8)]
Z_DOWN = [(i, (i - 2) % 8) for i in range(8)]
Y_SWAP = [(i, i ^ 1) for i in range(8)]


def z_up(a):
    return lax.ppermute(a, "dp", Z_UP)


def z_down(a):
    return lax.ppermute(a, "dp", Z_DOWN)


def y_swap(a):
    return lax.ppermute(a, "dp", Y_SWAP)


def adam_update(master, moment, second, grad):
    moment_next = beta_first * moment + (1.0 - beta_first) * grad
    second_next = beta_second * second + (1.0 - beta_second) * grad * grad
    step_size = moment_next / bias_first / (jnp.sqrt(second_next / bias_second) + adam_epsilon)
    master_next = master - learn_rate * (step_size + weight_decay * master)
    return (master_next, moment_next, second_next)


CAP = 48
HALF_SLOTS = 8 * CAP
SLOTS = 16 * CAP
TOK = 256
WIDTH = 2048
EXTRA = 128
VMEM_LIMIT = 48 * 1024 * 1024
YH_SWAP = [(i, i ^ 2) for i in range(16)]
X_GROUPS = [[x * 4 + h * 2 + c for x in range(4) for c in range(2)] for h in range(2)]


def yh_swap(a):
    return lax.ppermute(a, "expert", YH_SWAP)


def exchange(rows):
    return lax.all_to_all(
        rows.reshape(8, rows.shape[0] // 8, rows.shape[1]),
        "expert",
        split_axis=0,
        concat_axis=0,
        axis_index_groups=X_GROUPS,
        tiled=True,
    ).reshape(rows.shape)


def one_hots(aux_ref):
    number = lax.broadcasted_iota(jnp.int32, (HALF_SLOTS, TOK), 0)
    pos = aux_ref[0:2, :].astype(jnp.int32)
    return number == pos[0:1, :], number == pos[1:2, :]


def as_bf16(mask):
    return mask.astype(F32).astype(BF16)


def route_kernel(half_ref, ids_ref, gate_ref, near_ref, far_ref):
    ids0, ids1 = ids_ref[0:1, :], ids_ref[1:2, :]
    expert = lax.broadcasted_iota(jnp.int32, (16, TOK), 0)
    hit0 = expert == ids0
    hit1 = expert == ids1
    ahead = as_bf16(
        lax.broadcasted_iota(jnp.int32, (TOK, TOK), 0)
        < lax.broadcasted_iota(jnp.int32, (TOK, TOK), 1)
    )
    one0 = hit0.astype(F32)
    before0 = jnp.dot(as_bf16(hit0), ahead, preferred_element_type=F32)
    before1 = jnp.dot(as_bf16(hit1), ahead, preferred_element_type=F32)
    before1 = before1 + jnp.sum(one0, axis=1, keepdims=True)
    slot0 = jnp.sum(jnp.where(hit0, before0, 0.0), axis=0, keepdims=True)
    slot1 = jnp.sum(jnp.where(hit1, before1, 0.0), axis=0, keepdims=True)

    def place_in(ids, slot):
        return (((ids >> 2) * 2 + (ids & 1)) * CAP).astype(F32) + slot

    place0, place1 = place_in(ids0, slot0), place_in(ids1, slot1)
    here0 = ((ids0 >> 1) & 1) == half_ref[0]
    here1 = ((ids1 >> 1) & 1) == half_ref[0]
    near_ref[0:1, :] = jnp.where(here0, place0, -1.0)
    near_ref[1:2, :] = jnp.where(here1, place1, -1.0)
    far_ref[0:1, :] = jnp.where(here0, -1.0, place0)
    far_ref[1:2, :] = jnp.where(here1, -1.0, place1)
    near_ref[2:4, :] = gate_ref[...]
    far_ref[2:4, :] = gate_ref[...]

    def back_in(ids, slot):
        return (((ids >> 2) * 2 + (ids & 1)) * 2 * CAP).astype(F32) + slot

    back0, back1 = back_in(ids0, slot0), back_in(ids1, slot1)
    near_ref[4:5, :] = jnp.where(here0, back0, -1.0)
    near_ref[5:6, :] = jnp.where(here1, back1, -1.0)
    far_ref[4:5, :] = jnp.where(here0, -1.0, back0 + CAP)
    far_ref[5:6, :] = jnp.where(here1, -1.0, back1 + CAP)
    near_ref[6:8, :] = gate_ref[...]
    far_ref[6:8, :] = gate_ref[...]


def fill_tokens(column_ref, chosen, tok_ref, out_ref):
    for i in range(8):
        source = pl.multiple_of(column_ref[i] * 256, 256)
        out_ref[:, i * 256 : (i + 1) * 256] = jnp.dot(
            chosen, tok_ref[:, pl.ds(source, 256)], preferred_element_type=F32
        ).astype(BF16)


def fill_grads(first, second, chosen, aux_ref, grad_ref, out_ref, at):
    for i in range(8):
        out_ref[:, at + i * 256 : at + (i + 1) * 256] = jnp.dot(
            chosen, grad_ref[:, i * 256 : (i + 1) * 256], preferred_element_type=F32
        ).astype(BF16)
    gate = jnp.sum(
        jnp.where(first, aux_ref[2:3, :], 0.0) + jnp.where(second, aux_ref[3:4, :], 0.0),
        axis=1,
        keepdims=True,
    )
    out_ref[:, at + WIDTH :] = jnp.broadcast_to(gate, (HALF_SLOTS, EXTRA)).astype(BF16)


def spread_kernel(column_ref, aux_ref, tok_ref, grad_ref, out_ref):
    first, second = one_hots(aux_ref)
    chosen = as_bf16(first | second)
    fill_tokens(column_ref, chosen, tok_ref, out_ref)
    fill_grads(first, second, chosen, aux_ref, grad_ref, out_ref, WIDTH)


def spread_tokens_kernel(column_ref, aux_ref, tok_ref, out_ref):
    first, second = one_hots(aux_ref)
    fill_tokens(column_ref, as_bf16(first | second), tok_ref, out_ref)


def spread_grads_kernel(aux_ref, grad_ref, out_ref):
    first, second = one_hots(aux_ref)
    fill_grads(first, second, as_bf16(first | second), aux_ref, grad_ref, out_ref, 0)


def collect_kernel(near_aux_ref, far_aux_ref, rows_ref, near_ref, far_ref):
    to_tokens = (((0,), (0,)), ((), ()))
    number = lax.broadcasted_iota(jnp.int32, (SLOTS, TOK), 0)
    for aux_ref, out_ref in ((near_aux_ref, near_ref), (far_aux_ref, far_ref)):
        pos = aux_ref[4:6, :].astype(jnp.int32)
        first, second = number == pos[0:1, :], number == pos[1:2, :]
        out_ref[:, :WIDTH] = lax.dot_general(
            as_bf16(first | second),
            rows_ref[:, :WIDTH],
            to_tokens,
            preferred_element_type=F32,
        ).astype(out_ref.dtype)
        score = rows_ref[:, WIDTH:]
        score0 = lax.dot_general(as_bf16(first), score, to_tokens, preferred_element_type=F32)
        score1 = lax.dot_general(as_bf16(second), score, to_tokens, preferred_element_type=F32)
        lane = lax.broadcasted_iota(jnp.int32, (TOK, EXTRA), 1)
        out_ref[:, WIDTH:] = jnp.where(lane == 0, score0, score1).astype(out_ref.dtype)


def finish_kernel(column_ref, near_ref, far_ref, out_ref, score_ref):
    for i in range(8):
        target = pl.multiple_of(column_ref[i] * 256, 256)
        part = slice(i * 256, (i + 1) * 256)
        out_ref[:, pl.ds(target, 256)] = (near_ref[:, part] + far_ref[:, part].astype(F32)).astype(
            BF16
        )
    score_ref[...] = (near_ref[:, WIDTH:] + far_ref[:, WIDTH:].astype(F32)).astype(BF16)


HIDDEN = 768
SCALE_IN = WIDTH ** (-0.5)
SCALE_OUT = HIDDEN ** (-0.5)
BOTH = (slice(0, HALF_SLOTS), slice(HALF_SLOTS, SLOTS))
TN = (((0,), (0,)), ((), ()))
NT = (((1,), (1,)), ((), ()))


def dot(a, b, dims=(((1,), (0,)), ((), ()))):
    return lax.dot_general(a, b, dims, preferred_element_type=F32)


def pack_down(down):
    tail = [down[32 * j : 32 * j + 32, 1536:] for j in range(3)]
    return jnp.concatenate([down[:, :1536], jnp.concatenate(tail, axis=1)], axis=0)


def unpack_down(packed):
    tail = [packed[96:128, 512 * j : 512 * j + 512] for j in range(3)]
    return jnp.concatenate([packed[:96], jnp.concatenate(tail, axis=0)], axis=1)


def gate_up_parts(refs):
    own, other, below, above, up2, down2, up3, down3 = refs
    return [
        [(own, 0, 256)],
        [(other, 0, 256)],
        [(above, 0, 256)],
        [(down2, 192, 256)],
        [(up2, 0, 128), (down2, 0, 128)],
        [(up3, 0, 128), (down3, 0, 128)],
        [(below, 0, 256)],
        [(up2, 192, 256)],
    ]


def down_parts(refs):
    own, other, below, above, up2, down2, up3, down3 = refs
    return [
        [(own, 256, 128)],
        [(other, 256, 128)],
        [(above, 256, 128)],
        [(down2, 448, 128)],
        [(up2, 128, 64), (down2, 128, 64)],
        [(up3, 128, 64), (down3, 128, 64)],
        [(below, 256, 128)],
        [(up2, 448, 128)],
    ]


def read(pieces, columns):
    got = [ref[at : at + rows, columns] for ref, at, rows in pieces]
    return got[0] if len(got) == 1 else jnp.concatenate(got, axis=0)


def forward_kernel(column_ref, near_ref, far_ref, *refs):
    weights, (act_ref, slope_ref, swish_ref, down_ref) = refs[:8], refs[8:]
    blocks = gate_up_parts(weights)
    for rows, x_ref in zip(BOTH, (near_ref, far_ref)):
        for f in range(3):
            lo = slice(f * 256, f * 256 + 256)
            hi = slice(HIDDEN + f * 256, HIDDEN + f * 256 + 256)
            gate = jnp.zeros((HALF_SLOTS, 256), F32)
            up = jnp.zeros((HALF_SLOTS, 256), F32)
            for i, pieces in enumerate(blocks):
                x = x_ref[:, i * 256 : i * 256 + 256]
                gate += dot(x, read(pieces, lo))
                up += dot(x, read(pieces, hi))
            gate = gate * SCALE_IN
            up = up * SCALE_IN
            sig = jax.nn.sigmoid(gate)
            swish = gate * sig
            act_ref[rows, lo] = (swish * up).astype(BF16)
            slope_ref[rows, lo] = up * sig * (1.0 + gate * (1.0 - sig))
            swish_ref[rows, lo] = swish
    for i, pieces in enumerate(down_parts(weights)):
        row = pl.multiple_of(column_ref[i] * 96, 32)
        packed = read(pieces, slice(None))
        down_ref[pl.ds(row, 96), :1536] = packed[:96]
        for j in range(3):
            down_ref[pl.ds(row + 32 * j, 32), 1536:] = packed[96:128, 512 * j : 512 * j + 512]


def backward_kernel(
    column_ref,
    near_ref,
    far_in_ref,
    far_grad_ref,
    act_ref,
    slope_ref,
    swish_ref,
    down_ref,
    proj_ref,
    far_plane_ref,
    parts_ref,
    scaled_ref,
    whole_ref,
):
    for rows, grad_ref, at in ((BOTH[0], near_ref, WIDTH), (BOTH[1], far_grad_ref, 0)):
        gate = grad_ref[:, at + WIDTH : at + WIDTH + EXTRA].astype(F32)
        gate = gate[:, 0:1]
        for n in range(4):
            grad = grad_ref[:, at + n * 512 : at + n * 512 + 512].astype(F32)
            scaled_ref[rows, n * 512 : n * 512 + 512] = (gate * grad).astype(BF16)
    for rows in BOTH:
        for f in range(3):
            lo = slice(f * 256, f * 256 + 256)
            grad_act = SCALE_OUT * dot(scaled_ref[rows, :], down_ref[lo, :], NT)
            proj_ref[rows, lo] = (grad_act * slope_ref[rows, lo]).astype(BF16)
            proj_ref[rows, HIDDEN + f * 256 : HIDDEN + f * 256 + 256] = (
                grad_act * swish_ref[rows, lo]
            ).astype(BF16)
    plane_product(near_ref, far_in_ref, proj_ref, far_plane_ref, 2)
    for n in range(4):
        part = slice(n * 512, n * 512 + 512)
        for f in range(3):
            lo = slice(f * 256, f * 256 + 256)
            whole_ref[lo, part] = (SCALE_OUT * dot(act_ref[:, lo], scaled_ref[:, part], TN)).astype(
                BF16
            )
    for i in range(8):
        row = pl.multiple_of(column_ref[i] * 96, 32)
        parts_ref[i, 0:96, :] = whole_ref[pl.ds(row, 96), :1536]
        for j in range(3):
            parts_ref[i, 96:128, 512 * j : 512 * j + 512] = whole_ref[
                pl.ds(row + 32 * j, 32), 1536:
            ]


def plane_product(near_ref, far_ref, proj_ref, out_ref, k):
    for half in range(2):
        at = k * 512 + half * 256
        for n in range(3):
            part = slice(n * 512, n * 512 + 512)
            total = dot(near_ref[:, at : at + 256], proj_ref[BOTH[0], part], TN)
            total += dot(far_ref[:, at : at + 256], proj_ref[BOTH[1], part], TN)
            out_ref[half * 256 : half * 256 + 256, part] = (SCALE_IN * total).astype(BF16)


def planes_kernel(near_ref, far_ref, proj_ref, above_ref, below_ref, own_ref):
    for k, out_ref in ((1, above_ref), (3, below_ref), (0, own_ref)):
        plane_product(near_ref, far_ref, proj_ref, out_ref, k)


def back_kernel(near_ref, far_grad_ref, act_ref, proj_ref, down_ref, *refs):
    blocks, out_ref = gate_up_parts(refs[:8]), refs[8]
    for which, (rows, grad_ref, at) in enumerate(
        ((BOTH[0], near_ref, WIDTH), (BOTH[1], far_grad_ref, 0))
    ):

        def store(columns, value):
            value = value.astype(BF16)
            for i in range(8):
                out_ref[i * 96 + which * 48 : i * 96 + which * 48 + 48, columns] = value[
                    i * 48 : i * 48 + 48
                ]

        for i, pieces in enumerate(blocks):
            route = SCALE_IN * dot(proj_ref[rows, :], read(pieces, slice(None)), NT)
            store(slice(i * 256, i * 256 + 256), route)
        score = jnp.zeros((HALF_SLOTS, 1), F32)
        for n in range(8):
            part = slice(n * 256, n * 256 + 256)
            out = SCALE_OUT * dot(act_ref[rows, :], down_ref[:, part])
            grad = grad_ref[:, at + n * 256 : at + n * 256 + 256].astype(F32)
            score += jnp.sum(grad * out, axis=1, keepdims=True)
        store(slice(WIDTH, WIDTH + EXTRA), jnp.broadcast_to(score, (HALF_SLOTS, EXTRA)))


def add(*refs_or_values):
    total = refs_or_values[0].astype(F32)
    for value in refs_or_values[1:]:
        total = total + value.astype(F32)
    return total


def second_kernel(far_ref, above_ref, below_ref, parts_ref, up_ref, down_ref, y_ref, o_up, o_down):
    o_up[0:128] = add(above_ref[256:384], up_ref[...]).astype(BF16)
    o_up[128:256] = above_ref[384:512]
    o_up[256:384] = far_ref[0:128]
    o_up[384:448] = add(parts_ref[4, 0:64], y_ref[0:64]).astype(BF16)
    o_down[0:128] = below_ref[256:384]
    o_down[128:256] = add(below_ref[384:512], down_ref[...]).astype(BF16)
    o_down[256:384] = far_ref[128:256]
    o_down[384:448] = add(parts_ref[4, 64:128], y_ref[64:128]).astype(BF16)


def third_kernel(
    above_ref, below_ref, own_ref, parts_ref, up_ref, down_ref, y_ref, o_up, o_down, o_y
):
    o_up[0:128] = add(above_ref[0:128], up_ref[256:384]).astype(BF16)
    o_up[128:256] = above_ref[128:256]
    o_up[256:320] = add(parts_ref[2, 0:64], y_ref[0:64], up_ref[384:448]).astype(BF16)
    o_up[320:384] = add(parts_ref[2, 64:128], y_ref[64:128]).astype(BF16)
    o_down[0:128] = below_ref[0:128]
    o_down[128:256] = add(below_ref[128:256], down_ref[256:384]).astype(BF16)
    o_down[256:320] = add(parts_ref[6, 0:64], y_ref[128:192]).astype(BF16)
    o_down[320:384] = add(parts_ref[6, 64:128], y_ref[192:256], down_ref[384:448]).astype(BF16)
    o_y[0:256] = add(own_ref[256:512], up_ref[0:256], down_ref[0:256]).astype(BF16)
    o_y[256:384] = parts_ref[1]


def update_kernel(
    own_ref, parts_ref, up_ref, down_ref, y_ref, w_gu, w_dn, m_gu, m_dn, s_gu, s_dn, out_ref, sum_ref
):
    grad = add(own_ref[0:256], up_ref[0:256], down_ref[0:256], y_ref[0:256])
    out_ref[0:256] = adam_update(w_gu[...], m_gu[...], s_gu[...], grad)[0].astype(BF16)
    sum_ref[...] = add(parts_ref[0], up_ref[256:384], down_ref[256:384], y_ref[256:384])
    new = adam_update(
        w_dn[:, :1536], m_dn[:, :1536], s_dn[:, :1536], sum_ref[0:96, :]
    )[0]
    out_ref[256:352] = new.astype(BF16)
    for j in range(3):
        rows = slice(32 * j, 32 * j + 32)
        part = slice(512 * j, 512 * j + 512)
        new = adam_update(
            w_dn[rows, 1536:], m_dn[rows, 1536:], s_dn[rows, 1536:], sum_ref[96:128, part]
        )[0]
        out_ref[352:384, part] = new.astype(BF16)


def tie(*arrays):
    return lax.optimization_barrier(arrays)


def place(full, block, shard):
    return lax.dynamic_update_slice(full, block, (shard * block.shape[0], 0))


def assemble(blocks, z, y):
    rows, columns = blocks[(0, 0)].shape
    full = jnp.zeros((8 * rows, columns), BF16)
    for (k, dy), block in blocks.items():
        full = place(full, block, ((z + k) % 4) * 2 + (y ^ dy))
    return full


def bf(*shape):
    return jax.ShapeDtypeStruct(shape, BF16)


def f32(*shape):
    return jax.ShapeDtypeStruct(shape, F32)


def call(kernel, outs, inputs, scalars=0, scratch=(), flops=0):
    vmem = pl.BlockSpec(memory_space=pltpu.VMEM)
    smem = pl.BlockSpec(memory_space=pltpu.SMEM)
    moved = sum(a.size * a.dtype.itemsize for a in inputs) + sum(
        o.size * o.dtype.itemsize for o in outs
    )
    got = pl.pallas_call(
        kernel,
        out_shape=outs,
        in_specs=[smem] * scalars + [vmem] * (len(inputs) - scalars),
        out_specs=(vmem,) * len(outs),
        scratch_shapes=scratch,
        cost_estimate=pl.CostEstimate(flops=flops, bytes_accessed=moved, transcendentals=0),
        compiler_params=pltpu.CompilerParams(vmem_limit_bytes=VMEM_LIMIT),
    )(*inputs)
    return got if len(outs) > 1 else got[0]


def local(
    tokens,
    out_grad,
    expert_ids,
    gate_values,
    master_gate_up,
    master_down,
    moment_gate_up,
    moment_down,
    second_gate_up,
    second_down,
):
    r = lax.axis_index("dp")
    z, y = r // 2, r % 2
    order = [(k, dy) for k in range(4) for dy in range(2)]
    columns = jnp.stack([((z + k) % 4) * 2 + (y ^ dy) for k, dy in order])
    half = ((lax.axis_index("expert") >> 1) & 1).reshape(1)

    own = jnp.concatenate(
        [master_gate_up[0].astype(BF16), pack_down(master_down[0].astype(BF16))], axis=0
    )
    near_aux, far_aux = call(
        route_kernel,
        (f32(8, TOK), f32(8, TOK)),
        (half, expert_ids.T, gate_values.astype(F32).T),
        scalars=1,
    )
    near = exchange(
        call(
            spread_kernel,
            (bf(HALF_SLOTS, 2 * WIDTH + EXTRA),),
            (columns, near_aux, tokens, out_grad),
            scalars=1,
        )
    )
    below, above, other = z_up(own), z_down(own), y_swap(own)
    their_aux = yh_swap(far_aux)
    below, above, other, their_aux, tok_next = tie(below, above, other, their_aux, tokens)

    up2 = z_up(jnp.concatenate([below[:128], below[256:320], other], axis=0))
    down2 = z_down(jnp.concatenate([above[128:256], above[320:384], other], axis=0))
    their_tok = yh_swap(tok_next)
    their_tok, grad_next = tie(their_tok, out_grad)
    their_grad = yh_swap(grad_next)
    send_far = call(
        spread_tokens_kernel,
        (bf(HALF_SLOTS, WIDTH),),
        (columns, their_aux, their_tok),
        scalars=1,
    )
    send_far, near = tie(send_far, near)
    far_in = exchange(send_far)
    up2, down2, their_grad = tie(up2, down2, their_grad)

    up3 = z_up(jnp.concatenate([up2[192:320], up2[448:512]], axis=0))
    down3 = z_down(jnp.concatenate([down2[320:448], down2[512:576]], axis=0))
    send_far = call(spread_grads_kernel, (bf(HALF_SLOTS, WIDTH + EXTRA),), (their_aux, their_grad))
    send_far, far_in = tie(send_far, far_in)
    far_grad = exchange(send_far)
    up3, down3, far_in = tie(up3, down3, far_in)
    weights = (own, other, below, above, up2, down2, up3, down3)

    act, slope, swish, down = call(
        forward_kernel,
        (
            bf(SLOTS, HIDDEN),
            f32(SLOTS, HIDDEN),
            f32(SLOTS, HIDDEN),
            bf(HIDDEN, WIDTH),
        ),
        (columns, near, far_in) + weights,
        scalars=1,
        flops=4_800_000_000,
    )
    proj, far_plane, parts = call(
        backward_kernel,
        (bf(SLOTS, 2 * HIDDEN), bf(512, 1536), bf(8, 128, 1536)),
        (columns, near, far_in, far_grad, act, slope, swish, down),
        scalars=1,
        scratch=(pltpu.VMEM((SLOTS, WIDTH), BF16), pltpu.VMEM((HIDDEN, WIDTH), BF16)),
        flops=6_000_000_000,
    )

    t_up = z_up(far_plane[256:384])
    t_down = z_down(far_plane[384:512])
    t_y = y_swap(parts[5])
    above_plane, below_plane, own_plane = call(
        planes_kernel,
        (bf(512, 1536),) * 3,
        (near, far_in, proj),
        flops=3_600_000_000,
    )
    t_up, t_down, t_y, above_plane, below_plane, own_plane, late_proj = tie(
        t_up, t_down, t_y, above_plane, below_plane, own_plane, proj
    )
    s_up, s_down = call(
        second_kernel,
        (bf(448, 1536), bf(448, 1536)),
        (far_plane, above_plane, below_plane, parts, t_up, t_down, t_y),
    )
    s_y = jnp.concatenate([parts[3], parts[7]], axis=0)
    t_up, t_down, t_y = z_up(s_up), z_down(s_down), y_swap(s_y)
    back = call(
        back_kernel,
        (bf(SLOTS, WIDTH + EXTRA),),
        (near, far_grad, act, late_proj, down) + weights,
        flops=7_200_000_000,
    )
    t_up, t_down, t_y, back = tie(t_up, t_down, t_y, back)
    s_up, s_down, s_y = call(
        third_kernel,
        (bf(384, 1536),) * 3,
        (above_plane, below_plane, own_plane, parts, t_up, t_down, t_y),
    )
    t_up, t_down, t_y = z_up(s_up), z_down(s_down), y_swap(s_y)
    returned = exchange(back)
    t_up, t_down, t_y = tie(t_up, t_down, t_y)
    state = (
        master_gate_up[0],
        master_down[0],
        moment_gate_up[0],
        moment_down[0],
        second_gate_up[0],
        second_down[0],
    )
    new_own = call(
        update_kernel,
        (bf(384, 1536),),
        (own_plane, parts, t_up, t_down, t_y) + state,
        scratch=(pltpu.VMEM((128, 1536), F32),),
    )

    below, above, other = z_up(new_own), z_down(new_own), y_swap(new_own)
    grad_gate_up = add(own_plane[:256], t_up[:256], t_down[:256], t_y[:256])
    grad_down = unpack_down(add(parts[0], t_up[256:], t_down[256:], t_y[256:]))
    master_gu_next, moment_gu_next, second_gu_next = adam_update(
        state[0], state[2], state[4], grad_gate_up
    )
    master_dn_next, moment_dn_next, second_dn_next = adam_update(
        state[1], state[3], state[5], grad_down
    )
    below, above, other, returned = tie(below, above, other, returned)
    gu = {(0, 0): new_own[:256], (3, 0): below[:256], (1, 0): above[:256], (0, 1): other[:256]}
    dn = {(0, 0): new_own[256:], (3, 0): below[256:], (1, 0): above[256:], (0, 1): other[256:]}
    up2 = z_up(jnp.concatenate([below[:128], below[256:320], other[:256]], axis=0))
    down2 = z_down(jnp.concatenate([above[128:256], above[320:384], other[:256]], axis=0))
    side2 = y_swap(jnp.concatenate([above[256:], below[256:]], axis=0))
    near_sum, far_sum = call(
        collect_kernel,
        (f32(TOK, WIDTH + EXTRA), bf(TOK, WIDTH + EXTRA)),
        (near_aux, their_aux, returned),
        flops=1_700_000_000,
    )
    far_sum = yh_swap(far_sum)
    up2, down2, side2 = tie(up2, down2, side2)
    gu[(2, 0)] = jnp.concatenate([up2[:128], down2[:128]], axis=0)
    dn[(2, 0)] = jnp.concatenate([up2[128:192], down2[128:192]], axis=0)
    gu[(3, 1)], gu[(1, 1)] = up2[192:], down2[192:]
    dn[(1, 1)], dn[(3, 1)] = side2[:128], side2[128:]
    up3, down3, side3 = z_up(up2[192:320]), z_down(down2[320:448]), y_swap(dn[(2, 0)])
    gu[(2, 1)] = jnp.concatenate([up3, down3], axis=0)
    dn[(2, 1)] = side3
    new_gate_up = assemble(gu, z, y)
    new_down = assemble({at: unpack_down(block) for at, block in dn.items()}, z, y)

    input_grad, scores = call(
        finish_kernel,
        (bf(TOK, WIDTH), bf(TOK, EXTRA)),
        (columns, near_sum, far_sum),
        scalars=1,
    )
    gate_grad = scores[:, :2]
    return (
        input_grad,
        gate_grad,
        new_gate_up[None],
        new_down[None],
        master_gu_next[None],
        master_dn_next[None],
        moment_gu_next[None],
        moment_dn_next[None],
        second_gu_next[None],
        second_dn_next[None],
    )


def solution(mesh):
    rows = P(("dp", "expert"), None)
    state = P("expert", "dp", None)
    whole = P("expert", None, None)
    return jax.shard_map(
        local,
        mesh=mesh,
        in_specs=(rows,) * 4 + (state,) * 6,
        out_specs=(rows, rows, whole, whole) + (state,) * 6,
        check_vma=False,
    )
```

time: 757 us -> 370 us (0.49)
  the two profiles are of different devices: /device:TPU:4 before, /device:TPU:16 now
where the time goes in v2:
time: 370 us; the launch traced here: 363 us
  waiting for transfers between devices  146 us (39%)
  Pallas kernels  77.9 us (21%)
  starting transfers between devices  64.5 us (17%)
  local copies, waits for them, and re-layouts  54.3 us (15%)
  other arithmetic  18.8 us (5%)
    pallas_call x13, Pallas kernels, call(): pl.pallas_call(kernel, out_shape=outs, in_specs=[smem] * scalars + [vmem]...  77.9 us
    ppermute x4, waiting for transfers between devices, yh_swap(): return lax.ppermute(a, 'expert', YH_SWAP)  67.9 us
    ppermute x9, waiting for transfers between devices, z_up(): return lax.ppermute(a, 'dp', Z_UP)  61.2 us
    ppermute x9, starting transfers between devices, z_down(): return lax.ppermute(a, 'dp', Z_DOWN)  27.1 us
    unnamed x89, local copies, waits for them, and re-layouts  26.2 us
    all_to_all x4, starting transfers between devices, exchange(): lax.all_to_all(rows.reshape(8, rows.shape[0] // 8, rows.shape[1]), 'exper...  17.9 us
    ppermute x7, waiting for transfers between devices, y_swap(): return lax.ppermute(a, 'dp', Y_SWAP)  16.3 us
    ppermute x4, starting transfers between devices, yh_swap(): return lax.ppermute(a, 'expert', YH_SWAP)  8.37 us
  transfers between devices with their start and end apart: 33, of which 15 were waited for; matrix products, arithmetic and copies ran while one was open for 10% of the time, Pallas kernels for 13%

profile of v2, /device:TPU:16, one launch (start us, length us, event | category | flops | bytes accessed | tf_op | source)
XLA Modules:
  0.0 363.1 jit_solution(8939540867073717697)
XLA Ops:
  2.4 1.2 copy-done.16
  4.8 3.3 shard_map.179
  8.1 4.6 %all-to-all-start = ((bf16[8,48,4224]{2,1,0:T(8,128)(2,1)}), bf16[8,48,4224]{2,1,0:T(8,128)(2,1)}, u32[]{:S(2)}, u32[]{:S(2)}) async-start(bf16[8,48,4224]{2,1,0:T(8,128)(2,1)} %bitcast.13), calls=%async_computation | async-start | bytes 6488064 | tf_op jit(solution)/shard_map/all_to_all | solution.py:60
  14.0 2.0 collective-permute-start
  16.0 2.2 collective-permute-start.1
  18.2 1.3 collective-permute-start.2
  21.1 25.1 %collective-permute-done.3.aux_ref.far_aux_ref = f32[8,256]{1,0:T(8,128)S(1)} collective-permute-done((f32[8,256]{1,0:T(8,128)S(1)}, f32[8,256]{1,0:T(8,128)S(1)}, u32[]{:S(2)}, u32[]{:S(2)}) %collective-permute-start.3) | collective-permute-done | bytes 8224 | tf_op jit(solution)/shard_map/ppermute | solution.py:56
  46.3 3.0 collective-permute-start.4
  49.4 2.0 pad_maximum_fusion
  51.4 3.2 collective-permute-start.6
  54.7 17.6 %collective-permute-done.4.tok_ref = bf16[256,2048]{1,0:T(8,128)(2,1)S(1)} collective-permute-done((bf16[256,2048]{1,0:T(8,128)(2,1)S(1)}, bf16[256,2048]{1,0:T(8,128)(2,1)S(1)}, u32[]{:S(2)}, u32[]{:S(2)}) %collective-permute-start.4) | collective-permute-done | bytes 1048608 | tf_op jit(solution)/shard_map/ppermute | solution.py:56
  72.3 2.3 shard_map.178
  74.5 4.4 %all-to-all-start.1 = ((bf16[8,48,2048]{2,1,0:T(8,128)(2,1)}), bf16[8,48,2048]{2,1,0:T(8,128)(2,1)S(1)}, u32[]{:S(2)}, u32[]{:S(2)}) async-start(bf16[8,48,2048]{2,1,0:T(8,128)(2,1)} %bitcast.15), calls=%async_computation.1 | async-start | bytes 3145728 | tf_op jit(solution)/shard_map/all_to_all | solution.py:60
  78.9 2.7 collective-permute-start.7
  81.6 10.9 %collective-permute-done.5.refs_4_ = bf16[576,1536]{1,0:T(8,128)(2,1)} collective-permute-done((bf16[576,1536]{1,0:T(8,128)(2,1)}, bf16[576,1536]{1,0:T(8,128)(2,1)}, u32[]{:S(2)}, u32[]{:S(2)}) %collective-permute-start.5) | collective-permute-done | bytes 1769504 | tf_op jit(solution)/shard_map/ppermute | solution.py:25
  92.5 13.5 %collective-permute-done.7.grad_ref = bf16[256,2048]{1,0:T(8,128)(2,1)S(1)} collective-permute-done((bf16[256,2048]{1,0:T(8,128)(2,1)S(1)}, bf16[256,2048]{1,0:T(8,128)(2,1)S(1)}, u32[]{:S(2)}, u32[]{:S(2)}) %collective-permute-start.7) | collective-permute-done | bytes 1048608 | tf_op jit(solution)/shard_map/ppermute | solution.py:56
  106.0 1.6 slice.284
  107.6 1.8 slice.283
  109.4 1.6 slice.286
  112.0 1.8 shard_map.180
  115.0 4.4 %all-to-all-start.2 = ((bf16[8,48,2176]{2,1,0:T(8,128)(2,1)}), bf16[8,48,2176]{2,1,0:T(8,128)(2,1)S(1)}, u32[]{:S(2)}, u32[]{:S(2)}) async-start(bf16[8,48,2176]{2,1,0:T(8,128)(2,1)} %bitcast.17), calls=%async_computation.2 | async-start | bytes 3342336 | tf_op jit(solution)/shard_map/all_to_all | solution.py:60
  119.4 1.3 pad_maximum_fusion.7
  121.8 3.5 collective-permute-start.9
  125.2 12.5 %collective-permute-done.8.refs_6_ = bf16[192,1536]{1,0:T(8,128)(2,1)S(1)} collective-permute-done((bf16[192,1536]{1,0:T(8,128)(2,1)S(1)}, bf16[192,1536]{1,0:T(8,128)(2,1)S(1)}, u32[]{:S(2)}, u32[]{:S(2)}) %collective-permute-start.8) | collective-permute-done | bytes 589856 | tf_op jit(solution)/shard_map/ppermute | solution.py:25
  138.2 1.3 copy-done.21
  139.5 12.6 %shard_map.181 = (bf16[768,768]{1,0:T(8,128)(2,1)S(1)}, f32[768,768]{1,0:T(8,128)}, f32[768,768]{1,0:T(8,128)}, bf16[768,2048]{1,0:T(8,128)(2,1)}) custom-call(s32[8]{0:T(128)S(1)} %stack.35.column_ref, bf16[384,4224]{1,0:T(8,128)(2,1)} %bitcast.14.near_ref, bf16[384,2048]{1,0:T(8,128)(2,1)} %bitcast.112, bf16[384,1536]{1,0:T(8,128)(2,1)S(1)} %copy-done.11, ...), custom_call_target="tpu_custom_call" | custom-call | flops 4800000000 | bytes 23298080 | tf_op jit(solution)/shard_map/pallas_call | solution.py:439
  154.0 2.0 copy-done.9
  156.0 1.3 copy-done.27
  157.2 13.3 %shard_map.182 = (bf16[768,1536]{1,0:T(8,128)(2,1)}, bf16[512,1536]{1,0:T(8,128)(2,1)S(1)}, bf16[8,128,1536]{2,1,0:T(8,128)(2,1)}) custom-call(s32[8]{0:T(128)S(1)} %stack.35.column_ref, bf16[384,4224]{1,0:T(8,128)(2,1)} %bitcast.14.near_ref, bf16[384,2048]{1,0:T(8,128)(2,1)S(1)} %bitcast.114, bf16[384,2176]{1,0:T(8,128)(2,1)S(1)} %bitcast.110, ...), custom_call_target="tpu_custom_call" | custom-call | flops 6000000000 | bytes 22609952 | tf_op jit(solution)/shard_map/pallas_call | solution.py:439
  171.2 3.2 collective-permute-start.11
  174.4 1.3 slice_bitcast_fusion.3
  175.7 1.4 collective-permute-start.12
  177.1 8.2 %shard_map.183 = (bf16[512,1536]{1,0:T(8,128)(2,1)S(1)}, bf16[512,1536]{1,0:T(8,128)(2,1)S(1)}, bf16[512,1536]{1,0:T(8,128)(2,1)S(1)}) custom-call(bf16[384,4224]{1,0:T(8,128)(2,1)} %bitcast.14.near_ref, bf16[384,2048]{1,0:T(8,128)(2,1)} %bitcast.113, bf16[768,1536]{1,0:T(8,128)(2,1)} %get-tuple-element.106.proj_ref), custom_call_target="tpu_custom_call" | custom-call | flops 3600000000 | bytes 11894784 | tf_op jit(solution)/shard_map/pallas_call | solution.py:439
  188.8 3.3 shard_map.184
  192.2 3.2 collective-permute-start.14
  196.5 14.7 %shard_map.185 = bf16[768,2176]{1,0:T(8,128)(2,1)} custom-call(bf16[384,4224]{1,0:T(8,128)(2,1)} %bitcast.14.near_ref, bf16[384,2176]{1,0:T(8,128)(2,1)} %bitcast.111, bf16[768,768]{1,0:T(8,128)(2,1)S(1)} %copy-done.28, bf16[768,1536]{1,0:T(8,128)(2,1)} %get-tuple-element.106.proj_ref, bf16[768,2048]{1,0:T(8,128)(2,1)} %get-tuple-element.91.down_ref, ...), custom_call_target="tpu_custom_call" | custom-call | flops 7200000000 | bytes 24379392 | tf_op jit(solution)/shard_map/pallas_call | solution.py:439
  211.2 2.0 collective-permute-done.15.y_ref
  213.3 11.0 %collective-permute-done.13.up_ref = bf16[448,1536]{1,0:T(8,128)(2,1)S(1)} collective-permute-done((bf16[448,1536]{1,0:T(8,128)(2,1)S(1)}, bf16[448,1536]{1,0:T(8,128)(2,1)S(1)}, u32[]{:S(2)}, u32[]{:S(2)}) %collective-permute-start.13) | collective-permute-done | bytes 1376288 | tf_op jit(solution)/shard_map/ppermute | solution.py:25
  225.4 5.7 %shard_map.186 = (bf16[384,1536]{1,0:T(8,128)(2,1)}, bf16[384,1536]{1,0:T(8,128)(2,1)}, bf16[384,1536]{1,0:T(8,128)(2,1)}) custom-call(bf16[512,1536]{1,0:T(8,128)(2,1)} %copy-done.3, bf16[512,1536]{1,0:T(8,128)(2,1)} %copy-done.4, bf16[512,1536]{1,0:T(8,128)(2,1)} %copy-done, bf16[8,128,1536]{2,1,0:T(8,128)(2,1)} %get-tuple-element.93.parts_ref, ...), custom_call_target="tpu_custom_call" | custom-call | bytes 14942208 | tf_op jit(solution)/shard_map/pallas_call | solution.py:439
  231.1 3.6 collective-permute-start.17
  235.6 4.5 %all-to-all-start.3 = ((bf16[8,96,2176]{2,1,0:T(8,128)(2,1)}), bf16[8,96,2176]{2,1,0:T(8,128)(2,1)}, u32[]{:S(2)}, u32[]{:S(2)}) async-start(bf16[8,96,2176]{2,1,0:T(8,128)(2,1)} %bitcast.120), calls=%async_computation.3 | async-start | bytes 6684672 | tf_op jit(solution)/shard_map/all_to_all | solution.py:60
  240.1 18.1 %collective-permute-done.16.up_ref = bf16[384,1536]{1,0:T(8,128)(2,1)S(1)} collective-permute-done((bf16[384,1536]{1,0:T(8,128)(2,1)}, bf16[384,1536]{1,0:T(8,128)(2,1)S(1)}, u32[]{:S(2)}, u32[]{:S(2)}) %collective-permute-start.16) | collective-permute-done | bytes 1179680 | tf_op jit(solution)/shard_map/ppermute | solution.py:25
  258.3 2.0 collective-permute-done.18.y_ref
  262.5 6.5 %shard_map.187 = bf16[384,1536]{1,0:T(8,128)(2,1)S(1)} custom-call(bf16[512,1536]{1,0:T(8,128)(2,1)} %copy-done, bf16[8,128,1536]{2,1,0:T(8,128)(2,1)} %get-tuple-element.93.parts_ref, bf16[384,1536]{1,0:T(8,128)(2,1)S(1)} %collective-permute-done.16.up_ref, bf16[384,1536]{1,0:T(8,128)(2,1)S(1)} %collective-permute-done.17.down_ref, ...), custom_call_target="tpu_custom_call" | custom-call | bytes 16515072 | tf_op jit(solution)/shard_map/pallas_call | solution.py:439
  269.1 3.2 collective-permute-start.20
  273.3 1.3 fusion.6
  275.2 1.8 multiply_subtract_fusion
  277.4 2.0 copy-done.31
  281.2 5.4 %fusion.8 = (f32[1,256,1536]{2,1,0:T(8,128)}, f32[1,256,1536]{2,1,0:T(8,128)}, f32[1,256,1536]{2,1,0:T(8,128)}) fusion(f32[1,256,1536]{2,1,0:T(8,128)S(1)} %copy-done.33, bf16[384,1536]{1,0:T(8,128)(2,1)} %collective-permute-done.18.y_ref, bf16[384,1536]{1,0:T(8,128)(2,1)S(1)} %collective-permute-done.17.down_ref, ...), kind=kLoop, calls=%fused_computation.38 | loop fusion | flops 8650752 | bytes 12582912 | tf_op jit(solution)/shard_map/broadcast_in_dim | solution.py:632
  286.6 8.0 %collective-permute-done.19 = bf16[384,1536]{1,0:T(8,128)(2,1)S(1)} collective-permute-done((bf16[384,1536]{1,0:T(8,128)(2,1)S(1)}, bf16[384,1536]{1,0:T(8,128)(2,1)S(1)}, u32[]{:S(2)}, u32[]{:S(2)}) %collective-permute-start.19) | collective-permute-done | bytes 1179680 | tf_op jit(solution)/shard_map/ppermute | solution.py:25
  296.6 1.6 fusion.27
  298.4 4.4 %shard_map.188 = (f32[256,2176]{1,0:T(8,128)S(1)}, bf16[256,2176]{1,0:T(8,128)(2,1)S(1)}) custom-call(f32[8,256]{1,0:T(8,128)S(1)} %get-tuple-element.69.aux_ref.near_aux_ref, f32[8,256]{1,0:T(8,128)S(1)} %collective-permute-done.3.aux_ref.far_aux_ref, bf16[768,2176]{1,0:T(8,128)(2,1)} %bitcast.27.rows_ref), custom_call_target="tpu_custom_call" | custom-call | flops 1700000000 | bytes 6701056 | tf_op jit(solution)/shard_map/pallas_call | solution.py:439
  302.8 2.1 collective-permute-start.22
  306.1 1.7 pad_maximum_fusion.2
  307.9 3.2 collective-permute-start.24
  312.0 2.3 collective-permute-start.25
  318.2 2.1 bitcast_dynamic-update-slice_fusion.2
  320.3 11.7 %collective-permute-done.22.far_ref = bf16[256,2176]{1,0:T(8,128)(2,1)S(1)} collective-permute-done((bf16[256,2176]{1,0:T(8,128)(2,1)S(1)}, bf16[256,2176]{1,0:T(8,128)(2,1)S(1)}, u32[]{:S(2)}, u32[]{:S(2)}) %collective-permute-start.22) | collective-permute-done | bytes 1114144 | tf_op jit(solution)/shard_map/ppermute | solution.py:56
  331.9 1.7 shard_map.189
  334.3 9.7 %collective-permute-done.25 = bf16[256,1536]{1,0:T(8,128)(2,1)} collective-permute-done((bf16[256,1536]{1,0:T(8,128)(2,1)}, bf16[256,1536]{1,0:T(8,128)(2,1)}, u32[]{:S(2)}, u32[]{:S(2)}) %collective-permute-start.25) | collective-permute-done | bytes 786464 | tf_op jit(solution)/shard_map/ppermute | solution.py:33
  351.0 1.7 collective-permute-start.27
  354.1 2.1 bitcast_dynamic-update-slice_fusion.1
  356.3 2.1 bitcast_dynamic-update-slice_fusion
  358.3 2.6 collective-permute-done.28
  (177 shorter events, 43.9 us)
Async XLA Ops:
  8.1 4.6 %copy-start.29 = (f32[1,256,1536]{2,1,0:T(8,128)S(1)}, f32[1,256,1536]{2,1,0:T(8,128)}, u32[]{:S(2)}) copy-start(f32[1,256,1536]{2,1,0:T(8,128)} %param.14) | copy-start | bytes 4718596
  8.1 66.5 %all-to-all-start = ((bf16[8,48,4224]{2,1,0:T(8,128)(2,1)}), bf16[8,48,4224]{2,1,0:T(8,128)(2,1)}, u32[]{:S(2)}, u32[]{:S(2)}) async-start(bf16[8,48,4224]{2,1,0:T(8,128)(2,1)} %bitcast.13), calls=%async_computation | async-start | bytes 6488064 | tf_op jit(solution)/shard_map/all_to_all | solution.py:60
  13.9 32.4 %copy-start.17 = (bf16[256,2048]{1,0:T(8,128)(2,1)S(1)}, bf16[256,2048]{1,0:T(8,128)(2,1)}, u32[]{:S(2)}) copy-start(bf16[256,2048]{1,0:T(8,128)(2,1)} %tok_ref.1) | copy-start | bytes 3145732
  14.0 32.2 %collective-permute-start = (bf16[384,1536]{1,0:T(8,128)(2,1)S(1)}, bf16[384,1536]{1,0:T(8,128)(2,1)S(1)}, u32[]{:S(2)}, u32[]{:S(2)}) collective-permute-start(bf16[384,1536]{1,0:T(8,128)(2,1)S(1)} %maximum_maximum_fusion.refs_0_), channel_id=1, source_target_pairs={{0,32},{16,48},{32,64},{48,80},{64,96},{80,112},{96,0},{112,16},{1... | collective-permute-start | bytes 3538952 | tf_op jit(solution)/shard_map/ppermute | solution.py:25
  16.0 30.2 %collective-permute-start.1 = (bf16[384,1536]{1,0:T(8,128)(2,1)S(1)}, bf16[384,1536]{1,0:T(8,128)(2,1)S(1)}, u32[]{:S(2)}, u32[]{:S(2)}) collective-permute-start(bf16[384,1536]{1,0:T(8,128)(2,1)S(1)} %maximum_maximum_fusion.refs_0_), channel_id=1, source_target_pairs={{0,96},{16,112},{32,0},{48,16},{64,32},{80,48},{96,64},{112,80},{1... | collective-permute-start | bytes 3538952 | tf_op jit(solution)/shard_map/ppermute | solution.py:29
  18.2 28.0 %collective-permute-start.2 = (bf16[384,1536]{1,0:T(8,128)(2,1)S(1)}, bf16[384,1536]{1,0:T(8,128)(2,1)S(1)}, u32[]{:S(2)}, u32[]{:S(2)}) collective-permute-start(bf16[384,1536]{1,0:T(8,128)(2,1)S(1)} %maximum_maximum_fusion.refs_0_), channel_id=1, source_target_pairs={{0,16},{16,0},{32,48},{48,32},{64,80},{80,64},{96,112},{112,96},{1... | collective-permute-start | bytes 3538952 | tf_op jit(solution)/shard_map/ppermute | solution.py:33
  20.5 25.7 %collective-permute-start.3 = (f32[8,256]{1,0:T(8,128)S(1)}, f32[8,256]{1,0:T(8,128)S(1)}, u32[]{:S(2)}, u32[]{:S(2)}) collective-permute-start(f32[8,256]{1,0:T(8,128)S(1)} %get-tuple-element.70), channel_id=1, source_target_pairs={{0,2},{1,3},{2,0},{3,1},{4,6},{5,7},{6,4},{7,5},{8,10},{9,11},{10,... | collective-permute-start | bytes 24584 | tf_op jit(solution)/shard_map/ppermute | solution.py:56
  46.2 3.1 copy-start.20
  46.2 3.1 copy-start.43
  46.3 5.1 %copy-start.13 = (bf16[384,1536]{1,0:T(8,128)(2,1)}, bf16[384,1536]{1,0:T(8,128)(2,1)S(1)}, u32[]{:S(2)}) copy-start(bf16[384,1536]{1,0:T(8,128)(2,1)S(1)} %collective-permute-done.2.refs_1_) | copy-start | bytes 3538948
  46.3 26.0 %collective-permute-start.4 = (bf16[256,2048]{1,0:T(8,128)(2,1)S(1)}, bf16[256,2048]{1,0:T(8,128)(2,1)S(1)}, u32[]{:S(2)}, u32[]{:S(2)}) collective-permute-start(bf16[256,2048]{1,0:T(8,128)(2,1)S(1)} %copy-done.17), channel_id=1, source_target_pairs={{0,2},{1,3},{2,0},{3,1},{4,6},{5,7},{6,4},{7,5},{8,10},{9,11},{10,... | collective-permute-start | bytes 3145736 | tf_op jit(solution)/shard_map/ppermute | solution.py:56
  51.4 41.1 %collective-permute-start.5 = (bf16[576,1536]{1,0:T(8,128)(2,1)}, bf16[576,1536]{1,0:T(8,128)(2,1)}, u32[]{:S(2)}, u32[]{:S(2)}) collective-permute-start(bf16[576,1536]{1,0:T(8,128)(2,1)} %get-tuple-element.173), channel_id=1, source_target_pairs={{0,32},{16,48},{32,64},{48,80},{64,96},{80,112},{96,0},{112,16},{1... | collective-permute-start | bytes 5308424 | tf_op jit(solution)/shard_map/ppermute | solution.py:25
  51.4 41.1 %collective-permute-start.6 = (bf16[576,1536]{1,0:T(8,128)(2,1)}, bf16[576,1536]{1,0:T(8,128)(2,1)}, u32[]{:S(2)}, u32[]{:S(2)}) collective-permute-start(bf16[576,1536]{1,0:T(8,128)(2,1)} %get-tuple-element.172), channel_id=1, source_target_pairs={{0,96},{16,112},{32,0},{48,16},{64,32},{80,48},{96,64},{112,80},{1... | collective-permute-start | bytes 5308424 | tf_op jit(solution)/shard_map/ppermute | solution.py:29
  74.5 4.4 %copy-start.19 = (bf16[256,2048]{1,0:T(8,128)(2,1)S(1)}, bf16[256,2048]{1,0:T(8,128)(2,1)}, u32[]{:S(2)}) copy-start(bf16[256,2048]{1,0:T(8,128)(2,1)} %grad_ref.1) | copy-start | bytes 3145732
  74.5 39.3 %all-to-all-start.1 = ((bf16[8,48,2048]{2,1,0:T(8,128)(2,1)}), bf16[8,48,2048]{2,1,0:T(8,128)(2,1)S(1)}, u32[]{:S(2)}, u32[]{:S(2)}) async-start(bf16[8,48,2048]{2,1,0:T(8,128)(2,1)} %bitcast.15), calls=%async_computation.1 | async-start | bytes 3145728 | tf_op jit(solution)/shard_map/all_to_all | solution.py:60
  78.9 27.1 %collective-permute-start.7 = (bf16[256,2048]{1,0:T(8,128)(2,1)S(1)}, bf16[256,2048]{1,0:T(8,128)(2,1)S(1)}, u32[]{:S(2)}, u32[]{:S(2)}) collective-permute-start(bf16[256,2048]{1,0:T(8,128)(2,1)S(1)} %copy-done.19), channel_id=1, source_target_pairs={{0,2},{1,3},{2,0},{3,1},{4,6},{5,7},{6,4},{7,5},{8,10},{9,11},{10,... | collective-permute-start | bytes 3145736 | tf_op jit(solution)/shard_map/ppermute | solution.py:56
  115.0 39.0 %all-to-all-start.2 = ((bf16[8,48,2176]{2,1,0:T(8,128)(2,1)}), bf16[8,48,2176]{2,1,0:T(8,128)(2,1)S(1)}, u32[]{:S(2)}, u32[]{:S(2)}) async-start(bf16[8,48,2176]{2,1,0:T(8,128)(2,1)} %bitcast.17), calls=%async_computation.2 | async-start | bytes 3342336 | tf_op jit(solution)/shard_map/all_to_all | solution.py:60
  119.4 18.8 %copy-start.11 = (bf16[384,1536]{1,0:T(8,128)(2,1)S(1)}, bf16[384,1536]{1,0:T(8,128)(2,1)}, u32[]{:S(2)}) copy-start(bf16[384,1536]{1,0:T(8,128)(2,1)} %copy-done.10) | copy-start | bytes 3538948
  119.4 18.8 %copy-start.14 = (bf16[384,1536]{1,0:T(8,128)(2,1)S(1)}, bf16[384,1536]{1,0:T(8,128)(2,1)}, u32[]{:S(2)}) copy-start(bf16[384,1536]{1,0:T(8,128)(2,1)} %copy-done.13) | copy-start | bytes 3538948
  120.7 17.0 %collective-permute-start.8 = (bf16[192,1536]{1,0:T(8,128)(2,1)S(1)}, bf16[192,1536]{1,0:T(8,128)(2,1)S(1)}, u32[]{:S(2)}, u32[]{:S(2)}) collective-permute-start(bf16[192,1536]{1,0:T(8,128)(2,1)S(1)} %pad_maximum_fusion.7), channel_id=1, source_target_pairs={{0,32},{16,48},{32,64},{48,80},{64,96},{80,112},{96,0},{112,16},{1... | collective-permute-start | bytes 1769480 | tf_op jit(solution)/shard_map/ppermute | solution.py:25
  121.8 16.4 %collective-permute-start.9 = (bf16[192,1536]{1,0:T(8,128)(2,1)S(1)}, bf16[192,1536]{1,0:T(8,128)(2,1)S(1)}, u32[]{:S(2)}, u32[]{:S(2)}) collective-permute-start(bf16[192,1536]{1,0:T(8,128)(2,1)S(1)} %pad_maximum_fusion.8), channel_id=1, source_target_pairs={{0,96},{16,112},{32,0},{48,16},{64,32},{80,48},{96,64},{112,80},{1... | collective-permute-start | bytes 1769480 | tf_op jit(solution)/shard_map/ppermute | solution.py:29
  138.2 1.3 copy-start.21
  154.0 16.6 %copy-start.7 = (bf16[8,48,2176]{2,1,0:T(8,128)(2,1)}, bf16[8,48,2176]{2,1,0:T(8,128)(2,1)S(1)}, u32[]{:S(2)}) copy-start(bf16[8,48,2176]{2,1,0:T(8,128)(2,1)S(1)} %all-to-all-done.2) | copy-start | bytes 5013508
  154.0 2.0 copy-start.9
  170.6 18.2 %collective-permute-start.10 = (bf16[128,1536]{1,0:T(8,128)(2,1)S(1)}, bf16[128,1536]{1,0:T(8,128)(2,1)S(1)}, u32[]{:S(2)}, u32[]{:S(2)}) collective-permute-start(bf16[128,1536]{1,0:T(8,128)(2,1)S(1)} %get-tuple-element.148), channel_id=1, source_target_pairs={{0,32},{16,48},{32,64},{48,80},{64,96},{80,112},{96,0},{112,16},{1... | collective-permute-start | bytes 1179656 | tf_op jit(solution)/shard_map/ppermute | solution.py:25
  171.2 17.6 %collective-permute-start.11 = (bf16[128,1536]{1,0:T(8,128)(2,1)S(1)}, bf16[128,1536]{1,0:T(8,128)(2,1)S(1)}, u32[]{:S(2)}, u32[]{:S(2)}) collective-permute-start(bf16[128,1536]{1,0:T(8,128)(2,1)S(1)} %get-tuple-element.147), channel_id=1, source_target_pairs={{0,96},{16,112},{32,0},{48,16},{64,32},{80,48},{96,64},{112,80},{1... | collective-permute-start | bytes 1179656 | tf_op jit(solution)/shard_map/ppermute | solution.py:29
  175.7 13.0 %collective-permute-start.12 = (bf16[128,1536]{1,0:T(8,128)(2,1)S(1)}, bf16[128,1536]{1,0:T(8,128)(2,1)S(1)}, u32[]{:S(2)}, u32[]{:S(2)}) collective-permute-start(bf16[128,1536]{1,0:T(8,128)(2,1)S(1)} %get-tuple-element.146), channel_id=1, source_target_pairs={{0,16},{16,0},{32,48},{48,32},{64,80},{80,64},{96,112},{112,96},{1... | collective-permute-start | bytes 1179656 | tf_op jit(solution)/shard_map/ppermute | solution.py:33
  188.8 7.7 %copy-start.15 = (bf16[384,1536]{1,0:T(8,128)(2,1)S(1)}, bf16[384,1536]{1,0:T(8,128)(2,1)}, u32[]{:S(2)}) copy-start(bf16[384,1536]{1,0:T(8,128)(2,1)} %copy-done.13) | copy-start | bytes 3538948
  188.8 7.7 %copy-start.22 = (bf16[384,1536]{1,0:T(8,128)(2,1)S(1)}, bf16[384,1536]{1,0:T(8,128)(2,1)}, u32[]{:S(2)}) copy-start(bf16[384,1536]{1,0:T(8,128)(2,1)} %copy-done.20) | copy-start | bytes 3538948
  188.8 7.7 %copy-start.25 = (bf16[192,1536]{1,0:T(8,128)(2,1)S(1)}, bf16[192,1536]{1,0:T(8,128)(2,1)}, u32[]{:S(2)}) copy-start(bf16[192,1536]{1,0:T(8,128)(2,1)} %copy-done.24) | copy-start | bytes 1769476
  188.8 7.7 %copy-start.28 = (bf16[768,768]{1,0:T(8,128)(2,1)S(1)}, bf16[768,768]{1,0:T(8,128)(2,1)}, u32[]{:S(2)}) copy-start(bf16[768,768]{1,0:T(8,128)(2,1)} %copy-done.26) | copy-start | bytes 3538948
  192.1 4.4 %copy-start.12 = (bf16[384,1536]{1,0:T(8,128)(2,1)S(1)}, bf16[384,1536]{1,0:T(8,128)(2,1)}, u32[]{:S(2)}) copy-start(bf16[384,1536]{1,0:T(8,128)(2,1)} %copy-done.10) | copy-start | bytes 3538948
  192.1 32.2 %collective-permute-start.13 = (bf16[448,1536]{1,0:T(8,128)(2,1)S(1)}, bf16[448,1536]{1,0:T(8,128)(2,1)S(1)}, u32[]{:S(2)}, u32[]{:S(2)}) collective-permute-start(bf16[448,1536]{1,0:T(8,128)(2,1)S(1)} %get-tuple-element.104), channel_id=1, source_target_pairs={{0,32},{16,48},{32,64},{48,80},{64,96},{80,112},{96,0},{112,16},{1... | collective-permute-start | bytes 4128776 | tf_op jit(solution)/shard_map/ppermute | solution.py:25
  192.2 32.1 %collective-permute-start.14 = (bf16[448,1536]{1,0:T(8,128)(2,1)S(1)}, bf16[448,1536]{1,0:T(8,128)(2,1)S(1)}, u32[]{:S(2)}, u32[]{:S(2)}) collective-permute-start(bf16[448,1536]{1,0:T(8,128)(2,1)S(1)} %get-tuple-element.105), channel_id=1, source_target_pairs={{0,96},{16,112},{32,0},{48,16},{64,32},{80,48},{96,64},{112,80},{1... | collective-permute-start | bytes 4128776 | tf_op jit(solution)/shard_map/ppermute | solution.py:29
  195.5 17.8 %collective-permute-start.15 = (bf16[256,1536]{1,0:T(8,128)(2,1)S(1)}, bf16[256,1536]{1,0:T(8,128)(2,1)S(1)}, u32[]{:S(2)}, u32[]{:S(2)}) collective-permute-start(bf16[256,1536]{1,0:T(8,128)(2,1)S(1)} %pad_maximum_fusion.4), channel_id=1, source_target_pairs={{0,16},{16,0},{32,48},{48,32},{64,80},{80,64},{96,112},{112,96},{1... | collective-permute-start | bytes 2359304 | tf_op jit(solution)/shard_map/ppermute | solution.py:33
  231.1 27.2 %collective-permute-start.16 = (bf16[384,1536]{1,0:T(8,128)(2,1)}, bf16[384,1536]{1,0:T(8,128)(2,1)S(1)}, u32[]{:S(2)}, u32[]{:S(2)}) collective-permute-start(bf16[384,1536]{1,0:T(8,128)(2,1)} %get-tuple-element.110), channel_id=1, source_target_pairs={{0,32},{16,48},{32,64},{48,80},{64,96},{80,112},{96,0},{112,16},{1... | collective-permute-start | bytes 3538952 | tf_op jit(solution)/shard_map/ppermute | solution.py:25
  231.1 27.2 %collective-permute-start.17 = (bf16[384,1536]{1,0:T(8,128)(2,1)}, bf16[384,1536]{1,0:T(8,128)(2,1)S(1)}, u32[]{:S(2)}, u32[]{:S(2)}) collective-permute-start(bf16[384,1536]{1,0:T(8,128)(2,1)} %get-tuple-element.111), channel_id=1, source_target_pairs={{0,96},{16,112},{32,0},{48,16},{64,32},{80,48},{96,64},{112,80},{1... | collective-permute-start | bytes 3538952 | tf_op jit(solution)/shard_map/ppermute | solution.py:29
  234.7 25.5 %collective-permute-start.18 = (bf16[384,1536]{1,0:T(8,128)(2,1)}, bf16[384,1536]{1,0:T(8,128)(2,1)}, u32[]{:S(2)}, u32[]{:S(2)}) collective-permute-start(bf16[384,1536]{1,0:T(8,128)(2,1)} %get-tuple-element.112), channel_id=1, source_target_pairs={{0,16},{16,0},{32,48},{48,32},{64,80},{80,64},{96,112},{112,96},{1... | collective-permute-start | bytes 3538952 | tf_op jit(solution)/shard_map/ppermute | solution.py:33
  235.6 61.0 %all-to-all-start.3 = ((bf16[8,96,2176]{2,1,0:T(8,128)(2,1)}), bf16[8,96,2176]{2,1,0:T(8,128)(2,1)}, u32[]{:S(2)}, u32[]{:S(2)}) async-start(bf16[8,96,2176]{2,1,0:T(8,128)(2,1)} %bitcast.120), calls=%async_computation.3 | async-start | bytes 6684672 | tf_op jit(solution)/shard_map/all_to_all | solution.py:60
  269.0 25.6 %collective-permute-start.19 = (bf16[384,1536]{1,0:T(8,128)(2,1)S(1)}, bf16[384,1536]{1,0:T(8,128)(2,1)S(1)}, u32[]{:S(2)}, u32[]{:S(2)}) collective-permute-start(bf16[384,1536]{1,0:T(8,128)(2,1)S(1)} %shard_map.187), channel_id=1, source_target_pairs={{0,32},{16,48},{32,64},{48,80},{64,96},{80,112},{96,0},{112,16},{1... | collective-permute-start | bytes 3538952 | tf_op jit(solution)/shard_map/ppermute | solution.py:25
  269.1 25.5 %collective-permute-start.20 = (bf16[384,1536]{1,0:T(8,128)(2,1)S(1)}, bf16[384,1536]{1,0:T(8,128)(2,1)S(1)}, u32[]{:S(2)}, u32[]{:S(2)}) collective-permute-start(bf16[384,1536]{1,0:T(8,128)(2,1)S(1)} %shard_map.187), channel_id=1, source_target_pairs={{0,96},{16,112},{32,0},{48,16},{64,32},{80,48},{96,64},{112,80},{1... | collective-permute-start | bytes 3538952 | tf_op jit(solution)/shard_map/ppermute | solution.py:29
  272.3 24.3 %collective-permute-start.21 = (bf16[384,1536]{1,0:T(8,128)(2,1)S(1)}, bf16[384,1536]{1,0:T(8,128)(2,1)}, u32[]{:S(2)}, u32[]{:S(2)}) collective-permute-start(bf16[384,1536]{1,0:T(8,128)(2,1)S(1)} %shard_map.187), channel_id=1, source_target_pairs={{0,16},{16,0},{32,48},{48,32},{64,80},{80,64},{96,112},{112,96},{1... | collective-permute-start | bytes 3538952 | tf_op jit(solution)/shard_map/ppermute | solution.py:33
  275.1 4.3 %copy-start.31 = (bf16[1,2048,1536]{2,1,0:T(8,128)(2,1)}, bf16[1,2048,1536]{2,1,0:T(8,128)(2,1)S(1)}, u32[]{:S(2)}) copy-start(bf16[1,2048,1536]{2,1,0:T(8,128)(2,1)S(1)} %fusion.2) | copy-start | bytes 18874372
  275.2 4.4 %copy-start.32 = (f32[1,256,1536]{2,1,0:T(8,128)S(1)}, f32[1,256,1536]{2,1,0:T(8,128)}, u32[]{:S(2)}) copy-start(f32[1,256,1536]{2,1,0:T(8,128)} %param.16) | copy-start | bytes 4718596
  275.2 4.3 %copy-start.33 = (f32[1,256,1536]{2,1,0:T(8,128)S(1)}, f32[1,256,1536]{2,1,0:T(8,128)}, u32[]{:S(2)}) copy-start(f32[1,256,1536]{2,1,0:T(8,128)} %param.18) | copy-start | bytes 4718596
  277.0 3.7 %copy-start.1 = (bf16[512,1536]{1,0:T(8,128)(2,1)S(1)}, bf16[512,1536]{1,0:T(8,128)(2,1)}, u32[]{:S(2)}) copy-start(bf16[512,1536]{1,0:T(8,128)(2,1)} %copy-done) | copy-start | bytes 4718596
  277.0 4.1 %copy-start.30 = (f32[1,256,1536]{2,1,0:T(8,128)S(1)}, f32[1,256,1536]{2,1,0:T(8,128)}, u32[]{:S(2)}) copy-start(f32[1,256,1536]{2,1,0:T(8,128)} %param.14) | copy-start | bytes 4718596
  281.2 5.4 %copy-start.39 = (bf16[1,768,2048]{2,1,0:T(8,128)(2,1)}, bf16[1,768,2048]{2,1,0:T(8,128)(2,1)S(1)}, u32[]{:S(2)}) copy-start(bf16[1,768,2048]{2,1,0:T(8,128)(2,1)S(1)} %fusion.9) | copy-start | bytes 9437188
  296.6 1.7 copy-start.37
  302.8 3.3 slice-start
  302.8 3.3 slice-start.2
  302.8 29.1 %collective-permute-start.22 = (bf16[256,2176]{1,0:T(8,128)(2,1)S(1)}, bf16[256,2176]{1,0:T(8,128)(2,1)S(1)}, u32[]{:S(2)}, u32[]{:S(2)}) collective-permute-start(bf16[256,2176]{1,0:T(8,128)(2,1)S(1)} %get-tuple-element.119), channel_id=1, source_target_pairs={{0,2},{1,3},{2,0},{3,1},{4,6},{5,7},{6,4},{7,5},{8,10},{9,11},{10,... | collective-permute-start | bytes 3342344 | tf_op jit(solution)/shard_map/ppermute | solution.py:56
  306.1 10.2 %copy-start.40 = (bf16[1,768,2048]{2,1,0:T(8,128)(2,1)S(1)}, bf16[1,768,2048]{2,1,0:T(8,128)(2,1)}, u32[]{:S(2)}) copy-start(bf16[1,768,2048]{2,1,0:T(8,128)(2,1)} %copy-done.39) | copy-start | bytes 9437188
  307.9 6.5 %copy-start.38 = (bf16[384,1536]{1,0:T(8,128)(2,1)S(1)}, bf16[384,1536]{1,0:T(8,128)(2,1)}, u32[]{:S(2)}) copy-start(bf16[384,1536]{1,0:T(8,128)(2,1)} %copy-done.36) | copy-start | bytes 3538948
  307.9 36.1 %collective-permute-start.23 = (bf16[448,1536]{1,0:T(8,128)(2,1)}, bf16[448,1536]{1,0:T(8,128)(2,1)}, u32[]{:S(2)}, u32[]{:S(2)}) collective-permute-start(bf16[448,1536]{1,0:T(8,128)(2,1)} %get-tuple-element.186), channel_id=1, source_target_pairs={{0,32},{16,48},{32,64},{48,80},{64,96},{80,112},{96,0},{112,16},{1... | collective-permute-start | bytes 4128776 | tf_op jit(solution)/shard_map/ppermute | solution.py:25
  307.9 36.1 %collective-permute-start.24 = (bf16[448,1536]{1,0:T(8,128)(2,1)}, bf16[448,1536]{1,0:T(8,128)(2,1)}, u32[]{:S(2)}, u32[]{:S(2)}) collective-permute-start(bf16[448,1536]{1,0:T(8,128)(2,1)} %get-tuple-element.185), channel_id=1, source_target_pairs={{0,96},{16,112},{32,0},{48,16},{64,32},{80,48},{96,64},{112,80},{1... | collective-permute-start | bytes 4128776 | tf_op jit(solution)/shard_map/ppermute | solution.py:29
  311.1 4.2 %copy-start.35 = (bf16[384,1536]{1,0:T(8,128)(2,1)S(1)}, bf16[384,1536]{1,0:T(8,128)(2,1)}, u32[]{:S(2)}) copy-start(bf16[384,1536]{1,0:T(8,128)(2,1)} %copy-done.34) | copy-start | bytes 3538948
  312.0 4.2 %slice-start.3 = ((bf16[384,1536]{1,0:T(8,128)(2,1)}), bf16[96,1536]{1,0:T(8,128)(2,1)S(1)}, s32[]{:S(2)}) async-start(bf16[384,1536]{1,0:T(8,128)(2,1)} %copy-done.36), calls=%async_computation.7 | async-start | bytes 589824 | tf_op jit(solution)/shard_map/slice | solution.py:207
  312.0 31.9 %collective-permute-start.25 = (bf16[256,1536]{1,0:T(8,128)(2,1)}, bf16[256,1536]{1,0:T(8,128)(2,1)}, u32[]{:S(2)}, u32[]{:S(2)}) collective-permute-start(bf16[256,1536]{1,0:T(8,128)(2,1)} %pad_maximum_fusion.5), channel_id=1, source_target_pairs={{0,16},{16,0},{32,48},{48,32},{64,80},{80,64},{96,112},{112,96},{1... | collective-permute-start | bytes 2359304 | tf_op jit(solution)/shard_map/ppermute | solution.py:33
  315.3 1.8 slice-start.1
  351.0 10.0 %collective-permute-start.27 = (bf16[128,1536]{1,0:T(8,128)(2,1)S(1)}, bf16[128,1536]{1,0:T(8,128)(2,1)S(1)}, u32[]{:S(2)}, u32[]{:S(2)}) collective-permute-start(bf16[128,1536]{1,0:T(8,128)(2,1)S(1)} %get-tuple-element.154), channel_id=1, source_target_pairs={{0,96},{16,112},{32,0},{48,16},{64,32},{80,48},{96,64},{112,80},{1... | collective-permute-start | bytes 1179656 | tf_op jit(solution)/shard_map/ppermute | solution.py:29
  352.8 9.0 %collective-permute-start.26 = (bf16[128,1536]{1,0:T(8,128)(2,1)S(1)}, bf16[128,1536]{1,0:T(8,128)(2,1)S(1)}, u32[]{:S(2)}, u32[]{:S(2)}) collective-permute-start(bf16[128,1536]{1,0:T(8,128)(2,1)S(1)} %get-tuple-element.152), channel_id=1, source_target_pairs={{0,32},{16,48},{32,64},{48,80},{64,96},{80,112},{96,0},{112,16},{1... | collective-permute-start | bytes 1179656 | tf_op jit(solution)/shard_map/ppermute | solution.py:25
  353.1 7.8 %collective-permute-start.28 = (bf16[128,1536]{1,0:T(8,128)(2,1)S(1)}, bf16[128,1536]{1,0:T(8,128)(2,1)S(1)}, u32[]{:S(2)}, u32[]{:S(2)}) collective-permute-start(bf16[128,1536]{1,0:T(8,128)(2,1)S(1)} %pad_maximum_fusion.9), channel_id=1, source_target_pairs={{0,16},{16,0},{32,48},{48,32},{64,80},{80,64},{96,112},{112,96},{1... | collective-permute-start | bytes 1179656 | tf_op jit(solution)/shard_map/ppermute | solution.py:33
  361.0 1.9 copy-start.41
  (17 other events, 18.4 us)

commit v3 on v2

--- a/solution.py
+++ b/solution.py
@@ -1,3 +1,6 @@
+import functools
+import math
+
 import jax
 import jax.numpy as jnp
 from jax import lax
@@ -47,7 +50,6 @@
 TOK = 256
 WIDTH = 2048
 EXTRA = 128
-VMEM_LIMIT = 48 * 1024 * 1024
 YH_SWAP = [(i, i ^ 2) for i in range(16)]
 X_GROUPS = [[x * 4 + h * 2 + c for x in range(4) for c in range(2)] for h in range(2)]
 
@@ -207,32 +209,26 @@
     return jnp.concatenate([packed[:96], jnp.concatenate(tail, axis=0)], axis=1)
 
 
-def gate_up_parts(refs):
+def shard_parts(refs):
     own, other, below, above, up2, down2, up3, down3 = refs
     return [
-        [(own, 0, 256)],
-        [(other, 0, 256)],
-        [(above, 0, 256)],
-        [(down2, 192, 256)],
-        [(up2, 0, 128), (down2, 0, 128)],
-        [(up3, 0, 128), (down3, 0, 128)],
-        [(below, 0, 256)],
-        [(up2, 192, 256)],
+        ((own, 0), (own, 192)),
+        ((other, 0), (other, 192)),
+        ((above, 0), (above, 192)),
+        ((down2, 0), (down2, 192)),
+        ((up3, 0), (down3, 0)),
+        ((up3, 192), (down3, 192)),
+        ((below, 0), (below, 192)),
+        ((up2, 0), (up2, 192)),
     ]
 
 
+def gate_up_parts(refs):
+    return [[(ref, at, 128) for ref, at in halves] for halves in shard_parts(refs)]
+
+
 def down_parts(refs):
-    own, other, below, above, up2, down2, up3, down3 = refs
-    return [
-        [(own, 256, 128)],
-        [(other, 256, 128)],
-        [(above, 256, 128)],
-        [(down2, 448, 128)],
-        [(up2, 128, 64), (down2, 128, 64)],
-        [(up3, 128, 64), (down3, 128, 64)],
-        [(below, 256, 128)],
-        [(up2, 448, 128)],
-    ]
+    return [[(ref, at + 128, 64) for ref, at in halves] for halves in shard_parts(refs)]
 
 
 def read(pieces, columns):
@@ -258,8 +254,8 @@
             sig = jax.nn.sigmoid(gate)
             swish = gate * sig
             act_ref[rows, lo] = (swish * up).astype(BF16)
-            slope_ref[rows, lo] = up * sig * (1.0 + gate * (1.0 - sig))
-            swish_ref[rows, lo] = swish
+            slope_ref[rows, lo] = (up * sig * (1.0 + gate * (1.0 - sig))).astype(BF16)
+            swish_ref[rows, lo] = swish.astype(BF16)
     for i, pieces in enumerate(down_parts(weights)):
         row = pl.multiple_of(column_ref[i] * 96, 32)
         packed = read(pieces, slice(None))
@@ -269,19 +265,15 @@
 
 
 def backward_kernel(
-    column_ref,
     near_ref,
     far_in_ref,
     far_grad_ref,
-    act_ref,
     slope_ref,
     swish_ref,
     down_ref,
     proj_ref,
     far_plane_ref,
-    parts_ref,
     scaled_ref,
-    whole_ref,
 ):
     for rows, grad_ref, at in ((BOTH[0], near_ref, WIDTH), (BOTH[1], far_grad_ref, 0)):
         gate = grad_ref[:, at + WIDTH : at + WIDTH + EXTRA].astype(F32)
@@ -293,11 +285,14 @@
         for f in range(3):
             lo = slice(f * 256, f * 256 + 256)
             grad_act = SCALE_OUT * dot(scaled_ref[rows, :], down_ref[lo, :], NT)
-            proj_ref[rows, lo] = (grad_act * slope_ref[rows, lo]).astype(BF16)
+            proj_ref[rows, lo] = (grad_act * slope_ref[rows, lo].astype(F32)).astype(BF16)
             proj_ref[rows, HIDDEN + f * 256 : HIDDEN + f * 256 + 256] = (
-                grad_act * swish_ref[rows, lo]
+                grad_act * swish_ref[rows, lo].astype(F32)
             ).astype(BF16)
     plane_product(near_ref, far_in_ref, proj_ref, far_plane_ref, 2)
+
+
+def parts_kernel(column_ref, act_ref, scaled_ref, parts_ref, whole_ref):
     for n in range(4):
         part = slice(n * 512, n * 512 + 512)
         for f in range(3):
@@ -324,9 +319,13 @@
             out_ref[half * 256 : half * 256 + 256, part] = (SCALE_IN * total).astype(BF16)
 
 
-def planes_kernel(near_ref, far_ref, proj_ref, above_ref, below_ref, own_ref):
-    for k, out_ref in ((1, above_ref), (3, below_ref), (0, own_ref)):
-        plane_product(near_ref, far_ref, proj_ref, out_ref, k)
+def planes_kernel(near_ref, far_ref, proj_ref, above_ref, below_ref):
+    plane_product(near_ref, far_ref, proj_ref, above_ref, 1)
+    plane_product(near_ref, far_ref, proj_ref, below_ref, 3)
+
+
+def own_plane_kernel(near_ref, far_ref, proj_ref, own_ref):
+    plane_product(near_ref, far_ref, proj_ref, own_ref, 0)
 
 
 def back_kernel(near_ref, far_grad_ref, act_ref, proj_ref, down_ref, *refs):
@@ -359,6 +358,77 @@
     for value in refs_or_values[1:]:
         total = total + value.astype(F32)
     return total
+
+
+def copy_all(pairs, sems):
+    copies = [
+        pltpu.make_async_copy(source, target, sems.at[i]) for i, (source, target) in enumerate(pairs)
+    ]
+    for copy in copies:
+        copy.start()
+    for copy in copies:
+        copy.wait()
+
+
+def pass_on_kernel(below_ref, above_ref, up2_ref, down2_ref, up_ref, down_ref, sems):
+    copy_all(
+        [
+            (below_ref.at[0:192], up_ref.at[0:192]),
+            (above_ref.at[192:384], down_ref.at[0:192]),
+            (up2_ref.at[0:192], up_ref.at[192:384]),
+            (down2_ref.at[192:384], down_ref.at[192:384]),
+        ],
+        sems,
+    )
+
+
+def pass_on(below, above, up2, down2):
+    vmem = pl.BlockSpec(memory_space=pltpu.VMEM)
+    return pl.pallas_call(
+        pass_on_kernel,
+        out_shape=(bf(384, 1536), bf(384, 1536)),
+        in_specs=[pl.BlockSpec(memory_space=pl.ANY)] * 4,
+        out_specs=(vmem, vmem),
+        scratch_shapes=[pltpu.SemaphoreType.DMA((4,))],
+        cost_estimate=pl.CostEstimate(flops=0, bytes_accessed=4_800_000, transcendentals=0),
+        compiler_params=pltpu.CompilerParams(vmem_limit_bytes=6 << 20),
+    )(below, above, up2, down2)
+
+
+def place_kernel(pieces, column_ref, *refs):
+    gu_ref, dn_ref, sems = refs[-3:]
+    pairs = []
+    for block, (first, first_at), (last, last_at) in pieces:
+        row = pl.multiple_of(column_ref[block] * 256, 256)
+        pairs.append((refs[first].at[pl.ds(first_at, 128)], gu_ref.at[pl.ds(row, 128)]))
+        pairs.append((refs[last].at[pl.ds(last_at, 128)], gu_ref.at[pl.ds(row + 128, 128)]))
+        row = pl.multiple_of(column_ref[block] * 96, 32)
+        first_at, last_at = first_at + 128, last_at + 128
+        main = pl.ds(0, 1536)
+        pairs.append((refs[first].at[pl.ds(first_at, 64)], dn_ref.at[pl.ds(row, 64), main]))
+        pairs.append((refs[last].at[pl.ds(last_at, 32)], dn_ref.at[pl.ds(row + 64, 32), main]))
+        for j in range(3):
+            tail = refs[last].at[pl.ds(last_at + 32, 32), pl.ds(512 * j, 512)]
+            pairs.append((tail, dn_ref.at[pl.ds(row + 32 * j, 32), pl.ds(1536, 512)]))
+    copy_all(pairs, sems)
+
+
+def place_shards(columns, shards, pieces, whole=()):
+    anywhere = pl.BlockSpec(memory_space=pl.ANY)
+    vmem = pl.BlockSpec(memory_space=pltpu.VMEM)
+    given = len(shards)
+    return pl.pallas_call(
+        functools.partial(place_kernel, pieces),
+        out_shape=(bf(8 * 256, 1536), bf(8 * 96, WIDTH)),
+        in_specs=[pl.BlockSpec(memory_space=pltpu.SMEM)] + [vmem] * given + [anywhere] * len(whole),
+        out_specs=(anywhere, anywhere),
+        scratch_shapes=[pltpu.SemaphoreType.DMA((7 * len(pieces),))],
+        input_output_aliases={given + 1: 0, given + 2: 1} if whole else {},
+        cost_estimate=pl.CostEstimate(
+            flops=0, bytes_accessed=2_400_000 * len(pieces), transcendentals=0
+        ),
+        compiler_params=pltpu.CompilerParams(vmem_limit_bytes=16 << 20),
+    )(columns, *shards, *whole)
 
 
 def second_kernel(far_ref, above_ref, below_ref, parts_ref, up_ref, down_ref, y_ref, o_up, o_down):
@@ -388,38 +458,43 @@
 
 
 def update_kernel(
-    own_ref, parts_ref, up_ref, down_ref, y_ref, w_gu, w_dn, m_gu, m_dn, s_gu, s_dn, out_ref, sum_ref
+    own_ref, parts_ref, up_ref, down_ref, y_ref, w_gu, m_gu, s_gu, w_dn, m_dn, s_dn, w_tail, m_tail,
+    s_tail, out_ref
 ):
-    grad = add(own_ref[0:256], up_ref[0:256], down_ref[0:256], y_ref[0:256])
-    out_ref[0:256] = adam_update(w_gu[...], m_gu[...], s_gu[...], grad)[0].astype(BF16)
-    sum_ref[...] = add(parts_ref[0], up_ref[256:384], down_ref[256:384], y_ref[256:384])
-    new = adam_update(
-        w_dn[:, :1536], m_dn[:, :1536], s_dn[:, :1536], sum_ref[0:96, :]
-    )[0]
-    out_ref[256:352] = new.astype(BF16)
-    for j in range(3):
-        rows = slice(32 * j, 32 * j + 32)
-        part = slice(512 * j, 512 * j + 512)
-        new = adam_update(
-            w_dn[rows, 1536:], m_dn[rows, 1536:], s_dn[rows, 1536:], sum_ref[96:128, part]
-        )[0]
-        out_ref[352:384, part] = new.astype(BF16)
+    grad = add(own_ref[...], up_ref[0:256], down_ref[0:256], y_ref[0:256])
+    new = adam_update(w_gu[...], m_gu[...], s_gu[...], grad)[0].astype(BF16)
+    out_ref[0:128] = new[:128]
+    out_ref[192:320] = new[128:]
+    grad = add(parts_ref[0], up_ref[256:384], down_ref[256:384], y_ref[256:384])
+    new = adam_update(w_dn[...], m_dn[...], s_dn[...], grad[:96])[0].astype(BF16)
+    out_ref[128:192] = new[:64]
+    out_ref[320:352] = new[64:]
+    new = adam_update(w_tail[...], m_tail[...], s_tail[...], grad[96:])[0].astype(BF16)
+    out_ref[352:384] = new
+
+
+def update_call(own_plane, parts, t_up, t_down, t_y, state):
+    gu = pl.BlockSpec((256, 512), lambda c: (0, c))
+    packed = pl.BlockSpec((384, 512), lambda c: (0, c))
+    part = pl.BlockSpec((1, 128, 512), lambda c: (0, 0, c))
+    dn = pl.BlockSpec((96, 512), lambda c: (0, c))
+    tail = pl.BlockSpec((32, 512), lambda c: (c, 3))
+    w_gu, w_dn, m_gu, m_dn, s_gu, s_dn = state
+    return pl.pallas_call(
+        update_kernel,
+        out_shape=bf(384, 1536),
+        grid=(3,),
+        in_specs=[gu, part, packed, packed, packed] + [gu] * 3 + [dn] * 3 + [tail] * 3,
+        out_specs=packed,
+        cost_estimate=pl.CostEstimate(
+            flops=20_000_000, bytes_accessed=12_000_000, transcendentals=1_000_000
+        ),
+        compiler_params=pltpu.CompilerParams(vmem_limit_bytes=48 << 20),
+    )(own_plane, parts, t_up, t_down, t_y, w_gu, m_gu, s_gu, w_dn, m_dn, s_dn, w_dn, m_dn, s_dn)
 
 
 def tie(*arrays):
     return lax.optimization_barrier(arrays)
-
-
-def place(full, block, shard):
-    return lax.dynamic_update_slice(full, block, (shard * block.shape[0], 0))
-
-
-def assemble(blocks, z, y):
-    rows, columns = blocks[(0, 0)].shape
-    full = jnp.zeros((8 * rows, columns), BF16)
-    for (k, dy), block in blocks.items():
-        full = place(full, block, ((z + k) % 4) * 2 + (y ^ dy))
-    return full
 
 
 def bf(*shape):
@@ -436,6 +511,7 @@
     moved = sum(a.size * a.dtype.itemsize for a in inputs) + sum(
         o.size * o.dtype.itemsize for o in outs
     )
+    held = sum(math.prod(s.shape) * 2 for s in scratch)
     got = pl.pallas_call(
         kernel,
         out_shape=outs,
@@ -443,7 +519,7 @@
         out_specs=(vmem,) * len(outs),
         scratch_shapes=scratch,
         cost_estimate=pl.CostEstimate(flops=flops, bytes_accessed=moved, transcendentals=0),
-        compiler_params=pltpu.CompilerParams(vmem_limit_bytes=VMEM_LIMIT),
+        compiler_params=pltpu.CompilerParams(vmem_limit_bytes=moved + held + (3 << 20)),
     )(*inputs)
     return got if len(outs) > 1 else got[0]
 
@@ -466,32 +542,35 @@
     columns = jnp.stack([((z + k) % 4) * 2 + (y ^ dy) for k, dy in order])
     half = ((lax.axis_index("expert") >> 1) & 1).reshape(1)
 
-    own = jnp.concatenate(
-        [master_gate_up[0].astype(BF16), pack_down(master_down[0].astype(BF16))], axis=0
-    )
+    gu = master_gate_up[0].astype(BF16)
+    dn = pack_down(master_down[0].astype(BF16))
+    own = jnp.concatenate([gu[:128], dn[:64], gu[128:], dn[64:]], axis=0)
+    below, above, other = z_up(own), z_down(own), y_swap(own)
     near_aux, far_aux = call(
         route_kernel,
         (f32(8, TOK), f32(8, TOK)),
         (half, expert_ids.T, gate_values.astype(F32).T),
         scalars=1,
     )
-    near = exchange(
-        call(
-            spread_kernel,
-            (bf(HALF_SLOTS, 2 * WIDTH + EXTRA),),
-            (columns, near_aux, tokens, out_grad),
-            scalars=1,
-        )
-    )
-    below, above, other = z_up(own), z_down(own), y_swap(own)
-    their_aux = yh_swap(far_aux)
-    below, above, other, their_aux, tok_next = tie(below, above, other, their_aux, tokens)
-
-    up2 = z_up(jnp.concatenate([below[:128], below[256:320], other], axis=0))
-    down2 = z_down(jnp.concatenate([above[128:256], above[320:384], other], axis=0))
-    their_tok = yh_swap(tok_next)
-    their_tok, grad_next = tie(their_tok, out_grad)
-    their_grad = yh_swap(grad_next)
+    near = call(
+        spread_kernel,
+        (bf(HALF_SLOTS, 2 * WIDTH + EXTRA),),
+        (columns, near_aux, tokens, out_grad),
+        scalars=1,
+    )
+    below, above, other, far_aux, near, tok_next, grad_next = tie(
+        below, above, other, far_aux, near, tokens, out_grad
+    )
+
+    up2, down2 = z_up(other), z_down(other)
+    their_aux, their_tok = yh_swap(far_aux), yh_swap(tok_next)
+    near = exchange(near)
+    up2, down2, their_aux, their_tok, grad_next = tie(
+        up2, down2, their_aux, their_tok, grad_next
+    )
+
+    up3, down3 = pass_on(below, above, up2, down2)
+    up3, down3, their_grad = z_up(up3), z_down(down3), yh_swap(grad_next)
     send_far = call(
         spread_tokens_kernel,
         (bf(HALF_SLOTS, WIDTH),),
@@ -500,48 +579,50 @@
     )
     send_far, near = tie(send_far, near)
     far_in = exchange(send_far)
-    up2, down2, their_grad = tie(up2, down2, their_grad)
-
-    up3 = z_up(jnp.concatenate([up2[192:320], up2[448:512]], axis=0))
-    down3 = z_down(jnp.concatenate([down2[320:448], down2[512:576]], axis=0))
+    up3, down3, their_grad = tie(up3, down3, their_grad)
     send_far = call(spread_grads_kernel, (bf(HALF_SLOTS, WIDTH + EXTRA),), (their_aux, their_grad))
     send_far, far_in = tie(send_far, far_in)
     far_grad = exchange(send_far)
-    up3, down3, far_in = tie(up3, down3, far_in)
     weights = (own, other, below, above, up2, down2, up3, down3)
 
     act, slope, swish, down = call(
         forward_kernel,
         (
             bf(SLOTS, HIDDEN),
-            f32(SLOTS, HIDDEN),
-            f32(SLOTS, HIDDEN),
+            bf(SLOTS, HIDDEN),
+            bf(SLOTS, HIDDEN),
             bf(HIDDEN, WIDTH),
         ),
         (columns, near, far_in) + weights,
         scalars=1,
         flops=4_800_000_000,
     )
-    proj, far_plane, parts = call(
+    proj, far_plane, scaled = call(
         backward_kernel,
-        (bf(SLOTS, 2 * HIDDEN), bf(512, 1536), bf(8, 128, 1536)),
-        (columns, near, far_in, far_grad, act, slope, swish, down),
-        scalars=1,
-        scratch=(pltpu.VMEM((SLOTS, WIDTH), BF16), pltpu.VMEM((HIDDEN, WIDTH), BF16)),
-        flops=6_000_000_000,
+        (bf(SLOTS, 2 * HIDDEN), bf(512, 1536), bf(SLOTS, WIDTH)),
+        (near, far_in, far_grad, slope, swish, down),
+        flops=3_600_000_000,
     )
 
     t_up = z_up(far_plane[256:384])
     t_down = z_down(far_plane[384:512])
+    parts = call(
+        parts_kernel,
+        (bf(8, 128, 1536),),
+        (columns, act, scaled),
+        scalars=1,
+        scratch=(pltpu.VMEM((HIDDEN, WIDTH), BF16),),
+        flops=2_400_000_000,
+    )
     t_y = y_swap(parts[5])
-    above_plane, below_plane, own_plane = call(
+    above_plane, below_plane = call(
         planes_kernel,
-        (bf(512, 1536),) * 3,
+        (bf(512, 1536),) * 2,
         (near, far_in, proj),
-        flops=3_600_000_000,
-    )
-    t_up, t_down, t_y, above_plane, below_plane, own_plane, late_proj = tie(
-        t_up, t_down, t_y, above_plane, below_plane, own_plane, proj
+        flops=2_400_000_000,
+    )
+    t_up, t_down, t_y, above_plane, below_plane, late_proj = tie(
+        t_up, t_down, t_y, above_plane, below_plane, proj
     )
     s_up, s_down = call(
         second_kernel,
@@ -550,13 +631,16 @@
     )
     s_y = jnp.concatenate([parts[3], parts[7]], axis=0)
     t_up, t_down, t_y = z_up(s_up), z_down(s_down), y_swap(s_y)
+    own_plane = call(
+        own_plane_kernel, (bf(512, 1536),), (near, far_in, late_proj), flops=1_200_000_000
+    )
     back = call(
         back_kernel,
         (bf(SLOTS, WIDTH + EXTRA),),
         (near, far_grad, act, late_proj, down) + weights,
         flops=7_200_000_000,
     )
-    t_up, t_down, t_y, back = tie(t_up, t_down, t_y, back)
+    t_up, t_down, t_y, back, own_plane = tie(t_up, t_down, t_y, back, own_plane)
     s_up, s_down, s_y = call(
         third_kernel,
         (bf(384, 1536),) * 3,
@@ -573,12 +657,7 @@
         second_gate_up[0],
         second_down[0],
     )
-    new_own = call(
-        update_kernel,
-        (bf(384, 1536),),
-        (own_plane, parts, t_up, t_down, t_y) + state,
-        scratch=(pltpu.VMEM((128, 1536), F32),),
-    )
+    new_own = update_call(own_plane, parts, t_up, t_down, t_y, state)
 
     below, above, other = z_up(new_own), z_down(new_own), y_swap(new_own)
     grad_gate_up = add(own_plane[:256], t_up[:256], t_down[:256], t_y[:256])
@@ -589,35 +668,60 @@
     master_dn_next, moment_dn_next, second_dn_next = adam_update(
         state[1], state[3], state[5], grad_down
     )
-    below, above, other, returned = tie(below, above, other, returned)
-    gu = {(0, 0): new_own[:256], (3, 0): below[:256], (1, 0): above[:256], (0, 1): other[:256]}
-    dn = {(0, 0): new_own[256:], (3, 0): below[256:], (1, 0): above[256:], (0, 1): other[256:]}
-    up2 = z_up(jnp.concatenate([below[:128], below[256:320], other[:256]], axis=0))
-    down2 = z_down(jnp.concatenate([above[128:256], above[320:384], other[:256]], axis=0))
-    side2 = y_swap(jnp.concatenate([above[256:], below[256:]], axis=0))
     near_sum, far_sum = call(
         collect_kernel,
         (f32(TOK, WIDTH + EXTRA), bf(TOK, WIDTH + EXTRA)),
         (near_aux, their_aux, returned),
         flops=1_700_000_000,
     )
+    below, above, other, far_sum, *kept = tie(
+        below,
+        above,
+        other,
+        far_sum,
+        master_gu_next,
+        moment_gu_next,
+        second_gu_next,
+        master_dn_next,
+        moment_dn_next,
+        second_dn_next,
+    )
+    (
+        master_gu_next,
+        moment_gu_next,
+        second_gu_next,
+        master_dn_next,
+        moment_dn_next,
+        second_dn_next,
+    ) = kept
+    up2, down2 = z_up(other), z_down(other)
     far_sum = yh_swap(far_sum)
-    up2, down2, side2 = tie(up2, down2, side2)
-    gu[(2, 0)] = jnp.concatenate([up2[:128], down2[:128]], axis=0)
-    dn[(2, 0)] = jnp.concatenate([up2[128:192], down2[128:192]], axis=0)
-    gu[(3, 1)], gu[(1, 1)] = up2[192:], down2[192:]
-    dn[(1, 1)], dn[(3, 1)] = side2[:128], side2[128:]
-    up3, down3, side3 = z_up(up2[192:320]), z_down(down2[320:448]), y_swap(dn[(2, 0)])
-    gu[(2, 1)] = jnp.concatenate([up3, down3], axis=0)
-    dn[(2, 1)] = side3
-    new_gate_up = assemble(gu, z, y)
-    new_down = assemble({at: unpack_down(block) for at, block in dn.items()}, z, y)
-
+
+    pieces = [(i, (n, 0), (n, 192)) for n, i in enumerate((0, 1, 2, 6))]
+    new_gate_up, new_down = place_shards(columns, (new_own, other, above, below), pieces)
+    up2, down2, far_sum, new_gate_up, new_down = tie(up2, down2, far_sum, new_gate_up, new_down)
+    up3, down3 = pass_on(below, above, up2, down2)
+    up3, down3 = z_up(up3), z_down(down3)
+    new_gate_up, new_down = place_shards(
+        columns,
+        (down2, up2),
+        [(3, (0, 0), (0, 192)), (7, (1, 0), (1, 192))],
+        (new_gate_up, new_down),
+    )
     input_grad, scores = call(
         finish_kernel,
         (bf(TOK, WIDTH), bf(TOK, EXTRA)),
         (columns, near_sum, far_sum),
         scalars=1,
+    )
+    up3, down3, new_gate_up, new_down, input_grad = tie(
+        up3, down3, new_gate_up, new_down, input_grad
+    )
+    new_gate_up, new_down = place_shards(
+        columns,
+        (up3, down3),
+        [(4, (0, 0), (1, 0)), (5, (0, 192), (1, 192))],
+        (new_gate_up, new_down),
     )
     gate_grad = scores[:, :2]
     return (

time: 370 us -> 337 us (0.911)
  the two profiles are of different devices: /device:TPU:16 before, /device:TPU:4 now
where the time goes in v3:
time: 337 us; the launch traced here: 330 us
  waiting for transfers between devices  138 us (41%)
  starting transfers between devices  71.2 us (21%)
  Pallas kernels  65.9 us (20%)
  local copies, waits for them, and re-layouts  43.5 us (13%)
  other arithmetic  10.2 us (3%)
    ppermute x9, waiting for transfers between devices, z_up(): return lax.ppermute(a, 'dp', Z_UP)  65.5 us
    ppermute x4, waiting for transfers between devices, yh_swap(): return lax.ppermute(a, 'expert', YH_SWAP)  61.4 us
    pallas_call x14, Pallas kernels, call(): pl.pallas_call(kernel, out_shape=outs, in_specs=[smem] * scalars + [vmem]...  48.3 us
    unnamed x127, local copies, waits for them, and re-layouts  43.1 us
    ppermute x9, starting transfers between devices, z_down(): return lax.ppermute(a, 'dp', Z_DOWN)  27.6 us
    all_to_all x4, starting transfers between devices, exchange(): lax.all_to_all(rows.reshape(8, rows.shape[0] // 8, rows.shape[1]), 'exper...  22.5 us
    ppermute x4, starting transfers between devices, yh_swap(): return lax.ppermute(a, 'expert', YH_SWAP)  9.89 us
    pallas_call x3, Pallas kernels, place_shards(): pl.pallas_call(functools.partial(place_kernel, pieces), out_shape=(bf(8 *...  9.21 us
  transfers between devices with their start and end apart: 31, of which 13 were waited for; matrix products, arithmetic and copies ran while one was open for 3% of the time, Pallas kernels for 16%

profile of v3, /device:TPU:4, one launch (start us, length us, event | category | flops | bytes accessed | tf_op | source)
XLA Modules:
  0.0 329.9 jit_solution(8167528454215785039)
XLA Ops:
  0.7 1.3 bitcast_convert_fusion
  2.6 2.0 collective-permute-start
  4.5 2.2 collective-permute-start.1
  6.7 1.6 collective-permute-start.2
  11.6 1.6 shard_map.178
  13.3 1.7 copy-done.5
  14.9 17.7 %collective-permute-done.below_ref.refs_2_ = bf16[384,1536]{1,0:T(8,128)(2,1)S(1)} collective-permute-done((bf16[384,1536]{1,0:T(8,128)(2,1)S(1)}, bf16[384,1536]{1,0:T(8,128)(2,1)S(1)}, u32[]{:S(2)}, u32[]{:S(2)}) %collective-permute-start) | collective-permute-done | bytes 1179680 | tf_op jit(solution)/shard_map/ppermute | solution.py:28
  34.7 4.9 %all-to-all-start = ((bf16[8,48,4224]{2,1,0:T(8,128)(2,1)}), bf16[8,48,4224]{2,1,0:T(8,128)(2,1)S(1)}, u32[]{:S(2)}, u32[]{:S(2)}) async-start(bf16[8,48,4224]{2,1,0:T(8,128)(2,1)} %bitcast.63), calls=%async_computation | async-start | bytes 6488064 | tf_op jit(solution)/shard_map/all_to_all | solution.py:62
  39.9 3.0 collective-permute-start.4
  42.9 3.2 collective-permute-start.6
  46.4 23.0 %collective-permute-done.5.aux_ref.far_aux_ref = f32[8,256]{1,0:T(8,128)S(1)} collective-permute-done((f32[8,256]{1,0:T(8,128)S(1)}, f32[8,256]{1,0:T(8,128)S(1)}, u32[]{:S(2)}, u32[]{:S(2)}) %collective-permute-start.5) | collective-permute-done | bytes 8224 | tf_op jit(solution)/shard_map/ppermute | solution.py:58
  73.9 2.1 all-to-all-done
  76.0 7.3 %all-to-all-start.1 = ((bf16[8,48,2048]{2,1,0:T(8,128)(2,1)}), bf16[8,48,2048]{2,1,0:T(8,128)(2,1)}, u32[]{:S(2)}, u32[]{:S(2)}) async-start(bf16[8,48,2048]{2,1,0:T(8,128)(2,1)} %bitcast.71), calls=%async_computation.1 | async-start | bytes 3145728 | tf_op jit(solution)/shard_map/all_to_all | solution.py:62
  83.3 1.3 copy-done.18
  84.6 1.3 copy-done.22
  85.9 1.3 copy-done.26
  87.1 1.3 copy-done.30
  89.2 3.0 collective-permute-start.8
  92.2 3.2 collective-permute-start.9
  95.4 23.0 %collective-permute-done.9.grad_ref = bf16[256,2048]{1,0:T(8,128)(2,1)S(1)} collective-permute-done((bf16[256,2048]{1,0:T(8,128)(2,1)S(1)}, bf16[256,2048]{1,0:T(8,128)(2,1)S(1)}, u32[]{:S(2)}, u32[]{:S(2)}) %collective-permute-start.9) | collective-permute-done | bytes 1048608 | tf_op jit(solution)/shard_map/ppermute | solution.py:58
  122.3 5.3 %all-to-all-start.2 = ((bf16[8,48,2176]{2,1,0:T(8,128)(2,1)}), bf16[8,48,2176]{2,1,0:T(8,128)(2,1)}, u32[]{:S(2)}, u32[]{:S(2)}) async-start(bf16[8,48,2176]{2,1,0:T(8,128)(2,1)} %bitcast.70), calls=%async_computation.2 | async-start | bytes 3342336 | tf_op jit(solution)/shard_map/all_to_all | solution.py:62
  128.9 1.3 copy-done.19
  130.2 1.3 copy-done.23
  132.7 1.3 copy-done.31
  136.5 7.7 %shard_map.182 = (bf16[768,768]{1,0:T(8,128)(2,1)S(1)}, bf16[768,768]{1,0:T(8,128)(2,1)S(1)}, bf16[768,768]{1,0:T(8,128)(2,1)S(1)}, bf16[768,2048]{1,0:T(8,128)(2,1)S(1)}) custom-call(s32[8]{0:T(128)S(1)} %stack.35.column_ref, bf16[384,4224]{1,0:T(8,128)(2,1)S(1)} %bitcast.58, bf16[384,2048]{1,0:T(8,128)(2,1)} %bitcast.16.far_ref.far_in_ref, ...), custom_call_target="tpu_custom_call" | custom-call | flops 4800000000 | bytes 20938784 | tf_op jit(solution)/shard_map/pallas_call | solution.py:515
  144.3 1.7 copy-done.48
  149.0 1.9 copy-done.49
  153.5 6.6 %shard_map.183 = (bf16[768,1536]{1,0:T(8,128)(2,1)S(1)}, bf16[512,1536]{1,0:T(8,128)(2,1)S(1)}, bf16[768,2048]{1,0:T(8,128)(2,1)S(1)}) custom-call(bf16[384,4224]{1,0:T(8,128)(2,1)S(1)} %bitcast.59, bf16[384,2048]{1,0:T(8,128)(2,1)} %bitcast.16.far_ref.far_in_ref, bf16[384,2176]{1,0:T(8,128)(2,1)} %bitcast.18.far_grad_ref, bf16[768,768]{1,0:T(8,128)(2,1)S(1)} %copy-done.52, ...), custom_call_target="tpu_custom_call" | custom-call | flops 3600000000 | bytes 19070976 | tf_op jit(solution)/shard_map/pallas_call | solution.py:515
  160.2 3.2 collective-permute-start.11
  163.5 3.4 %shard_map.184.parts_ref = bf16[8,128,1536]{2,1,0:T(8,128)(2,1)S(1)} custom-call(s32[8]{0:T(128)S(1)} %stack.35.column_ref, bf16[768,768]{1,0:T(8,128)(2,1)S(1)} %copy-done.56, bf16[768,2048]{1,0:T(8,128)(2,1)S(1)} %get-tuple-element.121.scaled_ref), custom_call_target="tpu_custom_call" | custom-call | flops 2400000000 | bytes 7471136 | tf_op jit(solution)/shard_map/pallas_call | solution.py:515
  167.0 1.8 collective-permute-start.12
  168.8 4.8 %shard_map.185 = (bf16[512,1536]{1,0:T(8,128)(2,1)S(1)}, bf16[512,1536]{1,0:T(8,128)(2,1)S(1)}) custom-call(bf16[384,4224]{1,0:T(8,128)(2,1)S(1)} %bitcast.60, bf16[384,2048]{1,0:T(8,128)(2,1)} %bitcast.16.far_ref.far_in_ref, bf16[768,1536]{1,0:T(8,128)(2,1)S(1)} %get-tuple-element.132.proj_ref), custom_call_target="tpu_custom_call" | custom-call | flops 2400000000 | bytes 10321920 | tf_op jit(solution)/shard_map/pallas_call | solution.py:515
  173.7 4.2 %collective-permute-done.12.y_ref = bf16[128,1536]{1,0:T(8,128)(2,1)S(1)} collective-permute-done((bf16[128,1536]{1,0:T(8,128)(2,1)S(1)}, bf16[128,1536]{1,0:T(8,128)(2,1)S(1)}, u32[]{:S(2)}, u32[]{:S(2)}) %collective-permute-start.12) | collective-permute-done | bytes 393248 | tf_op jit(solution)/shard_map/ppermute | solution.py:36
  178.2 3.2 collective-permute-start.14
  182.4 1.6 collective-permute-start.15
  184.1 3.9 %shard_map.188.own_ref = bf16[512,1536]{1,0:T(8,128)(2,1)S(1)} custom-call(bf16[384,4224]{1,0:T(8,128)(2,1)S(1)} %bitcast.61, bf16[384,2048]{1,0:T(8,128)(2,1)} %bitcast.16.far_ref.far_in_ref, bf16[768,1536]{1,0:T(8,128)(2,1)S(1)} %get-tuple-element.132.proj_ref), custom_call_target="tpu_custom_call" | custom-call | flops 1200000000 | bytes 8749056 | tf_op jit(solution)/shard_map/pallas_call | solution.py:515
  188.1 9.9 %shard_map.187 = bf16[768,2176]{1,0:T(8,128)(2,1)S(1)} custom-call(bf16[384,4224]{1,0:T(8,128)(2,1)S(1)} %bitcast.62, bf16[384,2176]{1,0:T(8,128)(2,1)} %bitcast.18.far_grad_ref, bf16[768,768]{1,0:T(8,128)(2,1)S(1)} %copy-done.57, bf16[768,1536]{1,0:T(8,128)(2,1)S(1)} %get-tuple-element.132.proj_ref, bf16[768,2048]{1,0:T(8,128)(2,1)S(1)} %copy-done.50, ...), custom_call_target="tpu_custom_call" | custom-call | flops 7200000000 | bytes 24379392 | tf_op jit(solution)/shard_map/pallas_call | solution.py:515
  198.1 2.2 collective-permute-done.15.y_ref
  200.3 9.9 %collective-permute-done.13.up_ref = bf16[448,1536]{1,0:T(8,128)(2,1)S(1)} collective-permute-done((bf16[448,1536]{1,0:T(8,128)(2,1)S(1)}, bf16[448,1536]{1,0:T(8,128)(2,1)S(1)}, u32[]{:S(2)}, u32[]{:S(2)}) %collective-permute-start.13) | collective-permute-done | bytes 1376288 | tf_op jit(solution)/shard_map/ppermute | solution.py:28
  210.2 2.0 shard_map.189
  212.2 3.2 collective-permute-start.17
  215.5 1.8 collective-permute-start.18
  217.2 4.9 %all-to-all-start.3 = ((bf16[8,96,2176]{2,1,0:T(8,128)(2,1)}), bf16[8,96,2176]{2,1,0:T(8,128)(2,1)}, u32[]{:S(2)}, u32[]{:S(2)}) async-start(bf16[8,96,2176]{2,1,0:T(8,128)(2,1)} %bitcast.72), calls=%async_computation.3 | async-start | bytes 6684672 | tf_op jit(solution)/shard_map/all_to_all | solution.py:62
  222.2 17.1 %collective-permute-done.16.up_ref = bf16[384,1536]{1,0:T(8,128)(2,1)S(1)} collective-permute-done((bf16[384,1536]{1,0:T(8,128)(2,1)}, bf16[384,1536]{1,0:T(8,128)(2,1)S(1)}, u32[]{:S(2)}, u32[]{:S(2)}) %collective-permute-start.16) | collective-permute-done | bytes 1179680 | tf_op jit(solution)/shard_map/ppermute | solution.py:28
  242.3 5.1 %shard_map.190.refs_0_ = bf16[384,1536]{1,0:T(8,128)(2,1)S(1)} custom-call(bf16[512,1536]{1,0:T(8,128)(2,1)} %copy-done.1, bf16[8,128,1536]{2,1,0:T(8,128)(2,1)} %copy-done, bf16[384,1536]{1,0:T(8,128)(2,1)S(1)} %copy-done.12, bf16[384,1536]{1,0:T(8,128)(2,1)} %collective-permute-done.17.down_ref, bf16[384,1536]{1,0:T(8,128)(2,1)} %collective-permute-done.18.y_ref, ...), custom_call_target="tpu_custom_call" | custom-call | flops 20000000 | bytes 12000000 | tf_op jit(solution)/shard_map/pallas_call | solution.py:483
  247.5 3.2 collective-permute-start.20
  250.8 1.6 collective-permute-start.21
  252.3 1.4 fusion.6
  253.9 1.8 multiply_subtract_fusion.1
  257.5 4.6 %multiply_subtract_fusion = (f32[256,1536]{1,0:T(8,128)}, f32[256,1536]{1,0:T(8,128)}, f32[256,1536]{1,0:T(8,128)}) fusion(f32[1,256,1536]{2,1,0:T(8,128)S(1)} %copy-done.59, bf16[384,1536]{1,0:T(8,128)(2,1)} %collective-permute-done.18.y_ref, bf16[384,1536]{1,0:T(8,128)(2,1)} %collective-permute-done.17.down_ref, bf16[384,1536]{1,0:T(8,128)(2,1)S(1)} %copy-done.12, ...), kind=kLoop, calls=%fused_computation.4 | loop fusion | flops 8650752 | bytes 12582912 | tf_op jit(solution)/shard_map/sub | solution.py:43
  262.1 4.4 %shard_map.191 = (f32[256,2176]{1,0:T(8,128)S(1)}, bf16[256,2176]{1,0:T(8,128)(2,1)S(1)}) custom-call(f32[8,256]{1,0:T(8,128)S(1)} %copy-done.38, f32[8,256]{1,0:T(8,128)S(1)} %collective-permute-done.5.aux_ref.far_aux_ref, bf16[768,2176]{1,0:T(8,128)(2,1)} %bitcast.27.rows_ref), custom_call_target="tpu_custom_call" | custom-call | flops 1700000000 | bytes 6701056 | tf_op jit(solution)/shard_map/pallas_call | solution.py:515
  266.5 6.5 %collective-permute-done.19.refs_3_.below_ref = bf16[384,1536]{1,0:T(8,128)(2,1)} collective-permute-done((bf16[384,1536]{1,0:T(8,128)(2,1)S(1)}, bf16[384,1536]{1,0:T(8,128)(2,1)}, u32[]{:S(2)}, u32[]{:S(2)}) %collective-permute-start.19) | collective-permute-done | bytes 1179680 | tf_op jit(solution)/shard_map/ppermute | solution.py:28
  273.0 1.5 collective-permute-done.21.refs_1_
  274.5 3.2 collective-permute-start.23
  277.7 3.2 collective-permute-start.24
  280.9 4.4 %shard_map.192 = (bf16[2048,1536]{1,0:T(8,128)(2,1)}, bf16[768,2048]{1,0:T(8,128)(2,1)}) custom-call(s32[8]{0:T(128)S(1)} %stack.35.column_ref, bf16[384,1536]{1,0:T(8,128)(2,1)S(1)} %shard_map.190.refs_0_, bf16[384,1536]{1,0:T(8,128)(2,1)} %collective-permute-done.21.refs_1_, bf16[384,1536]{1,0:T(8,128)(2,1)} %collective-permute-done.20.refs_2_.above_ref, ...), custom_call_target="tpu_custom_call" | custom-call | bytes 9600000 | tf_op jit(solution)/shard_map/pallas_call | solution.py:420
  285.3 15.4 %collective-permute-done.24.far_ref = bf16[256,2176]{1,0:T(8,128)(2,1)S(1)} collective-permute-done((bf16[256,2176]{1,0:T(8,128)(2,1)S(1)}, bf16[256,2176]{1,0:T(8,128)(2,1)S(1)}, u32[]{:S(2)}, u32[]{:S(2)}) %collective-permute-start.24) | collective-permute-done | bytes 1114144 | tf_op jit(solution)/shard_map/ppermute | solution.py:58
  300.7 2.7 shard_map.193
  303.5 3.2 collective-permute-start.26
  306.7 1.7 shard_map.195
  309.0 1.5 copy.24
  310.5 2.0 shard_map.194
  312.6 14.3 %collective-permute-done.25.refs_0_ = bf16[384,1536]{1,0:T(8,128)(2,1)S(1)} collective-permute-done((bf16[384,1536]{1,0:T(8,128)(2,1)}, bf16[384,1536]{1,0:T(8,128)(2,1)S(1)}, u32[]{:S(2)}, u32[]{:S(2)}) %collective-permute-start.25) | collective-permute-done | bytes 1179680 | tf_op jit(solution)/shard_map/ppermute | solution.py:28
  326.8 2.8 shard_map.196
  (162 shorter events, 33.7 us)
Async XLA Ops:
  0.6 1.6 copy-start.58
  2.4 5.9 %copy-start.62 = (bf16[256,2]{0,1:T(2,128)(2,1)S(1)}, bf16[256,2]{0,1:T(2,128)(2,1)}, u32[]{:S(2)}) copy-start(bf16[256,2]{0,1:T(2,128)(2,1)} %param.13) | copy-start | bytes 3076
  2.4 5.9 %copy-start.39 = (s32[256,2]{0,1:T(2,128)S(1)}, s32[256,2]{0,1:T(2,128)}, u32[]{:S(2)}) copy-start(s32[256,2]{0,1:T(2,128)} %param.12) | copy-start | bytes 6148
  2.5 10.7 %copy-start.14 = (bf16[384,1536]{1,0:T(8,128)(2,1)}, bf16[384,1536]{1,0:T(8,128)(2,1)S(1)}, u32[]{:S(2)}) copy-start(bf16[384,1536]{1,0:T(8,128)(2,1)S(1)} %fusion.3.refs_0_) | copy-start | bytes 3538948
  2.6 30.1 %collective-permute-start = (bf16[384,1536]{1,0:T(8,128)(2,1)S(1)}, bf16[384,1536]{1,0:T(8,128)(2,1)S(1)}, u32[]{:S(2)}, u32[]{:S(2)}) collective-permute-start(bf16[384,1536]{1,0:T(8,128)(2,1)S(1)} %fusion.3.refs_0_), channel_id=1, source_target_pairs={{0,32},{16,48},{32,64},{48,80},{64,96},{80,112},{96,0},{112,16},{1... | collective-permute-start | bytes 3538952 | tf_op jit(solution)/shard_map/ppermute | solution.py:28
  4.5 29.1 %collective-permute-start.1 = (bf16[384,1536]{1,0:T(8,128)(2,1)S(1)}, bf16[384,1536]{1,0:T(8,128)(2,1)S(1)}, u32[]{:S(2)}, u32[]{:S(2)}) collective-permute-start(bf16[384,1536]{1,0:T(8,128)(2,1)S(1)} %fusion.3.refs_0_), channel_id=1, source_target_pairs={{0,96},{16,112},{32,0},{48,16},{64,32},{80,48},{96,64},{112,80},{1... | collective-permute-start | bytes 3538952 | tf_op jit(solution)/shard_map/ppermute | solution.py:32
  6.7 27.9 %collective-permute-start.2 = (bf16[384,1536]{1,0:T(8,128)(2,1)S(1)}, bf16[384,1536]{1,0:T(8,128)(2,1)}, u32[]{:S(2)}, u32[]{:S(2)}) collective-permute-start(bf16[384,1536]{1,0:T(8,128)(2,1)S(1)} %fusion.3.refs_0_), channel_id=1, source_target_pairs={{0,16},{16,0},{32,48},{48,32},{64,80},{80,64},{96,112},{112,96},{1... | collective-permute-start | bytes 3538952 | tf_op jit(solution)/shard_map/ppermute | solution.py:36
  9.1 4.1 %copy-start.37 = (f32[8,256]{1,0:T(8,128)}, f32[8,256]{1,0:T(8,128)S(1)}, u32[]{:S(2)}) copy-start(f32[8,256]{1,0:T(8,128)S(1)} %get-tuple-element.94.aux_ref.near_aux_ref) | copy-start | bytes 24580
  13.2 1.7 copy-start.5
  34.7 11.4 %copy-start.47 = (f32[8,256]{1,0:T(8,128)S(1)}, f32[8,256]{1,0:T(8,128)}, u32[]{:S(2)}) copy-start(f32[8,256]{1,0:T(8,128)} %copy-done.46) | copy-start | bytes 24580
  34.7 41.3 %all-to-all-start = ((bf16[8,48,4224]{2,1,0:T(8,128)(2,1)}), bf16[8,48,4224]{2,1,0:T(8,128)(2,1)S(1)}, u32[]{:S(2)}, u32[]{:S(2)}) async-start(bf16[8,48,4224]{2,1,0:T(8,128)(2,1)} %bitcast.63), calls=%async_computation | async-start | bytes 6488064 | tf_op jit(solution)/shard_map/all_to_all | solution.py:62
  39.6 29.8 %collective-permute-start.3 = (bf16[384,1536]{1,0:T(8,128)(2,1)}, bf16[384,1536]{1,0:T(8,128)(2,1)S(1)}, u32[]{:S(2)}, u32[]{:S(2)}) collective-permute-start(bf16[384,1536]{1,0:T(8,128)(2,1)} %collective-permute-done.2.refs_1_), channel_id=1, source_target_pairs={{0,32},{16,48},{32,64},{48,80},{64,96},{80,112},{96,0},{112,16},{1... | collective-permute-start | bytes 3538952 | tf_op jit(solution)/shard_map/ppermute | solution.py:28
  39.9 30.6 %collective-permute-start.4 = (bf16[384,1536]{1,0:T(8,128)(2,1)}, bf16[384,1536]{1,0:T(8,128)(2,1)S(1)}, u32[]{:S(2)}, u32[]{:S(2)}) collective-permute-start(bf16[384,1536]{1,0:T(8,128)(2,1)} %collective-permute-done.2.refs_1_), channel_id=1, source_target_pairs={{0,96},{16,112},{32,0},{48,16},{64,32},{80,48},{96,64},{112,80},{1... | collective-permute-start | bytes 3538952 | tf_op jit(solution)/shard_map/ppermute | solution.py:32
  42.9 26.5 %collective-permute-start.6 = (bf16[256,2048]{1,0:T(8,128)(2,1)}, bf16[256,2048]{1,0:T(8,128)(2,1)S(1)}, u32[]{:S(2)}, u32[]{:S(2)}) collective-permute-start(bf16[256,2048]{1,0:T(8,128)(2,1)} %tok_ref.1), channel_id=1, source_target_pairs={{0,2},{1,3},{2,0},{3,1},{4,6},{5,7},{6,4},{7,5},{8,10},{9,11},{10,... | collective-permute-start | bytes 3145736 | tf_op jit(solution)/shard_map/ppermute | solution.py:58
  46.1 23.3 %collective-permute-start.5 = (f32[8,256]{1,0:T(8,128)S(1)}, f32[8,256]{1,0:T(8,128)S(1)}, u32[]{:S(2)}, u32[]{:S(2)}) collective-permute-start(f32[8,256]{1,0:T(8,128)S(1)} %copy-done.47), channel_id=1, source_target_pairs={{0,2},{1,3},{2,0},{3,1},{4,6},{5,7},{6,4},{7,5},{8,10},{9,11},{10,... | collective-permute-start | bytes 24584 | tf_op jit(solution)/shard_map/ppermute | solution.py:58
  76.0 73.1 %copy-start.3 = (bf16[8,48,4224]{2,1,0:T(8,128)(2,1)}, bf16[8,48,4224]{2,1,0:T(8,128)(2,1)S(1)}, u32[]{:S(2)}) copy-start(bf16[8,48,4224]{2,1,0:T(8,128)(2,1)S(1)} %all-to-all-done) | copy-start | bytes 9732100
  76.0 46.4 %all-to-all-start.1 = ((bf16[8,48,2048]{2,1,0:T(8,128)(2,1)}), bf16[8,48,2048]{2,1,0:T(8,128)(2,1)}, u32[]{:S(2)}, u32[]{:S(2)}) async-start(bf16[8,48,2048]{2,1,0:T(8,128)(2,1)} %bitcast.71), calls=%async_computation.1 | async-start | bytes 3145728 | tf_op jit(solution)/shard_map/all_to_all | solution.py:62
  88.4 3.8 %copy-start.35 = (bf16[256,2048]{1,0:T(8,128)(2,1)S(1)}, bf16[256,2048]{1,0:T(8,128)(2,1)}, u32[]{:S(2)}) copy-start(bf16[256,2048]{1,0:T(8,128)(2,1)} %grad_ref.1) | copy-start | bytes 3145732
  88.9 29.5 %collective-permute-start.7 = (bf16[384,1536]{1,0:T(8,128)(2,1)S(1)}, bf16[384,1536]{1,0:T(8,128)(2,1)S(1)}, u32[]{:S(2)}, u32[]{:S(2)}) collective-permute-start(bf16[384,1536]{1,0:T(8,128)(2,1)S(1)} %get-tuple-element.107), channel_id=1, source_target_pairs={{0,32},{16,48},{32,64},{48,80},{64,96},{80,112},{96,0},{112,16},{1... | collective-permute-start | bytes 3538952 | tf_op jit(solution)/shard_map/ppermute | solution.py:28
  89.2 30.2 %collective-permute-start.8 = (bf16[384,1536]{1,0:T(8,128)(2,1)S(1)}, bf16[384,1536]{1,0:T(8,128)(2,1)S(1)}, u32[]{:S(2)}, u32[]{:S(2)}) collective-permute-start(bf16[384,1536]{1,0:T(8,128)(2,1)S(1)} %get-tuple-element.108), channel_id=1, source_target_pairs={{0,96},{16,112},{32,0},{48,16},{64,32},{80,48},{96,64},{112,80},{1... | collective-permute-start | bytes 3538952 | tf_op jit(solution)/shard_map/ppermute | solution.py:32
  92.2 26.2 %collective-permute-start.9 = (bf16[256,2048]{1,0:T(8,128)(2,1)S(1)}, bf16[256,2048]{1,0:T(8,128)(2,1)S(1)}, u32[]{:S(2)}, u32[]{:S(2)}) collective-permute-start(bf16[256,2048]{1,0:T(8,128)(2,1)S(1)} %copy-done.35), channel_id=1, source_target_pairs={{0,2},{1,3},{2,0},{3,1},{4,6},{5,7},{6,4},{7,5},{8,10},{9,11},{10,... | collective-permute-start | bytes 3145736 | tf_op jit(solution)/shard_map/ppermute | solution.py:58
  122.3 26.7 %all-to-all-start.2 = ((bf16[8,48,2176]{2,1,0:T(8,128)(2,1)}), bf16[8,48,2176]{2,1,0:T(8,128)(2,1)}, u32[]{:S(2)}, u32[]{:S(2)}) async-start(bf16[8,48,2176]{2,1,0:T(8,128)(2,1)} %bitcast.70), calls=%async_computation.2 | async-start | bytes 3342336 | tf_op jit(solution)/shard_map/all_to_all | solution.py:62
  144.3 1.7 copy-start.48
  149.0 1.9 copy-start.49
  160.1 3.4 %copy-start.56 = (bf16[768,768]{1,0:T(8,128)(2,1)S(1)}, bf16[768,768]{1,0:T(8,128)(2,1)}, u32[]{:S(2)}) copy-start(bf16[768,768]{1,0:T(8,128)(2,1)} %copy-done.55) | copy-start | bytes 3538948
  160.2 13.5 %collective-permute-start.10 = (bf16[128,1536]{1,0:T(8,128)(2,1)S(1)}, bf16[128,1536]{1,0:T(8,128)(2,1)S(1)}, u32[]{:S(2)}, u32[]{:S(2)}) collective-permute-start(bf16[128,1536]{1,0:T(8,128)(2,1)S(1)} %get-tuple-element.196), channel_id=1, source_target_pairs={{0,32},{16,48},{32,64},{48,80},{64,96},{80,112},{96,0},{112,16},{1... | collective-permute-start | bytes 1179656 | tf_op jit(solution)/shard_map/ppermute | solution.py:28
  160.2 13.4 %collective-permute-start.11 = (bf16[128,1536]{1,0:T(8,128)(2,1)S(1)}, bf16[128,1536]{1,0:T(8,128)(2,1)S(1)}, u32[]{:S(2)}, u32[]{:S(2)}) collective-permute-start(bf16[128,1536]{1,0:T(8,128)(2,1)S(1)} %get-tuple-element.195), channel_id=1, source_target_pairs={{0,96},{16,112},{32,0},{48,16},{64,32},{80,48},{96,64},{112,80},{1... | collective-permute-start | bytes 1179656 | tf_op jit(solution)/shard_map/ppermute | solution.py:32
  163.5 5.3 %copy-start.4 = (bf16[8,48,4224]{2,1,0:T(8,128)(2,1)S(1)}, bf16[8,48,4224]{2,1,0:T(8,128)(2,1)}, u32[]{:S(2)}) copy-start(bf16[8,48,4224]{2,1,0:T(8,128)(2,1)} %copy-done.3) | copy-start | bytes 9732100
  166.9 43.3 %copy-start = (bf16[8,128,1536]{2,1,0:T(8,128)(2,1)}, bf16[8,128,1536]{2,1,0:T(8,128)(2,1)S(1)}, u32[]{:S(2)}) copy-start(bf16[8,128,1536]{2,1,0:T(8,128)(2,1)S(1)} %shard_map.184.parts_ref) | copy-start | bytes 9437188
  167.0 10.9 %collective-permute-start.12 = (bf16[128,1536]{1,0:T(8,128)(2,1)S(1)}, bf16[128,1536]{1,0:T(8,128)(2,1)S(1)}, u32[]{:S(2)}, u32[]{:S(2)}) collective-permute-start(bf16[128,1536]{1,0:T(8,128)(2,1)S(1)} %get-tuple-element.194), channel_id=1, source_target_pairs={{0,16},{16,0},{32,48},{48,32},{64,80},{80,64},{96,112},{112,96},{1... | collective-permute-start | bytes 1179656 | tf_op jit(solution)/shard_map/ppermute | solution.py:36
  177.8 10.2 %copy-start.50 = (bf16[768,2048]{1,0:T(8,128)(2,1)S(1)}, bf16[768,2048]{1,0:T(8,128)(2,1)}, u32[]{:S(2)}) copy-start(bf16[768,2048]{1,0:T(8,128)(2,1)} %copy-done.48) | copy-start | bytes 9437188
  178.1 32.0 %collective-permute-start.13 = (bf16[448,1536]{1,0:T(8,128)(2,1)S(1)}, bf16[448,1536]{1,0:T(8,128)(2,1)S(1)}, u32[]{:S(2)}, u32[]{:S(2)}) collective-permute-start(bf16[448,1536]{1,0:T(8,128)(2,1)S(1)} %get-tuple-element.130), channel_id=1, source_target_pairs={{0,32},{16,48},{32,64},{48,80},{64,96},{80,112},{96,0},{112,16},{1... | collective-permute-start | bytes 4128776 | tf_op jit(solution)/shard_map/ppermute | solution.py:28
  178.2 32.0 %collective-permute-start.14 = (bf16[448,1536]{1,0:T(8,128)(2,1)S(1)}, bf16[448,1536]{1,0:T(8,128)(2,1)S(1)}, u32[]{:S(2)}, u32[]{:S(2)}) collective-permute-start(bf16[448,1536]{1,0:T(8,128)(2,1)S(1)} %get-tuple-element.131), channel_id=1, source_target_pairs={{0,96},{16,112},{32,0},{48,16},{64,32},{80,48},{96,64},{112,80},{1... | collective-permute-start | bytes 4128776 | tf_op jit(solution)/shard_map/ppermute | solution.py:32
  181.4 6.6 %copy-start.57 = (bf16[768,768]{1,0:T(8,128)(2,1)S(1)}, bf16[768,768]{1,0:T(8,128)(2,1)}, u32[]{:S(2)}) copy-start(bf16[768,768]{1,0:T(8,128)(2,1)} %copy-done.55) | copy-start | bytes 3538948
  182.4 5.7 %copy-start.16 = (bf16[384,1536]{1,0:T(8,128)(2,1)S(1)}, bf16[384,1536]{1,0:T(8,128)(2,1)}, u32[]{:S(2)}) copy-start(bf16[384,1536]{1,0:T(8,128)(2,1)} %copy-done.14) | copy-start | bytes 3538948
  182.4 5.7 %copy-start.20 = (bf16[384,1536]{1,0:T(8,128)(2,1)S(1)}, bf16[384,1536]{1,0:T(8,128)(2,1)}, u32[]{:S(2)}) copy-start(bf16[384,1536]{1,0:T(8,128)(2,1)} %copy-done.17) | copy-start | bytes 3538948
  182.4 5.7 %copy-start.24 = (bf16[384,1536]{1,0:T(8,128)(2,1)S(1)}, bf16[384,1536]{1,0:T(8,128)(2,1)}, u32[]{:S(2)}) copy-start(bf16[384,1536]{1,0:T(8,128)(2,1)} %copy-done.21) | copy-start | bytes 3538948
  182.4 5.7 %copy-start.28 = (bf16[384,1536]{1,0:T(8,128)(2,1)S(1)}, bf16[384,1536]{1,0:T(8,128)(2,1)}, u32[]{:S(2)}) copy-start(bf16[384,1536]{1,0:T(8,128)(2,1)} %copy-done.25) | copy-start | bytes 3538948
  182.4 5.7 %copy-start.32 = (bf16[384,1536]{1,0:T(8,128)(2,1)S(1)}, bf16[384,1536]{1,0:T(8,128)(2,1)}, u32[]{:S(2)}) copy-start(bf16[384,1536]{1,0:T(8,128)(2,1)} %copy-done.29) | copy-start | bytes 3538948
  182.4 5.7 %copy-start.42 = (bf16[384,1536]{1,0:T(8,128)(2,1)S(1)}, bf16[384,1536]{1,0:T(8,128)(2,1)}, u32[]{:S(2)}) copy-start(bf16[384,1536]{1,0:T(8,128)(2,1)} %copy-done.40) | copy-start | bytes 3538948
  182.4 5.7 %copy-start.45 = (bf16[384,1536]{1,0:T(8,128)(2,1)S(1)}, bf16[384,1536]{1,0:T(8,128)(2,1)}, u32[]{:S(2)}) copy-start(bf16[384,1536]{1,0:T(8,128)(2,1)} %copy-done.43) | copy-start | bytes 3538948
  182.4 17.9 %collective-permute-start.15 = (bf16[256,1536]{1,0:T(8,128)(2,1)}, bf16[256,1536]{1,0:T(8,128)(2,1)S(1)}, u32[]{:S(2)}, u32[]{:S(2)}) collective-permute-start(bf16[256,1536]{1,0:T(8,128)(2,1)} %pad_maximum_fusion.2), channel_id=1, source_target_pairs={{0,16},{16,0},{32,48},{48,32},{64,80},{80,64},{96,112},{112,96},{1... | collective-permute-start | bytes 2359304 | tf_op jit(solution)/shard_map/ppermute | solution.py:36
  188.1 22.1 %copy-start.1 = (bf16[512,1536]{1,0:T(8,128)(2,1)}, bf16[512,1536]{1,0:T(8,128)(2,1)S(1)}, u32[]{:S(2)}) copy-start(bf16[512,1536]{1,0:T(8,128)(2,1)S(1)} %shard_map.188.own_ref) | copy-start | bytes 4718596
  198.1 14.2 %copy-start.13 = (bf16[768,2176]{1,0:T(8,128)(2,1)}, bf16[768,2176]{1,0:T(8,128)(2,1)S(1)}, u32[]{:S(2)}) copy-start(bf16[768,2176]{1,0:T(8,128)(2,1)S(1)} %shard_map.187) | copy-start | bytes 10027012
  212.2 27.1 %collective-permute-start.16 = (bf16[384,1536]{1,0:T(8,128)(2,1)}, bf16[384,1536]{1,0:T(8,128)(2,1)S(1)}, u32[]{:S(2)}, u32[]{:S(2)}) collective-permute-start(bf16[384,1536]{1,0:T(8,128)(2,1)} %get-tuple-element.137), channel_id=1, source_target_pairs={{0,32},{16,48},{32,64},{48,80},{64,96},{80,112},{96,0},{112,16},{1... | collective-permute-start | bytes 3538952 | tf_op jit(solution)/shard_map/ppermute | solution.py:28
  212.2 28.1 %collective-permute-start.17 = (bf16[384,1536]{1,0:T(8,128)(2,1)}, bf16[384,1536]{1,0:T(8,128)(2,1)}, u32[]{:S(2)}, u32[]{:S(2)}) collective-permute-start(bf16[384,1536]{1,0:T(8,128)(2,1)} %get-tuple-element.138), channel_id=1, source_target_pairs={{0,96},{16,112},{32,0},{48,16},{64,32},{80,48},{96,64},{112,80},{1... | collective-permute-start | bytes 3538952 | tf_op jit(solution)/shard_map/ppermute | solution.py:32
  215.5 25.6 %collective-permute-start.18 = (bf16[384,1536]{1,0:T(8,128)(2,1)}, bf16[384,1536]{1,0:T(8,128)(2,1)}, u32[]{:S(2)}, u32[]{:S(2)}) collective-permute-start(bf16[384,1536]{1,0:T(8,128)(2,1)} %get-tuple-element.139), channel_id=1, source_target_pairs={{0,16},{16,0},{32,48},{48,32},{64,80},{80,64},{96,112},{112,96},{1... | collective-permute-start | bytes 3538952 | tf_op jit(solution)/shard_map/ppermute | solution.py:36
  217.2 23.8 %copy-start.6 = (f32[1,96,2048]{2,1,0:T(8,128)S(1)}, f32[1,96,2048]{2,1,0:T(8,128)}, u32[]{:S(2)}) copy-start(f32[1,96,2048]{2,1,0:T(8,128)} %param.15) | copy-start | bytes 2359300
  217.2 23.8 %copy-start.7 = (f32[1,96,2048]{2,1,0:T(8,128)S(1)}, f32[1,96,2048]{2,1,0:T(8,128)}, u32[]{:S(2)}) copy-start(f32[1,96,2048]{2,1,0:T(8,128)} %param.17) | copy-start | bytes 2359300
  217.2 23.8 %copy-start.8 = (f32[1,96,2048]{2,1,0:T(8,128)S(1)}, f32[1,96,2048]{2,1,0:T(8,128)}, u32[]{:S(2)}) copy-start(f32[1,96,2048]{2,1,0:T(8,128)} %param.19) | copy-start | bytes 2359300
  217.2 44.8 %all-to-all-start.3 = ((bf16[8,96,2176]{2,1,0:T(8,128)(2,1)}), bf16[8,96,2176]{2,1,0:T(8,128)(2,1)}, u32[]{:S(2)}, u32[]{:S(2)}) async-start(bf16[8,96,2176]{2,1,0:T(8,128)(2,1)} %bitcast.72), calls=%async_computation.3 | async-start | bytes 6684672 | tf_op jit(solution)/shard_map/all_to_all | solution.py:62
  247.5 25.5 %collective-permute-start.19 = (bf16[384,1536]{1,0:T(8,128)(2,1)S(1)}, bf16[384,1536]{1,0:T(8,128)(2,1)}, u32[]{:S(2)}, u32[]{:S(2)}) collective-permute-start(bf16[384,1536]{1,0:T(8,128)(2,1)S(1)} %shard_map.190.refs_0_), channel_id=1, source_target_pairs={{0,32},{16,48},{32,64},{48,80},{64,96},{80,112},{96,0},{112,16},{1... | collective-permute-start | bytes 3538952 | tf_op jit(solution)/shard_map/ppermute | solution.py:28
  247.5 25.5 %collective-permute-start.20 = (bf16[384,1536]{1,0:T(8,128)(2,1)S(1)}, bf16[384,1536]{1,0:T(8,128)(2,1)}, u32[]{:S(2)}, u32[]{:S(2)}) collective-permute-start(bf16[384,1536]{1,0:T(8,128)(2,1)S(1)} %shard_map.190.refs_0_), channel_id=1, source_target_pairs={{0,96},{16,112},{32,0},{48,16},{64,32},{80,48},{96,64},{112,80},{1... | collective-permute-start | bytes 3538952 | tf_op jit(solution)/shard_map/ppermute | solution.py:32
  250.8 23.7 %collective-permute-start.21 = (bf16[384,1536]{1,0:T(8,128)(2,1)S(1)}, bf16[384,1536]{1,0:T(8,128)(2,1)}, u32[]{:S(2)}, u32[]{:S(2)}) collective-permute-start(bf16[384,1536]{1,0:T(8,128)(2,1)S(1)} %shard_map.190.refs_0_), channel_id=1, source_target_pairs={{0,16},{16,0},{32,48},{48,32},{64,80},{80,64},{96,112},{112,96},{1... | collective-permute-start | bytes 3538952 | tf_op jit(solution)/shard_map/ppermute | solution.py:36
  253.7 1.9 copy-start.61
  253.8 2.7 copy-start.2
  253.8 3.1 copy-start.59
  253.8 3.6 %copy-start.60 = (f32[1,256,1536]{2,1,0:T(8,128)S(1)}, f32[1,256,1536]{2,1,0:T(8,128)}, u32[]{:S(2)}) copy-start(f32[1,256,1536]{2,1,0:T(8,128)} %param.16) | copy-start | bytes 4718596
  257.5 4.6 %copy-start.38 = (f32[8,256]{1,0:T(8,128)S(1)}, f32[8,256]{1,0:T(8,128)}, u32[]{:S(2)}) copy-start(f32[8,256]{1,0:T(8,128)} %copy-done.37) | copy-start | bytes 24580
  274.5 26.2 %collective-permute-start.22 = (bf16[384,1536]{1,0:T(8,128)(2,1)}, bf16[384,1536]{1,0:T(8,128)(2,1)S(1)}, u32[]{:S(2)}, u32[]{:S(2)}) collective-permute-start(bf16[384,1536]{1,0:T(8,128)(2,1)} %collective-permute-done.21.refs_1_), channel_id=1, source_target_pairs={{0,32},{16,48},{32,64},{48,80},{64,96},{80,112},{96,0},{112,16},{1... | collective-permute-start | bytes 3538952 | tf_op jit(solution)/shard_map/ppermute | solution.py:28
  274.5 26.2 %collective-permute-start.23 = (bf16[384,1536]{1,0:T(8,128)(2,1)}, bf16[384,1536]{1,0:T(8,128)(2,1)S(1)}, u32[]{:S(2)}, u32[]{:S(2)}) collective-permute-start(bf16[384,1536]{1,0:T(8,128)(2,1)} %collective-permute-done.21.refs_1_), channel_id=1, source_target_pairs={{0,96},{16,112},{32,0},{48,16},{64,32},{80,48},{96,64},{112,80},{1... | collective-permute-start | bytes 3538952 | tf_op jit(solution)/shard_map/ppermute | solution.py:32
  277.7 23.0 %collective-permute-start.24 = (bf16[256,2176]{1,0:T(8,128)(2,1)S(1)}, bf16[256,2176]{1,0:T(8,128)(2,1)S(1)}, u32[]{:S(2)}, u32[]{:S(2)}) collective-permute-start(bf16[256,2176]{1,0:T(8,128)(2,1)S(1)} %get-tuple-element.148), channel_id=1, source_target_pairs={{0,2},{1,3},{2,0},{3,1},{4,6},{5,7},{6,4},{7,5},{8,10},{9,11},{10,... | collective-permute-start | bytes 3342344 | tf_op jit(solution)/shard_map/ppermute | solution.py:58
  303.4 23.4 %collective-permute-start.25 = (bf16[384,1536]{1,0:T(8,128)(2,1)}, bf16[384,1536]{1,0:T(8,128)(2,1)S(1)}, u32[]{:S(2)}, u32[]{:S(2)}) collective-permute-start(bf16[384,1536]{1,0:T(8,128)(2,1)} %get-tuple-element.153), channel_id=1, source_target_pairs={{0,32},{16,48},{32,64},{48,80},{64,96},{80,112},{96,0},{112,16},{1... | collective-permute-start | bytes 3538952 | tf_op jit(solution)/shard_map/ppermute | solution.py:28
  303.5 23.3 %collective-permute-start.26 = (bf16[384,1536]{1,0:T(8,128)(2,1)}, bf16[384,1536]{1,0:T(8,128)(2,1)}, u32[]{:S(2)}, u32[]{:S(2)}) collective-permute-start(bf16[384,1536]{1,0:T(8,128)(2,1)} %get-tuple-element.154), channel_id=1, source_target_pairs={{0,96},{16,112},{32,0},{48,16},{64,32},{80,48},{96,64},{112,80},{1... | collective-permute-start | bytes 3538952 | tf_op jit(solution)/shard_map/ppermute | solution.py:32
  (30 other events, 34.3 us)

commit v4 on v3

--- a/solution.py
+++ b/solution.py
@@ -382,7 +382,7 @@
     )
 
 
-def pass_on(below, above, up2, down2):
+def pass_on(below, above, up2, down2, grant):
     vmem = pl.BlockSpec(memory_space=pltpu.VMEM)
     return pl.pallas_call(
         pass_on_kernel,
@@ -391,7 +391,7 @@
         out_specs=(vmem, vmem),
         scratch_shapes=[pltpu.SemaphoreType.DMA((4,))],
         cost_estimate=pl.CostEstimate(flops=0, bytes_accessed=4_800_000, transcendentals=0),
-        compiler_params=pltpu.CompilerParams(vmem_limit_bytes=6 << 20),
+        compiler_params=pltpu.CompilerParams(vmem_limit_bytes=grant),
     )(below, above, up2, down2)
 
 
@@ -569,7 +569,7 @@
         up2, down2, their_aux, their_tok, grad_next
     )
 
-    up3, down3 = pass_on(below, above, up2, down2)
+    up3, down3 = pass_on(below, above, up2, down2, 56 << 20)
     up3, down3, their_grad = z_up(up3), z_down(down3), yh_swap(grad_next)
     send_far = call(
         spread_tokens_kernel,
@@ -700,7 +700,7 @@
     pieces = [(i, (n, 0), (n, 192)) for n, i in enumerate((0, 1, 2, 6))]
     new_gate_up, new_down = place_shards(columns, (new_own, other, above, below), pieces)
     up2, down2, far_sum, new_gate_up, new_down = tie(up2, down2, far_sum, new_gate_up, new_down)
-    up3, down3 = pass_on(below, above, up2, down2)
+    up3, down3 = pass_on(below, above, up2, down2, 6 << 20)
     up3, down3 = z_up(up3), z_down(down3)
     new_gate_up, new_down = place_shards(
         columns,

time: 337 us -> 332 us (0.985)
  local copies, waits for them, and re-layouts: 43.5 us -> 33.9 us
    unnamed x127 -> x111, local copies, waits for them, and re-layouts: 43.1 us -> 33.6 us
  transfers between devices with their start and end apart: 31 -> 31, of which waited for: 13 -> 14; matrix products, arithmetic and copies ran while one was open for 3% -> 3% of each run, Pallas kernels for 16% -> 17%
where the time goes in v4:
time: 332 us; the launch traced here: 326 us
  waiting for transfers between devices  139 us (42%)
  starting transfers between devices  71.7 us (22%)
  Pallas kernels  69.1 us (21%)
  local copies, waits for them, and re-layouts  33.9 us (10%)
  other arithmetic  10.2 us (3%)
    ppermute x9, waiting for transfers between devices, z_up(): return lax.ppermute(a, 'dp', Z_UP)  64.8 us
    ppermute x4, waiting for transfers between devices, yh_swap(): return lax.ppermute(a, 'expert', YH_SWAP)  61.4 us
    pallas_call x14, Pallas kernels, call(): pl.pallas_call(kernel, out_shape=outs, in_specs=[smem] * scalars + [vmem]...  48.9 us
    unnamed x111, local copies, waits for them, and re-layouts  33.6 us
    ppermute x9, starting transfers between devices, z_down(): return lax.ppermute(a, 'dp', Z_DOWN)  26.8 us
    all_to_all x4, starting transfers between devices, exchange(): lax.all_to_all(rows.reshape(8, rows.shape[0] // 8, rows.shape[1]), 'exper...  22.9 us
    ppermute x5, waiting for transfers between devices, y_swap(): return lax.ppermute(a, 'dp', Y_SWAP)  9.96 us
    ppermute x4, starting transfers between devices, yh_swap(): return lax.ppermute(a, 'expert', YH_SWAP)  9.89 us
  transfers between devices with their start and end apart: 31, of which 14 were waited for; matrix products, arithmetic and copies ran while one was open for 3% of the time, Pallas kernels for 17%

profile of v4, /device:TPU:4, one launch (start us, length us, event | category | flops | bytes accessed | tf_op | source)
XLA Modules:
  0.0 325.9 jit_solution(7103675837269696407)
XLA Ops:
  0.7 1.3 bitcast_convert_fusion
  2.6 2.0 collective-permute-start
  4.5 2.2 collective-permute-start.1
  6.7 1.6 collective-permute-start.2
  11.6 1.6 shard_map.178
  13.3 1.7 copy-done.5
  14.9 17.7 %collective-permute-done.below_ref.refs_2_ = bf16[384,1536]{1,0:T(8,128)(2,1)S(1)} collective-permute-done((bf16[384,1536]{1,0:T(8,128)(2,1)S(1)}, bf16[384,1536]{1,0:T(8,128)(2,1)S(1)}, u32[]{:S(2)}, u32[]{:S(2)}) %collective-permute-start) | collective-permute-done | bytes 1179680 | tf_op jit(solution)/shard_map/ppermute | solution.py:28
  32.6 1.6 collective-permute-done.2.refs_1_
  34.3 4.8 %all-to-all-start = ((bf16[8,48,4224]{2,1,0:T(8,128)(2,1)}), bf16[8,48,4224]{2,1,0:T(8,128)(2,1)S(1)}, u32[]{:S(2)}, u32[]{:S(2)}) async-start(bf16[8,48,4224]{2,1,0:T(8,128)(2,1)} %bitcast.63), calls=%async_computation | async-start | bytes 6488064 | tf_op jit(solution)/shard_map/all_to_all | solution.py:62
  39.7 2.6 collective-permute-start.4
  42.3 3.2 collective-permute-start.6
  45.9 23.0 %collective-permute-done.5.aux_ref.far_aux_ref = f32[8,256]{1,0:T(8,128)S(1)} collective-permute-done((f32[8,256]{1,0:T(8,128)}, f32[8,256]{1,0:T(8,128)S(1)}, u32[]{:S(2)}, u32[]{:S(2)}) %collective-permute-start.5) | collective-permute-done | bytes 8224 | tf_op jit(solution)/shard_map/ppermute | solution.py:58
  72.2 3.2 all-to-all-done
  75.4 7.3 %all-to-all-start.1 = ((bf16[8,48,2048]{2,1,0:T(8,128)(2,1)}), bf16[8,48,2048]{2,1,0:T(8,128)(2,1)}, u32[]{:S(2)}, u32[]{:S(2)}) async-start(bf16[8,48,2048]{2,1,0:T(8,128)(2,1)} %bitcast.71), calls=%async_computation.1 | async-start | bytes 3145728 | tf_op jit(solution)/shard_map/all_to_all | solution.py:62
  82.8 3.1 shard_map.180
  86.6 2.6 collective-permute-start.8
  89.2 3.2 collective-permute-start.9
  92.4 23.0 %collective-permute-done.9.grad_ref = bf16[256,2048]{1,0:T(8,128)(2,1)S(1)} collective-permute-done((bf16[256,2048]{1,0:T(8,128)(2,1)S(1)}, bf16[256,2048]{1,0:T(8,128)(2,1)S(1)}, u32[]{:S(2)}, u32[]{:S(2)}) %collective-permute-start.9) | collective-permute-done | bytes 1048608 | tf_op jit(solution)/shard_map/ppermute | solution.py:58
  119.3 5.0 %all-to-all-start.2 = ((bf16[8,48,2176]{2,1,0:T(8,128)(2,1)}), bf16[8,48,2176]{2,1,0:T(8,128)(2,1)}, u32[]{:S(2)}, u32[]{:S(2)}) async-start(bf16[8,48,2176]{2,1,0:T(8,128)(2,1)} %bitcast.70), calls=%async_computation.2 | async-start | bytes 3342336 | tf_op jit(solution)/shard_map/all_to_all | solution.py:62
  125.6 1.3 copy-done.18
  126.8 1.3 copy-done.21
  128.1 1.3 copy-done.24
  129.4 1.3 copy-done.34
  130.7 1.3 copy-done.37
  131.9 8.0 %shard_map.182 = (bf16[768,768]{1,0:T(8,128)(2,1)S(1)}, bf16[768,768]{1,0:T(8,128)(2,1)S(1)}, bf16[768,768]{1,0:T(8,128)(2,1)S(1)}, bf16[768,2048]{1,0:T(8,128)(2,1)S(1)}) custom-call(s32[8]{0:T(128)S(1)} %stack.35.column_ref, bf16[384,4224]{1,0:T(8,128)(2,1)S(1)} %bitcast.58, bf16[384,2048]{1,0:T(8,128)(2,1)} %bitcast.16.far_ref.far_in_ref, ...), custom_call_target="tpu_custom_call" | custom-call | flops 4800000000 | bytes 20938784 | tf_op jit(solution)/shard_map/pallas_call | solution.py:515
  140.0 1.7 copy-done.40
  144.8 1.9 copy-done.41
  149.2 6.6 %shard_map.183 = (bf16[768,1536]{1,0:T(8,128)(2,1)S(1)}, bf16[512,1536]{1,0:T(8,128)(2,1)S(1)}, bf16[768,2048]{1,0:T(8,128)(2,1)S(1)}) custom-call(bf16[384,4224]{1,0:T(8,128)(2,1)S(1)} %bitcast.59, bf16[384,2048]{1,0:T(8,128)(2,1)} %bitcast.16.far_ref.far_in_ref, bf16[384,2176]{1,0:T(8,128)(2,1)} %bitcast.18.far_grad_ref, bf16[768,768]{1,0:T(8,128)(2,1)S(1)} %copy-done.44, ...), custom_call_target="tpu_custom_call" | custom-call | flops 3600000000 | bytes 19070976 | tf_op jit(solution)/shard_map/pallas_call | solution.py:515
  156.0 3.2 collective-permute-start.11
  159.2 3.4 %shard_map.184.parts_ref = bf16[8,128,1536]{2,1,0:T(8,128)(2,1)S(1)} custom-call(s32[8]{0:T(128)S(1)} %stack.35.column_ref, bf16[768,768]{1,0:T(8,128)(2,1)S(1)} %copy-done.48, bf16[768,2048]{1,0:T(8,128)(2,1)S(1)} %get-tuple-element.121.scaled_ref), custom_call_target="tpu_custom_call" | custom-call | flops 2400000000 | bytes 7471136 | tf_op jit(solution)/shard_map/pallas_call | solution.py:515
  162.7 1.9 collective-permute-start.12
  164.6 4.8 %shard_map.185 = (bf16[512,1536]{1,0:T(8,128)(2,1)S(1)}, bf16[512,1536]{1,0:T(8,128)(2,1)S(1)}) custom-call(bf16[384,4224]{1,0:T(8,128)(2,1)S(1)} %bitcast.60, bf16[384,2048]{1,0:T(8,128)(2,1)} %bitcast.16.far_ref.far_in_ref, bf16[768,1536]{1,0:T(8,128)(2,1)S(1)} %get-tuple-element.132.proj_ref), custom_call_target="tpu_custom_call" | custom-call | flops 2400000000 | bytes 10321920 | tf_op jit(solution)/shard_map/pallas_call | solution.py:515
  169.5 4.1 %collective-permute-done.12.y_ref = bf16[128,1536]{1,0:T(8,128)(2,1)S(1)} collective-permute-done((bf16[128,1536]{1,0:T(8,128)(2,1)S(1)}, bf16[128,1536]{1,0:T(8,128)(2,1)S(1)}, u32[]{:S(2)}, u32[]{:S(2)}) %collective-permute-start.12) | collective-permute-done | bytes 393248 | tf_op jit(solution)/shard_map/ppermute | solution.py:36
  174.0 3.2 collective-permute-start.14
  178.2 1.7 collective-permute-start.15
  179.9 3.9 %shard_map.188.own_ref = bf16[512,1536]{1,0:T(8,128)(2,1)S(1)} custom-call(bf16[384,4224]{1,0:T(8,128)(2,1)S(1)} %bitcast.61, bf16[384,2048]{1,0:T(8,128)(2,1)} %bitcast.16.far_ref.far_in_ref, bf16[768,1536]{1,0:T(8,128)(2,1)S(1)} %get-tuple-element.132.proj_ref), custom_call_target="tpu_custom_call" | custom-call | flops 1200000000 | bytes 8749056 | tf_op jit(solution)/shard_map/pallas_call | solution.py:515
  183.8 10.3 %shard_map.187 = bf16[768,2176]{1,0:T(8,128)(2,1)S(1)} custom-call(bf16[384,4224]{1,0:T(8,128)(2,1)S(1)} %bitcast.62, bf16[384,2176]{1,0:T(8,128)(2,1)} %bitcast.18.far_grad_ref, bf16[768,768]{1,0:T(8,128)(2,1)S(1)} %copy-done.49, bf16[768,1536]{1,0:T(8,128)(2,1)S(1)} %get-tuple-element.132.proj_ref, bf16[768,2048]{1,0:T(8,128)(2,1)S(1)} %copy-done.42, ...), custom_call_target="tpu_custom_call" | custom-call | flops 7200000000 | bytes 24379392 | tf_op jit(solution)/shard_map/pallas_call | solution.py:515
  194.1 1.9 collective-permute-done.15.y_ref
  196.1 9.9 %collective-permute-done.13.up_ref = bf16[448,1536]{1,0:T(8,128)(2,1)S(1)} collective-permute-done((bf16[448,1536]{1,0:T(8,128)(2,1)S(1)}, bf16[448,1536]{1,0:T(8,128)(2,1)S(1)}, u32[]{:S(2)}, u32[]{:S(2)}) %collective-permute-start.13) | collective-permute-done | bytes 1376288 | tf_op jit(solution)/shard_map/ppermute | solution.py:28
  206.0 2.0 shard_map.189
  208.0 3.2 collective-permute-start.17
  211.2 1.8 collective-permute-start.18
  213.1 5.7 %all-to-all-start.3 = ((bf16[8,96,2176]{2,1,0:T(8,128)(2,1)}), bf16[8,96,2176]{2,1,0:T(8,128)(2,1)}, u32[]{:S(2)}, u32[]{:S(2)}) async-start(bf16[8,96,2176]{2,1,0:T(8,128)(2,1)} %bitcast.72), calls=%async_computation.3 | async-start | bytes 6684672 | tf_op jit(solution)/shard_map/all_to_all | solution.py:62
  218.7 16.3 %collective-permute-done.16.up_ref = bf16[384,1536]{1,0:T(8,128)(2,1)S(1)} collective-permute-done((bf16[384,1536]{1,0:T(8,128)(2,1)}, bf16[384,1536]{1,0:T(8,128)(2,1)S(1)}, u32[]{:S(2)}, u32[]{:S(2)}) %collective-permute-start.16) | collective-permute-done | bytes 1179680 | tf_op jit(solution)/shard_map/ppermute | solution.py:28
  238.2 5.1 %shard_map.190.refs_0_ = bf16[384,1536]{1,0:T(8,128)(2,1)S(1)} custom-call(bf16[512,1536]{1,0:T(8,128)(2,1)} %copy-done.1, bf16[8,128,1536]{2,1,0:T(8,128)(2,1)} %copy-done, bf16[384,1536]{1,0:T(8,128)(2,1)S(1)} %copy-done.12, bf16[384,1536]{1,0:T(8,128)(2,1)} %collective-permute-done.17.down_ref, bf16[384,1536]{1,0:T(8,128)(2,1)} %collective-permute-done.18.y_ref, ...), custom_call_target="tpu_custom_call" | custom-call | flops 20000000 | bytes 12000000 | tf_op jit(solution)/shard_map/pallas_call | solution.py:483
  243.4 3.2 collective-permute-start.20
  246.6 1.6 collective-permute-start.21
  248.2 1.4 fusion.6
  249.7 1.8 multiply_subtract_fusion.1
  253.3 4.6 %multiply_subtract_fusion = (f32[256,1536]{1,0:T(8,128)}, f32[256,1536]{1,0:T(8,128)}, f32[256,1536]{1,0:T(8,128)}) fusion(f32[1,256,1536]{2,1,0:T(8,128)S(1)} %copy-done.51, bf16[384,1536]{1,0:T(8,128)(2,1)} %collective-permute-done.18.y_ref, bf16[384,1536]{1,0:T(8,128)(2,1)} %collective-permute-done.17.down_ref, bf16[384,1536]{1,0:T(8,128)(2,1)S(1)} %copy-done.12, ...), kind=kLoop, calls=%fused_computation.4 | loop fusion | flops 8650752 | bytes 12582912 | tf_op jit(solution)/shard_map/sub | solution.py:43
  257.9 4.4 %shard_map.191 = (f32[256,2176]{1,0:T(8,128)S(1)}, bf16[256,2176]{1,0:T(8,128)(2,1)S(1)}) custom-call(f32[8,256]{1,0:T(8,128)S(1)} %copy-done.31, f32[8,256]{1,0:T(8,128)S(1)} %collective-permute-done.5.aux_ref.far_aux_ref, bf16[768,2176]{1,0:T(8,128)(2,1)} %bitcast.27.rows_ref), custom_call_target="tpu_custom_call" | custom-call | flops 1700000000 | bytes 6701056 | tf_op jit(solution)/shard_map/pallas_call | solution.py:515
  262.3 6.5 %collective-permute-done.19.refs_3_.below_ref = bf16[384,1536]{1,0:T(8,128)(2,1)} collective-permute-done((bf16[384,1536]{1,0:T(8,128)(2,1)S(1)}, bf16[384,1536]{1,0:T(8,128)(2,1)}, u32[]{:S(2)}, u32[]{:S(2)}) %collective-permute-start.19) | collective-permute-done | bytes 1179680 | tf_op jit(solution)/shard_map/ppermute | solution.py:28
  268.8 1.5 collective-permute-done.21.refs_1_
  270.3 3.2 collective-permute-start.23
  273.5 3.2 collective-permute-start.24
  276.7 4.4 %shard_map.192 = (bf16[2048,1536]{1,0:T(8,128)(2,1)}, bf16[768,2048]{1,0:T(8,128)(2,1)}) custom-call(s32[8]{0:T(128)S(1)} %stack.35.column_ref, bf16[384,1536]{1,0:T(8,128)(2,1)S(1)} %shard_map.190.refs_0_, bf16[384,1536]{1,0:T(8,128)(2,1)} %collective-permute-done.21.refs_1_, bf16[384,1536]{1,0:T(8,128)(2,1)} %collective-permute-done.20.refs_2_.above_ref, ...), custom_call_target="tpu_custom_call" | custom-call | bytes 9600000 | tf_op jit(solution)/shard_map/pallas_call | solution.py:420
  281.1 15.4 %collective-permute-done.24.far_ref = bf16[256,2176]{1,0:T(8,128)(2,1)S(1)} collective-permute-done((bf16[256,2176]{1,0:T(8,128)(2,1)S(1)}, bf16[256,2176]{1,0:T(8,128)(2,1)S(1)}, u32[]{:S(2)}, u32[]{:S(2)}) %collective-permute-start.24) | collective-permute-done | bytes 1114144 | tf_op jit(solution)/shard_map/ppermute | solution.py:58
  296.5 2.7 shard_map.193
  299.3 3.2 collective-permute-start.26
  302.5 1.7 shard_map.195
  304.8 1.5 copy.24
  306.3 2.0 shard_map.194
  308.4 14.3 %collective-permute-done.25.refs_0_ = bf16[384,1536]{1,0:T(8,128)(2,1)S(1)} collective-permute-done((bf16[384,1536]{1,0:T(8,128)(2,1)}, bf16[384,1536]{1,0:T(8,128)(2,1)S(1)}, u32[]{:S(2)}, u32[]{:S(2)}) %collective-permute-start.25) | collective-permute-done | bytes 1179680 | tf_op jit(solution)/shard_map/ppermute | solution.py:28
  322.6 2.8 shard_map.196
  (146 shorter events, 27.0 us)
Async XLA Ops:
  0.6 1.6 copy-start.50
  2.4 5.9 %copy-start.54 = (bf16[256,2]{0,1:T(2,128)(2,1)S(1)}, bf16[256,2]{0,1:T(2,128)(2,1)}, u32[]{:S(2)}) copy-start(bf16[256,2]{0,1:T(2,128)(2,1)} %param.13) | copy-start | bytes 3076
  2.4 5.9 %copy-start.32 = (s32[256,2]{0,1:T(2,128)S(1)}, s32[256,2]{0,1:T(2,128)}, u32[]{:S(2)}) copy-start(s32[256,2]{0,1:T(2,128)} %param.12) | copy-start | bytes 6148
  2.5 10.7 %copy-start.14 = (bf16[384,1536]{1,0:T(8,128)(2,1)}, bf16[384,1536]{1,0:T(8,128)(2,1)S(1)}, u32[]{:S(2)}) copy-start(bf16[384,1536]{1,0:T(8,128)(2,1)S(1)} %fusion.3.refs_0_) | copy-start | bytes 3538948
  2.6 30.1 %collective-permute-start = (bf16[384,1536]{1,0:T(8,128)(2,1)S(1)}, bf16[384,1536]{1,0:T(8,128)(2,1)S(1)}, u32[]{:S(2)}, u32[]{:S(2)}) collective-permute-start(bf16[384,1536]{1,0:T(8,128)(2,1)S(1)} %fusion.3.refs_0_), channel_id=1, source_target_pairs={{0,32},{16,48},{32,64},{48,80},{64,96},{80,112},{96,0},{112,16},{1... | collective-permute-start | bytes 3538952 | tf_op jit(solution)/shard_map/ppermute | solution.py:28
  4.5 28.1 %collective-permute-start.1 = (bf16[384,1536]{1,0:T(8,128)(2,1)S(1)}, bf16[384,1536]{1,0:T(8,128)(2,1)S(1)}, u32[]{:S(2)}, u32[]{:S(2)}) collective-permute-start(bf16[384,1536]{1,0:T(8,128)(2,1)S(1)} %fusion.3.refs_0_), channel_id=1, source_target_pairs={{0,96},{16,112},{32,0},{48,16},{64,32},{80,48},{96,64},{112,80},{1... | collective-permute-start | bytes 3538952 | tf_op jit(solution)/shard_map/ppermute | solution.py:32
  6.7 27.5 %collective-permute-start.2 = (bf16[384,1536]{1,0:T(8,128)(2,1)S(1)}, bf16[384,1536]{1,0:T(8,128)(2,1)}, u32[]{:S(2)}, u32[]{:S(2)}) collective-permute-start(bf16[384,1536]{1,0:T(8,128)(2,1)S(1)} %fusion.3.refs_0_), channel_id=1, source_target_pairs={{0,16},{16,0},{32,48},{48,32},{64,80},{80,64},{96,112},{112,96},{1... | collective-permute-start | bytes 3538952 | tf_op jit(solution)/shard_map/ppermute | solution.py:36
  9.1 4.1 %copy-start.30 = (f32[8,256]{1,0:T(8,128)}, f32[8,256]{1,0:T(8,128)S(1)}, u32[]{:S(2)}) copy-start(f32[8,256]{1,0:T(8,128)S(1)} %get-tuple-element.94.aux_ref.near_aux_ref) | copy-start | bytes 24580
  13.2 1.7 copy-start.5
  32.6 1.6 copy-start.17
  32.6 1.6 copy-start.20
  34.3 41.1 %all-to-all-start = ((bf16[8,48,4224]{2,1,0:T(8,128)(2,1)}), bf16[8,48,4224]{2,1,0:T(8,128)(2,1)S(1)}, u32[]{:S(2)}, u32[]{:S(2)}) async-start(bf16[8,48,4224]{2,1,0:T(8,128)(2,1)} %bitcast.63), calls=%async_computation | async-start | bytes 6488064 | tf_op jit(solution)/shard_map/all_to_all | solution.py:62
  39.1 29.8 %collective-permute-start.3 = (bf16[384,1536]{1,0:T(8,128)(2,1)}, bf16[384,1536]{1,0:T(8,128)(2,1)S(1)}, u32[]{:S(2)}, u32[]{:S(2)}) collective-permute-start(bf16[384,1536]{1,0:T(8,128)(2,1)} %collective-permute-done.2.refs_1_), channel_id=1, source_target_pairs={{0,32},{16,48},{32,64},{48,80},{64,96},{80,112},{96,0},{112,16},{1... | collective-permute-start | bytes 3538952 | tf_op jit(solution)/shard_map/ppermute | solution.py:28
  39.7 30.2 %collective-permute-start.4 = (bf16[384,1536]{1,0:T(8,128)(2,1)}, bf16[384,1536]{1,0:T(8,128)(2,1)}, u32[]{:S(2)}, u32[]{:S(2)}) collective-permute-start(bf16[384,1536]{1,0:T(8,128)(2,1)} %collective-permute-done.2.refs_1_), channel_id=1, source_target_pairs={{0,96},{16,112},{32,0},{48,16},{64,32},{80,48},{96,64},{112,80},{1... | collective-permute-start | bytes 3538952 | tf_op jit(solution)/shard_map/ppermute | solution.py:32
  42.3 26.5 %collective-permute-start.6 = (bf16[256,2048]{1,0:T(8,128)(2,1)}, bf16[256,2048]{1,0:T(8,128)(2,1)S(1)}, u32[]{:S(2)}, u32[]{:S(2)}) collective-permute-start(bf16[256,2048]{1,0:T(8,128)(2,1)} %tok_ref.1), channel_id=1, source_target_pairs={{0,2},{1,3},{2,0},{3,1},{4,6},{5,7},{6,4},{7,5},{8,10},{9,11},{10,... | collective-permute-start | bytes 3145736 | tf_op jit(solution)/shard_map/ppermute | solution.py:58
  45.5 23.3 %collective-permute-start.5 = (f32[8,256]{1,0:T(8,128)}, f32[8,256]{1,0:T(8,128)S(1)}, u32[]{:S(2)}, u32[]{:S(2)}) collective-permute-start(f32[8,256]{1,0:T(8,128)} %copy-done.39), channel_id=1, source_target_pairs={{0,2},{1,3},{2,0},{3,1},{4,6},{5,7},{6,4},{7,5},{8,10},{9,11},{10,... | collective-permute-start | bytes 24584 | tf_op jit(solution)/shard_map/ppermute | solution.py:58
  75.4 69.4 %copy-start.3 = (bf16[8,48,4224]{2,1,0:T(8,128)(2,1)}, bf16[8,48,4224]{2,1,0:T(8,128)(2,1)S(1)}, u32[]{:S(2)}) copy-start(bf16[8,48,4224]{2,1,0:T(8,128)(2,1)S(1)} %all-to-all-done) | copy-start | bytes 9732100
  75.4 43.8 %all-to-all-start.1 = ((bf16[8,48,2048]{2,1,0:T(8,128)(2,1)}), bf16[8,48,2048]{2,1,0:T(8,128)(2,1)}, u32[]{:S(2)}, u32[]{:S(2)}) async-start(bf16[8,48,2048]{2,1,0:T(8,128)(2,1)} %bitcast.71), calls=%async_computation.1 | async-start | bytes 3145728 | tf_op jit(solution)/shard_map/all_to_all | solution.py:62
  82.8 6.4 %copy-start.28 = (bf16[256,2048]{1,0:T(8,128)(2,1)S(1)}, bf16[256,2048]{1,0:T(8,128)(2,1)}, u32[]{:S(2)}) copy-start(bf16[256,2048]{1,0:T(8,128)(2,1)} %grad_ref.1) | copy-start | bytes 3145732
  85.9 29.5 %collective-permute-start.7 = (bf16[384,1536]{1,0:T(8,128)(2,1)}, bf16[384,1536]{1,0:T(8,128)(2,1)S(1)}, u32[]{:S(2)}, u32[]{:S(2)}) collective-permute-start(bf16[384,1536]{1,0:T(8,128)(2,1)} %get-tuple-element.107), channel_id=1, source_target_pairs={{0,32},{16,48},{32,64},{48,80},{64,96},{80,112},{96,0},{112,16},{1... | collective-permute-start | bytes 3538952 | tf_op jit(solution)/shard_map/ppermute | solution.py:28
  86.6 29.8 %collective-permute-start.8 = (bf16[384,1536]{1,0:T(8,128)(2,1)}, bf16[384,1536]{1,0:T(8,128)(2,1)S(1)}, u32[]{:S(2)}, u32[]{:S(2)}) collective-permute-start(bf16[384,1536]{1,0:T(8,128)(2,1)} %get-tuple-element.108), channel_id=1, source_target_pairs={{0,96},{16,112},{32,0},{48,16},{64,32},{80,48},{96,64},{112,80},{1... | collective-permute-start | bytes 3538952 | tf_op jit(solution)/shard_map/ppermute | solution.py:32
  89.2 26.2 %collective-permute-start.9 = (bf16[256,2048]{1,0:T(8,128)(2,1)S(1)}, bf16[256,2048]{1,0:T(8,128)(2,1)S(1)}, u32[]{:S(2)}, u32[]{:S(2)}) collective-permute-start(bf16[256,2048]{1,0:T(8,128)(2,1)S(1)} %copy-done.28), channel_id=1, source_target_pairs={{0,2},{1,3},{2,0},{3,1},{4,6},{5,7},{6,4},{7,5},{8,10},{9,11},{10,... | collective-permute-start | bytes 3145736 | tf_op jit(solution)/shard_map/ppermute | solution.py:58
  119.3 25.5 %all-to-all-start.2 = ((bf16[8,48,2176]{2,1,0:T(8,128)(2,1)}), bf16[8,48,2176]{2,1,0:T(8,128)(2,1)}, u32[]{:S(2)}, u32[]{:S(2)}) async-start(bf16[8,48,2176]{2,1,0:T(8,128)(2,1)} %bitcast.70), calls=%async_computation.2 | async-start | bytes 3342336 | tf_op jit(solution)/shard_map/all_to_all | solution.py:62
  139.9 1.7 copy-start.40
  144.8 1.9 copy-start.41
  155.8 3.4 %copy-start.48 = (bf16[768,768]{1,0:T(8,128)(2,1)S(1)}, bf16[768,768]{1,0:T(8,128)(2,1)}, u32[]{:S(2)}) copy-start(bf16[768,768]{1,0:T(8,128)(2,1)} %copy-done.47) | copy-start | bytes 3538948
  155.9 13.5 %collective-permute-start.10 = (bf16[128,1536]{1,0:T(8,128)(2,1)S(1)}, bf16[128,1536]{1,0:T(8,128)(2,1)S(1)}, u32[]{:S(2)}, u32[]{:S(2)}) collective-permute-start(bf16[128,1536]{1,0:T(8,128)(2,1)S(1)} %get-tuple-element.196), channel_id=1, source_target_pairs={{0,32},{16,48},{32,64},{48,80},{64,96},{80,112},{96,0},{112,16},{1... | collective-permute-start | bytes 1179656 | tf_op jit(solution)/shard_map/ppermute | solution.py:28
  156.0 13.5 %collective-permute-start.11 = (bf16[128,1536]{1,0:T(8,128)(2,1)S(1)}, bf16[128,1536]{1,0:T(8,128)(2,1)S(1)}, u32[]{:S(2)}, u32[]{:S(2)}) collective-permute-start(bf16[128,1536]{1,0:T(8,128)(2,1)S(1)} %get-tuple-element.195), channel_id=1, source_target_pairs={{0,96},{16,112},{32,0},{48,16},{64,32},{80,48},{96,64},{112,80},{1... | collective-permute-start | bytes 1179656 | tf_op jit(solution)/shard_map/ppermute | solution.py:32
  159.2 5.4 %copy-start.4 = (bf16[8,48,4224]{2,1,0:T(8,128)(2,1)S(1)}, bf16[8,48,4224]{2,1,0:T(8,128)(2,1)}, u32[]{:S(2)}) copy-start(bf16[8,48,4224]{2,1,0:T(8,128)(2,1)} %copy-done.3) | copy-start | bytes 9732100
  162.6 43.4 %copy-start = (bf16[8,128,1536]{2,1,0:T(8,128)(2,1)}, bf16[8,128,1536]{2,1,0:T(8,128)(2,1)S(1)}, u32[]{:S(2)}) copy-start(bf16[8,128,1536]{2,1,0:T(8,128)(2,1)S(1)} %shard_map.184.parts_ref) | copy-start | bytes 9437188
  162.7 10.9 %collective-permute-start.12 = (bf16[128,1536]{1,0:T(8,128)(2,1)S(1)}, bf16[128,1536]{1,0:T(8,128)(2,1)S(1)}, u32[]{:S(2)}, u32[]{:S(2)}) collective-permute-start(bf16[128,1536]{1,0:T(8,128)(2,1)S(1)} %get-tuple-element.194), channel_id=1, source_target_pairs={{0,16},{16,0},{32,48},{48,32},{64,80},{80,64},{96,112},{112,96},{1... | collective-permute-start | bytes 1179656 | tf_op jit(solution)/shard_map/ppermute | solution.py:36
  173.6 10.1 %copy-start.49 = (bf16[768,768]{1,0:T(8,128)(2,1)S(1)}, bf16[768,768]{1,0:T(8,128)(2,1)}, u32[]{:S(2)}) copy-start(bf16[768,768]{1,0:T(8,128)(2,1)} %copy-done.47) | copy-start | bytes 3538948
  173.9 32.1 %collective-permute-start.13 = (bf16[448,1536]{1,0:T(8,128)(2,1)S(1)}, bf16[448,1536]{1,0:T(8,128)(2,1)S(1)}, u32[]{:S(2)}, u32[]{:S(2)}) collective-permute-start(bf16[448,1536]{1,0:T(8,128)(2,1)S(1)} %get-tuple-element.130), channel_id=1, source_target_pairs={{0,32},{16,48},{32,64},{48,80},{64,96},{80,112},{96,0},{112,16},{1... | collective-permute-start | bytes 4128776 | tf_op jit(solution)/shard_map/ppermute | solution.py:28
  174.0 32.0 %collective-permute-start.14 = (bf16[448,1536]{1,0:T(8,128)(2,1)S(1)}, bf16[448,1536]{1,0:T(8,128)(2,1)S(1)}, u32[]{:S(2)}, u32[]{:S(2)}) collective-permute-start(bf16[448,1536]{1,0:T(8,128)(2,1)S(1)} %get-tuple-element.131), channel_id=1, source_target_pairs={{0,96},{16,112},{32,0},{48,16},{64,32},{80,48},{96,64},{112,80},{1... | collective-permute-start | bytes 4128776 | tf_op jit(solution)/shard_map/ppermute | solution.py:32
  177.2 6.5 %copy-start.42 = (bf16[768,2048]{1,0:T(8,128)(2,1)S(1)}, bf16[768,2048]{1,0:T(8,128)(2,1)}, u32[]{:S(2)}) copy-start(bf16[768,2048]{1,0:T(8,128)(2,1)} %copy-done.40) | copy-start | bytes 9437188
  178.2 5.6 %copy-start.16 = (bf16[384,1536]{1,0:T(8,128)(2,1)S(1)}, bf16[384,1536]{1,0:T(8,128)(2,1)}, u32[]{:S(2)}) copy-start(bf16[384,1536]{1,0:T(8,128)(2,1)} %copy-done.14) | copy-start | bytes 3538948
  178.2 5.6 %copy-start.19 = (bf16[384,1536]{1,0:T(8,128)(2,1)S(1)}, bf16[384,1536]{1,0:T(8,128)(2,1)}, u32[]{:S(2)}) copy-start(bf16[384,1536]{1,0:T(8,128)(2,1)} %copy-done.17) | copy-start | bytes 3538948
  178.2 5.6 %copy-start.22 = (bf16[384,1536]{1,0:T(8,128)(2,1)S(1)}, bf16[384,1536]{1,0:T(8,128)(2,1)}, u32[]{:S(2)}) copy-start(bf16[384,1536]{1,0:T(8,128)(2,1)} %copy-done.20) | copy-start | bytes 3538948
  178.2 5.6 %copy-start.25 = (bf16[384,1536]{1,0:T(8,128)(2,1)S(1)}, bf16[384,1536]{1,0:T(8,128)(2,1)}, u32[]{:S(2)}) copy-start(bf16[384,1536]{1,0:T(8,128)(2,1)} %copy-done.23) | copy-start | bytes 3538948
  178.2 5.6 %copy-start.35 = (bf16[384,1536]{1,0:T(8,128)(2,1)S(1)}, bf16[384,1536]{1,0:T(8,128)(2,1)}, u32[]{:S(2)}) copy-start(bf16[384,1536]{1,0:T(8,128)(2,1)} %copy-done.33) | copy-start | bytes 3538948
  178.2 5.6 %copy-start.38 = (bf16[384,1536]{1,0:T(8,128)(2,1)S(1)}, bf16[384,1536]{1,0:T(8,128)(2,1)}, u32[]{:S(2)}) copy-start(bf16[384,1536]{1,0:T(8,128)(2,1)} %copy-done.36) | copy-start | bytes 3538948
  178.2 17.9 %collective-permute-start.15 = (bf16[256,1536]{1,0:T(8,128)(2,1)}, bf16[256,1536]{1,0:T(8,128)(2,1)S(1)}, u32[]{:S(2)}, u32[]{:S(2)}) collective-permute-start(bf16[256,1536]{1,0:T(8,128)(2,1)} %pad_maximum_fusion.2), channel_id=1, source_target_pairs={{0,16},{16,0},{32,48},{48,32},{64,80},{80,64},{96,112},{112,96},{1... | collective-permute-start | bytes 2359304 | tf_op jit(solution)/shard_map/ppermute | solution.py:36
  183.8 22.2 %copy-start.1 = (bf16[512,1536]{1,0:T(8,128)(2,1)}, bf16[512,1536]{1,0:T(8,128)(2,1)S(1)}, u32[]{:S(2)}) copy-start(bf16[512,1536]{1,0:T(8,128)(2,1)S(1)} %shard_map.188.own_ref) | copy-start | bytes 4718596
  194.1 13.9 %copy-start.13 = (bf16[768,2176]{1,0:T(8,128)(2,1)}, bf16[768,2176]{1,0:T(8,128)(2,1)S(1)}, u32[]{:S(2)}) copy-start(bf16[768,2176]{1,0:T(8,128)(2,1)S(1)} %shard_map.187) | copy-start | bytes 10027012
  208.0 27.1 %collective-permute-start.16 = (bf16[384,1536]{1,0:T(8,128)(2,1)}, bf16[384,1536]{1,0:T(8,128)(2,1)S(1)}, u32[]{:S(2)}, u32[]{:S(2)}) collective-permute-start(bf16[384,1536]{1,0:T(8,128)(2,1)} %get-tuple-element.137), channel_id=1, source_target_pairs={{0,32},{16,48},{32,64},{48,80},{64,96},{80,112},{96,0},{112,16},{1... | collective-permute-start | bytes 3538952 | tf_op jit(solution)/shard_map/ppermute | solution.py:28
  208.0 28.1 %collective-permute-start.17 = (bf16[384,1536]{1,0:T(8,128)(2,1)}, bf16[384,1536]{1,0:T(8,128)(2,1)}, u32[]{:S(2)}, u32[]{:S(2)}) collective-permute-start(bf16[384,1536]{1,0:T(8,128)(2,1)} %get-tuple-element.138), channel_id=1, source_target_pairs={{0,96},{16,112},{32,0},{48,16},{64,32},{80,48},{96,64},{112,80},{1... | collective-permute-start | bytes 3538952 | tf_op jit(solution)/shard_map/ppermute | solution.py:32
  211.2 25.6 %collective-permute-start.18 = (bf16[384,1536]{1,0:T(8,128)(2,1)}, bf16[384,1536]{1,0:T(8,128)(2,1)}, u32[]{:S(2)}, u32[]{:S(2)}) collective-permute-start(bf16[384,1536]{1,0:T(8,128)(2,1)} %get-tuple-element.139), channel_id=1, source_target_pairs={{0,16},{16,0},{32,48},{48,32},{64,80},{80,64},{96,112},{112,96},{1... | collective-permute-start | bytes 3538952 | tf_op jit(solution)/shard_map/ppermute | solution.py:36
  213.1 23.8 %copy-start.6 = (f32[1,96,2048]{2,1,0:T(8,128)S(1)}, f32[1,96,2048]{2,1,0:T(8,128)}, u32[]{:S(2)}) copy-start(f32[1,96,2048]{2,1,0:T(8,128)} %param.15) | copy-start | bytes 2359300
  213.1 23.8 %copy-start.7 = (f32[1,96,2048]{2,1,0:T(8,128)S(1)}, f32[1,96,2048]{2,1,0:T(8,128)}, u32[]{:S(2)}) copy-start(f32[1,96,2048]{2,1,0:T(8,128)} %param.17) | copy-start | bytes 2359300
  213.1 23.8 %copy-start.8 = (f32[1,96,2048]{2,1,0:T(8,128)S(1)}, f32[1,96,2048]{2,1,0:T(8,128)}, u32[]{:S(2)}) copy-start(f32[1,96,2048]{2,1,0:T(8,128)} %param.19) | copy-start | bytes 2359300
  213.1 44.8 %all-to-all-start.3 = ((bf16[8,96,2176]{2,1,0:T(8,128)(2,1)}), bf16[8,96,2176]{2,1,0:T(8,128)(2,1)}, u32[]{:S(2)}, u32[]{:S(2)}) async-start(bf16[8,96,2176]{2,1,0:T(8,128)(2,1)} %bitcast.72), calls=%async_computation.3 | async-start | bytes 6684672 | tf_op jit(solution)/shard_map/all_to_all | solution.py:62
  243.3 25.5 %collective-permute-start.19 = (bf16[384,1536]{1,0:T(8,128)(2,1)S(1)}, bf16[384,1536]{1,0:T(8,128)(2,1)}, u32[]{:S(2)}, u32[]{:S(2)}) collective-permute-start(bf16[384,1536]{1,0:T(8,128)(2,1)S(1)} %shard_map.190.refs_0_), channel_id=1, source_target_pairs={{0,32},{16,48},{32,64},{48,80},{64,96},{80,112},{96,0},{112,16},{1... | collective-permute-start | bytes 3538952 | tf_op jit(solution)/shard_map/ppermute | solution.py:28
  243.4 25.5 %collective-permute-start.20 = (bf16[384,1536]{1,0:T(8,128)(2,1)S(1)}, bf16[384,1536]{1,0:T(8,128)(2,1)}, u32[]{:S(2)}, u32[]{:S(2)}) collective-permute-start(bf16[384,1536]{1,0:T(8,128)(2,1)S(1)} %shard_map.190.refs_0_), channel_id=1, source_target_pairs={{0,96},{16,112},{32,0},{48,16},{64,32},{80,48},{96,64},{112,80},{1... | collective-permute-start | bytes 3538952 | tf_op jit(solution)/shard_map/ppermute | solution.py:32
  246.6 23.7 %collective-permute-start.21 = (bf16[384,1536]{1,0:T(8,128)(2,1)S(1)}, bf16[384,1536]{1,0:T(8,128)(2,1)}, u32[]{:S(2)}, u32[]{:S(2)}) collective-permute-start(bf16[384,1536]{1,0:T(8,128)(2,1)S(1)} %shard_map.190.refs_0_), channel_id=1, source_target_pairs={{0,16},{16,0},{32,48},{48,32},{64,80},{80,64},{96,112},{112,96},{1... | collective-permute-start | bytes 3538952 | tf_op jit(solution)/shard_map/ppermute | solution.py:36
  249.6 1.9 copy-start.53
  249.7 2.7 copy-start.2
  249.7 3.1 copy-start.51
  249.7 3.6 %copy-start.52 = (f32[1,256,1536]{2,1,0:T(8,128)S(1)}, f32[1,256,1536]{2,1,0:T(8,128)}, u32[]{:S(2)}) copy-start(f32[1,256,1536]{2,1,0:T(8,128)} %param.16) | copy-start | bytes 4718596
  253.3 4.6 %copy-start.31 = (f32[8,256]{1,0:T(8,128)S(1)}, f32[8,256]{1,0:T(8,128)}, u32[]{:S(2)}) copy-start(f32[8,256]{1,0:T(8,128)} %copy-done.30) | copy-start | bytes 24580
  270.3 26.2 %collective-permute-start.22 = (bf16[384,1536]{1,0:T(8,128)(2,1)}, bf16[384,1536]{1,0:T(8,128)(2,1)S(1)}, u32[]{:S(2)}, u32[]{:S(2)}) collective-permute-start(bf16[384,1536]{1,0:T(8,128)(2,1)} %collective-permute-done.21.refs_1_), channel_id=1, source_target_pairs={{0,32},{16,48},{32,64},{48,80},{64,96},{80,112},{96,0},{112,16},{1... | collective-permute-start | bytes 3538952 | tf_op jit(solution)/shard_map/ppermute | solution.py:28
  270.3 26.2 %collective-permute-start.23 = (bf16[384,1536]{1,0:T(8,128)(2,1)}, bf16[384,1536]{1,0:T(8,128)(2,1)S(1)}, u32[]{:S(2)}, u32[]{:S(2)}) collective-permute-start(bf16[384,1536]{1,0:T(8,128)(2,1)} %collective-permute-done.21.refs_1_), channel_id=1, source_target_pairs={{0,96},{16,112},{32,0},{48,16},{64,32},{80,48},{96,64},{112,80},{1... | collective-permute-start | bytes 3538952 | tf_op jit(solution)/shard_map/ppermute | solution.py:32
  273.5 23.0 %collective-permute-start.24 = (bf16[256,2176]{1,0:T(8,128)(2,1)S(1)}, bf16[256,2176]{1,0:T(8,128)(2,1)S(1)}, u32[]{:S(2)}, u32[]{:S(2)}) collective-permute-start(bf16[256,2176]{1,0:T(8,128)(2,1)S(1)} %get-tuple-element.148), channel_id=1, source_target_pairs={{0,2},{1,3},{2,0},{3,1},{4,6},{5,7},{6,4},{7,5},{8,10},{9,11},{10,... | collective-permute-start | bytes 3342344 | tf_op jit(solution)/shard_map/ppermute | solution.py:58
  299.2 23.4 %collective-permute-start.25 = (bf16[384,1536]{1,0:T(8,128)(2,1)}, bf16[384,1536]{1,0:T(8,128)(2,1)S(1)}, u32[]{:S(2)}, u32[]{:S(2)}) collective-permute-start(bf16[384,1536]{1,0:T(8,128)(2,1)} %get-tuple-element.153), channel_id=1, source_target_pairs={{0,32},{16,48},{32,64},{48,80},{64,96},{80,112},{96,0},{112,16},{1... | collective-permute-start | bytes 3538952 | tf_op jit(solution)/shard_map/ppermute | solution.py:28
  299.3 23.3 %collective-permute-start.26 = (bf16[384,1536]{1,0:T(8,128)(2,1)}, bf16[384,1536]{1,0:T(8,128)(2,1)}, u32[]{:S(2)}, u32[]{:S(2)}) collective-permute-start(bf16[384,1536]{1,0:T(8,128)(2,1)} %get-tuple-element.154), channel_id=1, source_target_pairs={{0,96},{16,112},{32,0},{48,16},{64,32},{80,48},{96,64},{112,80},{1... | collective-permute-start | bytes 3538952 | tf_op jit(solution)/shard_map/ppermute | solution.py:32
  (22 other events, 24.7 us)

commit v5 on v4

--- a/solution.py
+++ b/solution.py
@@ -489,7 +489,7 @@
         cost_estimate=pl.CostEstimate(
             flops=20_000_000, bytes_accessed=12_000_000, transcendentals=1_000_000
         ),
-        compiler_params=pltpu.CompilerParams(vmem_limit_bytes=48 << 20),
+        compiler_params=pltpu.CompilerParams(vmem_limit_bytes=24 << 20),
     )(own_plane, parts, t_up, t_down, t_y, w_gu, m_gu, s_gu, w_dn, m_dn, s_dn, w_dn, m_dn, s_dn)
 
 

time: 332 us -> 340 us (1.024)
  local copies, waits for them, and re-layouts: 33.9 us -> 40.6 us
    unnamed x111 -> x115, local copies, waits for them, and re-layouts: 33.6 us -> 40.2 us
  transfers between devices with their start and end apart: 31 -> 31, of which waited for: 14 -> 14; matrix products, arithmetic and copies ran while one was open for 3% -> 3% of each run, Pallas kernels for 17% -> 16%
where the time goes in v5:
time: 340 us; the launch traced here: 334 us
  waiting for transfers between devices  140 us (41%)
  starting transfers between devices  71.6 us (21%)
  Pallas kernels  69.3 us (20%)
  local copies, waits for them, and re-layouts  40.6 us (12%)
  other arithmetic  10.5 us (3%)
    ppermute x9, waiting for transfers between devices, z_up(): return lax.ppermute(a, 'dp', Z_UP)  64.8 us
    ppermute x4, waiting for transfers between devices, yh_swap(): return lax.ppermute(a, 'expert', YH_SWAP)  61 us
    pallas_call x14, Pallas kernels, call(): pl.pallas_call(kernel, out_shape=outs, in_specs=[smem] * scalars + [vmem]...  48.9 us
    unnamed x115, local copies, waits for them, and re-layouts  40.2 us
    ppermute x9, starting transfers between devices, z_down(): return lax.ppermute(a, 'dp', Z_DOWN)  26.8 us
    all_to_all x4, starting transfers between devices, exchange(): lax.all_to_all(rows.reshape(8, rows.shape[0] // 8, rows.shape[1]), 'exper...  22.8 us
    ppermute x5, waiting for transfers between devices, y_swap(): return lax.ppermute(a, 'dp', Y_SWAP)  10.9 us
    ppermute x4, starting transfers between devices, yh_swap(): return lax.ppermute(a, 'expert', YH_SWAP)  9.86 us
  transfers between devices with their start and end apart: 31, of which 14 were waited for; matrix products, arithmetic and copies ran while one was open for 3% of the time, Pallas kernels for 16%

profile of v5, /device:TPU:4, one launch (start us, length us, event | category | flops | bytes accessed | tf_op | source)
XLA Modules:
  0.0 333.7 jit_solution(3709658504893829116)
XLA Ops:
  0.7 1.3 bitcast_convert_fusion
  2.6 2.0 collective-permute-start
  4.5 2.2 collective-permute-start.1
  6.7 1.6 collective-permute-start.2
  11.6 1.6 shard_map.178
  13.2 1.7 copy-done.8
  14.9 17.7 %collective-permute-done.below_ref.refs_2_ = bf16[384,1536]{1,0:T(8,128)(2,1)S(1)} collective-permute-done((bf16[384,1536]{1,0:T(8,128)(2,1)S(1)}, bf16[384,1536]{1,0:T(8,128)(2,1)S(1)}, u32[]{:S(2)}, u32[]{:S(2)}) %collective-permute-start) | collective-permute-done | bytes 1179680 | tf_op jit(solution)/shard_map/ppermute | solution.py:28
  32.6 1.6 collective-permute-done.2.refs_1_
  34.3 4.8 %all-to-all-start = ((bf16[8,48,4224]{2,1,0:T(8,128)(2,1)}), bf16[8,48,4224]{2,1,0:T(8,128)(2,1)S(1)}, u32[]{:S(2)}, u32[]{:S(2)}) async-start(bf16[8,48,4224]{2,1,0:T(8,128)(2,1)} %bitcast.64), calls=%async_computation | async-start | bytes 6488064 | tf_op jit(solution)/shard_map/all_to_all | solution.py:62
  39.7 2.6 collective-permute-start.4
  42.3 3.2 collective-permute-start.6
  45.9 23.0 %collective-permute-done.5.aux_ref.far_aux_ref = f32[8,256]{1,0:T(8,128)S(1)} collective-permute-done((f32[8,256]{1,0:T(8,128)}, f32[8,256]{1,0:T(8,128)S(1)}, u32[]{:S(2)}, u32[]{:S(2)}) %collective-permute-start.5) | collective-permute-done | bytes 8224 | tf_op jit(solution)/shard_map/ppermute | solution.py:58
  72.2 3.2 all-to-all-done
  75.4 7.4 %all-to-all-start.1 = ((bf16[8,48,2048]{2,1,0:T(8,128)(2,1)}), bf16[8,48,2048]{2,1,0:T(8,128)(2,1)}, u32[]{:S(2)}, u32[]{:S(2)}) async-start(bf16[8,48,2048]{2,1,0:T(8,128)(2,1)} %bitcast.74), calls=%async_computation.1 | async-start | bytes 3145728 | tf_op jit(solution)/shard_map/all_to_all | solution.py:62
  82.8 3.1 shard_map.180
  86.6 2.6 collective-permute-start.8
  89.2 3.2 collective-permute-start.9
  92.4 23.0 %collective-permute-done.9.grad_ref = bf16[256,2048]{1,0:T(8,128)(2,1)S(1)} collective-permute-done((bf16[256,2048]{1,0:T(8,128)(2,1)S(1)}, bf16[256,2048]{1,0:T(8,128)(2,1)S(1)}, u32[]{:S(2)}, u32[]{:S(2)}) %collective-permute-start.9) | collective-permute-done | bytes 1048608 | tf_op jit(solution)/shard_map/ppermute | solution.py:58
  119.4 5.0 %all-to-all-start.2 = ((bf16[8,48,2176]{2,1,0:T(8,128)(2,1)}), bf16[8,48,2176]{2,1,0:T(8,128)(2,1)}, u32[]{:S(2)}, u32[]{:S(2)}) async-start(bf16[8,48,2176]{2,1,0:T(8,128)(2,1)} %bitcast.71), calls=%async_computation.2 | async-start | bytes 3342336 | tf_op jit(solution)/shard_map/all_to_all | solution.py:62
  132.0 8.0 %shard_map.182 = (bf16[768,768]{1,0:T(8,128)(2,1)S(1)}, bf16[768,768]{1,0:T(8,128)(2,1)S(1)}, bf16[768,768]{1,0:T(8,128)(2,1)S(1)}, bf16[768,2048]{1,0:T(8,128)(2,1)S(1)}) custom-call(s32[8]{0:T(128)S(1)} %stack.35.column_ref, bf16[384,4224]{1,0:T(8,128)(2,1)S(1)} %bitcast.59, bf16[384,2048]{1,0:T(8,128)(2,1)} %bitcast.16.far_ref.far_in_ref, ...), custom_call_target="tpu_custom_call" | custom-call | flops 4800000000 | bytes 20938784 | tf_op jit(solution)/shard_map/pallas_call | solution.py:515
  140.1 1.7 copy-done.46
  144.8 1.9 copy-done.47
  149.2 6.6 %shard_map.183 = (bf16[768,1536]{1,0:T(8,128)(2,1)S(1)}, bf16[512,1536]{1,0:T(8,128)(2,1)S(1)}, bf16[768,2048]{1,0:T(8,128)(2,1)S(1)}) custom-call(bf16[384,4224]{1,0:T(8,128)(2,1)S(1)} %bitcast.60, bf16[384,2048]{1,0:T(8,128)(2,1)} %bitcast.16.far_ref.far_in_ref, bf16[384,2176]{1,0:T(8,128)(2,1)} %bitcast.18.far_grad_ref, bf16[768,768]{1,0:T(8,128)(2,1)S(1)} %copy-done.50, ...), custom_call_target="tpu_custom_call" | custom-call | flops 3600000000 | bytes 19070976 | tf_op jit(solution)/shard_map/pallas_call | solution.py:515
  156.0 3.2 collective-permute-start.11
  159.2 3.4 %shard_map.184.parts_ref = bf16[8,128,1536]{2,1,0:T(8,128)(2,1)S(1)} custom-call(s32[8]{0:T(128)S(1)} %stack.35.column_ref, bf16[768,768]{1,0:T(8,128)(2,1)S(1)} %copy-done.54, bf16[768,2048]{1,0:T(8,128)(2,1)S(1)} %get-tuple-element.121.scaled_ref), custom_call_target="tpu_custom_call" | custom-call | flops 2400000000 | bytes 7471136 | tf_op jit(solution)/shard_map/pallas_call | solution.py:515
  162.7 1.9 collective-permute-start.12
  164.6 4.8 %shard_map.185 = (bf16[512,1536]{1,0:T(8,128)(2,1)S(1)}, bf16[512,1536]{1,0:T(8,128)(2,1)S(1)}) custom-call(bf16[384,4224]{1,0:T(8,128)(2,1)S(1)} %bitcast.61, bf16[384,2048]{1,0:T(8,128)(2,1)} %bitcast.16.far_ref.far_in_ref, bf16[768,1536]{1,0:T(8,128)(2,1)S(1)} %get-tuple-element.132.proj_ref), custom_call_target="tpu_custom_call" | custom-call | flops 2400000000 | bytes 10321920 | tf_op jit(solution)/shard_map/pallas_call | solution.py:515
  169.5 4.2 %collective-permute-done.12.y_ref = bf16[128,1536]{1,0:T(8,128)(2,1)S(1)} collective-permute-done((bf16[128,1536]{1,0:T(8,128)(2,1)S(1)}, bf16[128,1536]{1,0:T(8,128)(2,1)S(1)}, u32[]{:S(2)}, u32[]{:S(2)}) %collective-permute-start.12) | collective-permute-done | bytes 393248 | tf_op jit(solution)/shard_map/ppermute | solution.py:36
  174.0 3.2 collective-permute-start.14
  178.2 1.7 collective-permute-start.15
  179.9 3.9 %shard_map.188.own_ref = bf16[512,1536]{1,0:T(8,128)(2,1)S(1)} custom-call(bf16[384,4224]{1,0:T(8,128)(2,1)S(1)} %bitcast.62, bf16[384,2048]{1,0:T(8,128)(2,1)} %bitcast.16.far_ref.far_in_ref, bf16[768,1536]{1,0:T(8,128)(2,1)S(1)} %get-tuple-element.132.proj_ref), custom_call_target="tpu_custom_call" | custom-call | flops 1200000000 | bytes 8749056 | tf_op jit(solution)/shard_map/pallas_call | solution.py:515
  183.8 10.3 %shard_map.187 = bf16[768,2176]{1,0:T(8,128)(2,1)S(1)} custom-call(bf16[384,4224]{1,0:T(8,128)(2,1)S(1)} %bitcast.63, bf16[384,2176]{1,0:T(8,128)(2,1)} %bitcast.18.far_grad_ref, bf16[768,768]{1,0:T(8,128)(2,1)S(1)} %copy-done.55, bf16[768,1536]{1,0:T(8,128)(2,1)S(1)} %get-tuple-element.132.proj_ref, bf16[768,2048]{1,0:T(8,128)(2,1)S(1)} %copy-done.48, ...), custom_call_target="tpu_custom_call" | custom-call | flops 7200000000 | bytes 24379392 | tf_op jit(solution)/shard_map/pallas_call | solution.py:515
  194.2 1.9 collective-permute-done.15.y_ref
  196.1 9.9 %collective-permute-done.13.up_ref = bf16[448,1536]{1,0:T(8,128)(2,1)S(1)} collective-permute-done((bf16[448,1536]{1,0:T(8,128)(2,1)S(1)}, bf16[448,1536]{1,0:T(8,128)(2,1)S(1)}, u32[]{:S(2)}, u32[]{:S(2)}) %collective-permute-start.13) | collective-permute-done | bytes 1376288 | tf_op jit(solution)/shard_map/ppermute | solution.py:28
  206.0 2.0 shard_map.189
  208.0 3.2 collective-permute-start.17
  211.3 1.8 collective-permute-start.18
  213.1 5.6 %all-to-all-start.3 = ((bf16[8,96,2176]{2,1,0:T(8,128)(2,1)}), bf16[8,96,2176]{2,1,0:T(8,128)(2,1)}, u32[]{:S(2)}, u32[]{:S(2)}) async-start(bf16[8,96,2176]{2,1,0:T(8,128)(2,1)} %bitcast.75), calls=%async_computation.3 | async-start | bytes 6684672 | tf_op jit(solution)/shard_map/all_to_all | solution.py:62
  218.7 16.5 %collective-permute-done.16.up_ref = bf16[384,1536]{1,0:T(8,128)(2,1)} collective-permute-done((bf16[384,1536]{1,0:T(8,128)(2,1)}, bf16[384,1536]{1,0:T(8,128)(2,1)}, u32[]{:S(2)}, u32[]{:S(2)}) %collective-permute-start.16) | collective-permute-done | bytes 1179680 | tf_op jit(solution)/shard_map/ppermute | solution.py:28
  235.2 1.7 collective-permute-done.18.y_ref
  236.9 1.4 copy-done.1
  238.3 1.4 copy-done.4
  243.1 1.4 copy-done.16
  244.5 1.4 copy-done.18
  245.9 5.1 %shard_map.190.refs_0_ = bf16[384,1536]{1,0:T(8,128)(2,1)} custom-call(bf16[512,1536]{1,0:T(8,128)(2,1)S(1)} %copy-done.1, bf16[8,128,1536]{2,1,0:T(8,128)(2,1)S(1)} %shard_map.184.parts_ref, bf16[384,1536]{1,0:T(8,128)(2,1)} %collective-permute-done.16.up_ref, bf16[384,1536]{1,0:T(8,128)(2,1)} %collective-permute-done.17.down_ref, ...), custom_call_target="tpu_custom_call" | custom-call | flops 20000000 | bytes 12000000 | tf_op jit(solution)/shard_map/pallas_call | solution.py:483
  251.1 3.2 collective-permute-start.20
  254.3 1.6 collective-permute-start.21
  255.9 1.4 fusion.6
  257.5 1.8 multiply_subtract_fusion.1
  261.0 4.9 %multiply_subtract_fusion = (f32[256,1536]{1,0:T(8,128)}, f32[256,1536]{1,0:T(8,128)}, f32[256,1536]{1,0:T(8,128)}) fusion(f32[1,256,1536]{2,1,0:T(8,128)S(1)} %copy-done.5, bf16[384,1536]{1,0:T(8,128)(2,1)} %collective-permute-done.18.y_ref, bf16[384,1536]{1,0:T(8,128)(2,1)} %collective-permute-done.17.down_ref, ...), kind=kLoop, calls=%fused_computation.4 | loop fusion | flops 8650752 | bytes 12582912 | tf_op jit(solution)/shard_map/sub | solution.py:43
  265.9 4.4 %shard_map.191 = (f32[256,2176]{1,0:T(8,128)S(1)}, bf16[256,2176]{1,0:T(8,128)(2,1)S(1)}) custom-call(f32[8,256]{1,0:T(8,128)S(1)} %get-tuple-element.94.aux_ref.near_aux_ref, f32[8,256]{1,0:T(8,128)S(1)} %collective-permute-done.5.aux_ref.far_aux_ref, bf16[768,2176]{1,0:T(8,128)(2,1)} %bitcast.27.rows_ref), custom_call_target="tpu_custom_call" | custom-call | flops 1700000000 | bytes 6701056 | tf_op jit(solution)/shard_map/pallas_call | solution.py:515
  270.3 6.4 %collective-permute-done.19.refs_3_.below_ref = bf16[384,1536]{1,0:T(8,128)(2,1)} collective-permute-done((bf16[384,1536]{1,0:T(8,128)(2,1)}, bf16[384,1536]{1,0:T(8,128)(2,1)}, u32[]{:S(2)}, u32[]{:S(2)}) %collective-permute-start.19) | collective-permute-done | bytes 1179680 | tf_op jit(solution)/shard_map/ppermute | solution.py:28
  276.8 1.5 collective-permute-done.21.refs_1_
  278.2 3.2 collective-permute-start.23
  281.5 3.1 collective-permute-start.24
  284.6 4.7 %shard_map.192 = (bf16[2048,1536]{1,0:T(8,128)(2,1)}, bf16[768,2048]{1,0:T(8,128)(2,1)}) custom-call(s32[8]{0:T(128)S(1)} %stack.35.column_ref, bf16[384,1536]{1,0:T(8,128)(2,1)} %shard_map.190.refs_0_, bf16[384,1536]{1,0:T(8,128)(2,1)} %collective-permute-done.21.refs_1_, bf16[384,1536]{1,0:T(8,128)(2,1)} %collective-permute-done.20.refs_2_.above_ref, ...), custom_call_target="tpu_custom_call" | custom-call | bytes 9600000 | tf_op jit(solution)/shard_map/pallas_call | solution.py:420
  289.3 15.0 %collective-permute-done.24.far_ref = bf16[256,2176]{1,0:T(8,128)(2,1)S(1)} collective-permute-done((bf16[256,2176]{1,0:T(8,128)(2,1)S(1)}, bf16[256,2176]{1,0:T(8,128)(2,1)S(1)}, u32[]{:S(2)}, u32[]{:S(2)}) %collective-permute-start.24) | collective-permute-done | bytes 1114144 | tf_op jit(solution)/shard_map/ppermute | solution.py:58
  304.4 2.7 shard_map.193
  307.1 3.2 collective-permute-start.26
  310.4 1.7 shard_map.195
  312.7 1.5 copy.24
  314.1 2.0 shard_map.194
  316.2 14.2 %collective-permute-done.25.refs_0_ = bf16[384,1536]{1,0:T(8,128)(2,1)S(1)} collective-permute-done((bf16[384,1536]{1,0:T(8,128)(2,1)}, bf16[384,1536]{1,0:T(8,128)(2,1)S(1)}, u32[]{:S(2)}, u32[]{:S(2)}) %collective-permute-start.25) | collective-permute-done | bytes 1179680 | tf_op jit(solution)/shard_map/ppermute | solution.py:28
  330.5 2.8 shard_map.196
  (150 shorter events, 33.7 us)
Async XLA Ops:
  0.6 1.6 copy-start.3
  2.4 5.9 %copy-start.56 = (bf16[256,2]{0,1:T(2,128)(2,1)S(1)}, bf16[256,2]{0,1:T(2,128)(2,1)}, u32[]{:S(2)}) copy-start(bf16[256,2]{0,1:T(2,128)(2,1)} %param.13) | copy-start | bytes 3076
  2.4 5.9 %copy-start.38 = (s32[256,2]{0,1:T(2,128)S(1)}, s32[256,2]{0,1:T(2,128)}, u32[]{:S(2)}) copy-start(s32[256,2]{0,1:T(2,128)} %param.12) | copy-start | bytes 6148
  2.5 10.7 %copy-start.22 = (bf16[384,1536]{1,0:T(8,128)(2,1)}, bf16[384,1536]{1,0:T(8,128)(2,1)S(1)}, u32[]{:S(2)}) copy-start(bf16[384,1536]{1,0:T(8,128)(2,1)S(1)} %fusion.3.refs_0_) | copy-start | bytes 3538948
  2.6 30.1 %collective-permute-start = (bf16[384,1536]{1,0:T(8,128)(2,1)S(1)}, bf16[384,1536]{1,0:T(8,128)(2,1)S(1)}, u32[]{:S(2)}, u32[]{:S(2)}) collective-permute-start(bf16[384,1536]{1,0:T(8,128)(2,1)S(1)} %fusion.3.refs_0_), channel_id=1, source_target_pairs={{0,32},{16,48},{32,64},{48,80},{64,96},{80,112},{96,0},{112,16},{1... | collective-permute-start | bytes 3538952 | tf_op jit(solution)/shard_map/ppermute | solution.py:28
  4.5 28.1 %collective-permute-start.1 = (bf16[384,1536]{1,0:T(8,128)(2,1)S(1)}, bf16[384,1536]{1,0:T(8,128)(2,1)S(1)}, u32[]{:S(2)}, u32[]{:S(2)}) collective-permute-start(bf16[384,1536]{1,0:T(8,128)(2,1)S(1)} %fusion.3.refs_0_), channel_id=1, source_target_pairs={{0,96},{16,112},{32,0},{48,16},{64,32},{80,48},{96,64},{112,80},{1... | collective-permute-start | bytes 3538952 | tf_op jit(solution)/shard_map/ppermute | solution.py:32
  6.7 27.5 %collective-permute-start.2 = (bf16[384,1536]{1,0:T(8,128)(2,1)S(1)}, bf16[384,1536]{1,0:T(8,128)(2,1)}, u32[]{:S(2)}, u32[]{:S(2)}) collective-permute-start(bf16[384,1536]{1,0:T(8,128)(2,1)S(1)} %fusion.3.refs_0_), channel_id=1, source_target_pairs={{0,16},{16,0},{32,48},{48,32},{64,80},{80,64},{96,112},{112,96},{1... | collective-permute-start | bytes 3538952 | tf_op jit(solution)/shard_map/ppermute | solution.py:36
  13.2 1.7 copy-start.8
  32.6 1.6 copy-start.25
  32.6 1.6 copy-start.28
  34.3 41.1 %all-to-all-start = ((bf16[8,48,4224]{2,1,0:T(8,128)(2,1)}), bf16[8,48,4224]{2,1,0:T(8,128)(2,1)S(1)}, u32[]{:S(2)}, u32[]{:S(2)}) async-start(bf16[8,48,4224]{2,1,0:T(8,128)(2,1)} %bitcast.64), calls=%async_computation | async-start | bytes 6488064 | tf_op jit(solution)/shard_map/all_to_all | solution.py:62
  39.1 29.8 %collective-permute-start.3 = (bf16[384,1536]{1,0:T(8,128)(2,1)}, bf16[384,1536]{1,0:T(8,128)(2,1)S(1)}, u32[]{:S(2)}, u32[]{:S(2)}) collective-permute-start(bf16[384,1536]{1,0:T(8,128)(2,1)} %collective-permute-done.2.refs_1_), channel_id=1, source_target_pairs={{0,32},{16,48},{32,64},{48,80},{64,96},{80,112},{96,0},{112,16},{1... | collective-permute-start | bytes 3538952 | tf_op jit(solution)/shard_map/ppermute | solution.py:28
  39.7 30.2 %collective-permute-start.4 = (bf16[384,1536]{1,0:T(8,128)(2,1)}, bf16[384,1536]{1,0:T(8,128)(2,1)}, u32[]{:S(2)}, u32[]{:S(2)}) collective-permute-start(bf16[384,1536]{1,0:T(8,128)(2,1)} %collective-permute-done.2.refs_1_), channel_id=1, source_target_pairs={{0,96},{16,112},{32,0},{48,16},{64,32},{80,48},{96,64},{112,80},{1... | collective-permute-start | bytes 3538952 | tf_op jit(solution)/shard_map/ppermute | solution.py:32
  42.3 26.5 %collective-permute-start.6 = (bf16[256,2048]{1,0:T(8,128)(2,1)}, bf16[256,2048]{1,0:T(8,128)(2,1)S(1)}, u32[]{:S(2)}, u32[]{:S(2)}) collective-permute-start(bf16[256,2048]{1,0:T(8,128)(2,1)} %tok_ref.1), channel_id=1, source_target_pairs={{0,2},{1,3},{2,0},{3,1},{4,6},{5,7},{6,4},{7,5},{8,10},{9,11},{10,... | collective-permute-start | bytes 3145736 | tf_op jit(solution)/shard_map/ppermute | solution.py:58
  45.5 23.3 %collective-permute-start.5 = (f32[8,256]{1,0:T(8,128)}, f32[8,256]{1,0:T(8,128)S(1)}, u32[]{:S(2)}, u32[]{:S(2)}) collective-permute-start(f32[8,256]{1,0:T(8,128)} %copy-done.45), channel_id=1, source_target_pairs={{0,2},{1,3},{2,0},{3,1},{4,6},{5,7},{6,4},{7,5},{8,10},{9,11},{10,... | collective-permute-start | bytes 24584 | tf_op jit(solution)/shard_map/ppermute | solution.py:58
  75.4 69.4 %copy-start.6 = (bf16[8,48,4224]{2,1,0:T(8,128)(2,1)}, bf16[8,48,4224]{2,1,0:T(8,128)(2,1)S(1)}, u32[]{:S(2)}) copy-start(bf16[8,48,4224]{2,1,0:T(8,128)(2,1)S(1)} %all-to-all-done) | copy-start | bytes 9732100
  75.4 43.9 %all-to-all-start.1 = ((bf16[8,48,2048]{2,1,0:T(8,128)(2,1)}), bf16[8,48,2048]{2,1,0:T(8,128)(2,1)}, u32[]{:S(2)}, u32[]{:S(2)}) async-start(bf16[8,48,2048]{2,1,0:T(8,128)(2,1)} %bitcast.74), calls=%async_computation.1 | async-start | bytes 3145728 | tf_op jit(solution)/shard_map/all_to_all | solution.py:62
  82.8 6.4 %copy-start.36 = (bf16[256,2048]{1,0:T(8,128)(2,1)S(1)}, bf16[256,2048]{1,0:T(8,128)(2,1)}, u32[]{:S(2)}) copy-start(bf16[256,2048]{1,0:T(8,128)(2,1)} %grad_ref.1) | copy-start | bytes 3145732
  85.9 29.5 %collective-permute-start.7 = (bf16[384,1536]{1,0:T(8,128)(2,1)}, bf16[384,1536]{1,0:T(8,128)(2,1)S(1)}, u32[]{:S(2)}, u32[]{:S(2)}) collective-permute-start(bf16[384,1536]{1,0:T(8,128)(2,1)} %get-tuple-element.107), channel_id=1, source_target_pairs={{0,32},{16,48},{32,64},{48,80},{64,96},{80,112},{96,0},{112,16},{1... | collective-permute-start | bytes 3538952 | tf_op jit(solution)/shard_map/ppermute | solution.py:28
  86.6 29.8 %collective-permute-start.8 = (bf16[384,1536]{1,0:T(8,128)(2,1)}, bf16[384,1536]{1,0:T(8,128)(2,1)S(1)}, u32[]{:S(2)}, u32[]{:S(2)}) collective-permute-start(bf16[384,1536]{1,0:T(8,128)(2,1)} %get-tuple-element.108), channel_id=1, source_target_pairs={{0,96},{16,112},{32,0},{48,16},{64,32},{80,48},{96,64},{112,80},{1... | collective-permute-start | bytes 3538952 | tf_op jit(solution)/shard_map/ppermute | solution.py:32
  89.2 26.2 %collective-permute-start.9 = (bf16[256,2048]{1,0:T(8,128)(2,1)S(1)}, bf16[256,2048]{1,0:T(8,128)(2,1)S(1)}, u32[]{:S(2)}, u32[]{:S(2)}) collective-permute-start(bf16[256,2048]{1,0:T(8,128)(2,1)S(1)} %copy-done.36), channel_id=1, source_target_pairs={{0,2},{1,3},{2,0},{3,1},{4,6},{5,7},{6,4},{7,5},{8,10},{9,11},{10,... | collective-permute-start | bytes 3145736 | tf_op jit(solution)/shard_map/ppermute | solution.py:58
  119.4 25.4 %all-to-all-start.2 = ((bf16[8,48,2176]{2,1,0:T(8,128)(2,1)}), bf16[8,48,2176]{2,1,0:T(8,128)(2,1)}, u32[]{:S(2)}, u32[]{:S(2)}) async-start(bf16[8,48,2176]{2,1,0:T(8,128)(2,1)} %bitcast.71), calls=%async_computation.2 | async-start | bytes 3342336 | tf_op jit(solution)/shard_map/all_to_all | solution.py:62
  140.1 1.7 copy-start.46
  144.8 1.9 copy-start.47
  155.8 3.4 %copy-start.54 = (bf16[768,768]{1,0:T(8,128)(2,1)S(1)}, bf16[768,768]{1,0:T(8,128)(2,1)}, u32[]{:S(2)}) copy-start(bf16[768,768]{1,0:T(8,128)(2,1)} %copy-done.53) | copy-start | bytes 3538948
  155.9 13.5 %collective-permute-start.10 = (bf16[128,1536]{1,0:T(8,128)(2,1)S(1)}, bf16[128,1536]{1,0:T(8,128)(2,1)S(1)}, u32[]{:S(2)}, u32[]{:S(2)}) collective-permute-start(bf16[128,1536]{1,0:T(8,128)(2,1)S(1)} %get-tuple-element.196), channel_id=1, source_target_pairs={{0,32},{16,48},{32,64},{48,80},{64,96},{80,112},{96,0},{112,16},{1... | collective-permute-start | bytes 1179656 | tf_op jit(solution)/shard_map/ppermute | solution.py:28
  156.0 13.5 %collective-permute-start.11 = (bf16[128,1536]{1,0:T(8,128)(2,1)S(1)}, bf16[128,1536]{1,0:T(8,128)(2,1)S(1)}, u32[]{:S(2)}, u32[]{:S(2)}) collective-permute-start(bf16[128,1536]{1,0:T(8,128)(2,1)S(1)} %get-tuple-element.195), channel_id=1, source_target_pairs={{0,96},{16,112},{32,0},{48,16},{64,32},{80,48},{96,64},{112,80},{1... | collective-permute-start | bytes 1179656 | tf_op jit(solution)/shard_map/ppermute | solution.py:32
  159.2 5.4 %copy-start.7 = (bf16[8,48,4224]{2,1,0:T(8,128)(2,1)S(1)}, bf16[8,48,4224]{2,1,0:T(8,128)(2,1)}, u32[]{:S(2)}) copy-start(bf16[8,48,4224]{2,1,0:T(8,128)(2,1)} %copy-done.6) | copy-start | bytes 9732100
  162.7 10.9 %collective-permute-start.12 = (bf16[128,1536]{1,0:T(8,128)(2,1)S(1)}, bf16[128,1536]{1,0:T(8,128)(2,1)S(1)}, u32[]{:S(2)}, u32[]{:S(2)}) collective-permute-start(bf16[128,1536]{1,0:T(8,128)(2,1)S(1)} %get-tuple-element.194), channel_id=1, source_target_pairs={{0,16},{16,0},{32,48},{48,32},{64,80},{80,64},{96,112},{112,96},{1... | collective-permute-start | bytes 1179656 | tf_op jit(solution)/shard_map/ppermute | solution.py:36
  173.6 10.1 %copy-start.55 = (bf16[768,768]{1,0:T(8,128)(2,1)S(1)}, bf16[768,768]{1,0:T(8,128)(2,1)}, u32[]{:S(2)}) copy-start(bf16[768,768]{1,0:T(8,128)(2,1)} %copy-done.53) | copy-start | bytes 3538948
  173.9 32.0 %collective-permute-start.13 = (bf16[448,1536]{1,0:T(8,128)(2,1)S(1)}, bf16[448,1536]{1,0:T(8,128)(2,1)S(1)}, u32[]{:S(2)}, u32[]{:S(2)}) collective-permute-start(bf16[448,1536]{1,0:T(8,128)(2,1)S(1)} %get-tuple-element.130), channel_id=1, source_target_pairs={{0,32},{16,48},{32,64},{48,80},{64,96},{80,112},{96,0},{112,16},{1... | collective-permute-start | bytes 4128776 | tf_op jit(solution)/shard_map/ppermute | solution.py:28
  174.0 32.0 %collective-permute-start.14 = (bf16[448,1536]{1,0:T(8,128)(2,1)S(1)}, bf16[448,1536]{1,0:T(8,128)(2,1)S(1)}, u32[]{:S(2)}, u32[]{:S(2)}) collective-permute-start(bf16[448,1536]{1,0:T(8,128)(2,1)S(1)} %get-tuple-element.131), channel_id=1, source_target_pairs={{0,96},{16,112},{32,0},{48,16},{64,32},{80,48},{96,64},{112,80},{1... | collective-permute-start | bytes 4128776 | tf_op jit(solution)/shard_map/ppermute | solution.py:32
  177.3 6.5 %copy-start.48 = (bf16[768,2048]{1,0:T(8,128)(2,1)S(1)}, bf16[768,2048]{1,0:T(8,128)(2,1)}, u32[]{:S(2)}) copy-start(bf16[768,2048]{1,0:T(8,128)(2,1)} %copy-done.46) | copy-start | bytes 9437188
  178.2 5.6 %copy-start.24 = (bf16[384,1536]{1,0:T(8,128)(2,1)S(1)}, bf16[384,1536]{1,0:T(8,128)(2,1)}, u32[]{:S(2)}) copy-start(bf16[384,1536]{1,0:T(8,128)(2,1)} %copy-done.22) | copy-start | bytes 3538948
  178.2 5.6 %copy-start.27 = (bf16[384,1536]{1,0:T(8,128)(2,1)S(1)}, bf16[384,1536]{1,0:T(8,128)(2,1)}, u32[]{:S(2)}) copy-start(bf16[384,1536]{1,0:T(8,128)(2,1)} %copy-done.25) | copy-start | bytes 3538948
  178.2 5.6 %copy-start.30 = (bf16[384,1536]{1,0:T(8,128)(2,1)S(1)}, bf16[384,1536]{1,0:T(8,128)(2,1)}, u32[]{:S(2)}) copy-start(bf16[384,1536]{1,0:T(8,128)(2,1)} %copy-done.28) | copy-start | bytes 3538948
  178.2 5.6 %copy-start.33 = (bf16[384,1536]{1,0:T(8,128)(2,1)S(1)}, bf16[384,1536]{1,0:T(8,128)(2,1)}, u32[]{:S(2)}) copy-start(bf16[384,1536]{1,0:T(8,128)(2,1)} %copy-done.31) | copy-start | bytes 3538948
  178.2 5.6 %copy-start.41 = (bf16[384,1536]{1,0:T(8,128)(2,1)S(1)}, bf16[384,1536]{1,0:T(8,128)(2,1)}, u32[]{:S(2)}) copy-start(bf16[384,1536]{1,0:T(8,128)(2,1)} %copy-done.39) | copy-start | bytes 3538948
  178.2 5.6 %copy-start.44 = (bf16[384,1536]{1,0:T(8,128)(2,1)S(1)}, bf16[384,1536]{1,0:T(8,128)(2,1)}, u32[]{:S(2)}) copy-start(bf16[384,1536]{1,0:T(8,128)(2,1)} %copy-done.42) | copy-start | bytes 3538948
  178.2 17.9 %collective-permute-start.15 = (bf16[256,1536]{1,0:T(8,128)(2,1)}, bf16[256,1536]{1,0:T(8,128)(2,1)S(1)}, u32[]{:S(2)}, u32[]{:S(2)}) collective-permute-start(bf16[256,1536]{1,0:T(8,128)(2,1)} %pad_maximum_fusion.2), channel_id=1, source_target_pairs={{0,16},{16,0},{32,48},{48,32},{64,80},{80,64},{96,112},{112,96},{1... | collective-permute-start | bytes 2359304 | tf_op jit(solution)/shard_map/ppermute | solution.py:36
  183.8 22.2 %copy-start = (bf16[512,1536]{1,0:T(8,128)(2,1)}, bf16[512,1536]{1,0:T(8,128)(2,1)S(1)}, u32[]{:S(2)}) copy-start(bf16[512,1536]{1,0:T(8,128)(2,1)S(1)} %shard_map.188.own_ref) | copy-start | bytes 4718596
  194.1 13.9 %copy-start.21 = (bf16[768,2176]{1,0:T(8,128)(2,1)}, bf16[768,2176]{1,0:T(8,128)(2,1)S(1)}, u32[]{:S(2)}) copy-start(bf16[768,2176]{1,0:T(8,128)(2,1)S(1)} %shard_map.187) | copy-start | bytes 10027012
  208.0 27.2 %collective-permute-start.16 = (bf16[384,1536]{1,0:T(8,128)(2,1)}, bf16[384,1536]{1,0:T(8,128)(2,1)}, u32[]{:S(2)}, u32[]{:S(2)}) collective-permute-start(bf16[384,1536]{1,0:T(8,128)(2,1)} %get-tuple-element.137), channel_id=1, source_target_pairs={{0,32},{16,48},{32,64},{48,80},{64,96},{80,112},{96,0},{112,16},{1... | collective-permute-start | bytes 3538952 | tf_op jit(solution)/shard_map/ppermute | solution.py:28
  208.0 27.2 %collective-permute-start.17 = (bf16[384,1536]{1,0:T(8,128)(2,1)}, bf16[384,1536]{1,0:T(8,128)(2,1)}, u32[]{:S(2)}, u32[]{:S(2)}) collective-permute-start(bf16[384,1536]{1,0:T(8,128)(2,1)} %get-tuple-element.138), channel_id=1, source_target_pairs={{0,96},{16,112},{32,0},{48,16},{64,32},{80,48},{96,64},{112,80},{1... | collective-permute-start | bytes 3538952 | tf_op jit(solution)/shard_map/ppermute | solution.py:32
  211.3 25.6 %collective-permute-start.18 = (bf16[384,1536]{1,0:T(8,128)(2,1)}, bf16[384,1536]{1,0:T(8,128)(2,1)}, u32[]{:S(2)}, u32[]{:S(2)}) collective-permute-start(bf16[384,1536]{1,0:T(8,128)(2,1)} %get-tuple-element.139), channel_id=1, source_target_pairs={{0,16},{16,0},{32,48},{48,32},{64,80},{80,64},{96,112},{112,96},{1... | collective-permute-start | bytes 3538952 | tf_op jit(solution)/shard_map/ppermute | solution.py:36
  213.1 52.8 %all-to-all-start.3 = ((bf16[8,96,2176]{2,1,0:T(8,128)(2,1)}), bf16[8,96,2176]{2,1,0:T(8,128)(2,1)}, u32[]{:S(2)}, u32[]{:S(2)}) async-start(bf16[8,96,2176]{2,1,0:T(8,128)(2,1)} %bitcast.75), calls=%async_computation.3 | async-start | bytes 6684672 | tf_op jit(solution)/shard_map/all_to_all | solution.py:62
  236.9 1.4 copy-start.1
  238.3 1.4 copy-start.4
  243.1 1.4 copy-start.16
  251.0 6.4 %copy-start.10 = (f32[1,96,2048]{2,1,0:T(8,128)S(1)}, f32[1,96,2048]{2,1,0:T(8,128)}, u32[]{:S(2)}) copy-start(f32[1,96,2048]{2,1,0:T(8,128)} %param.15) | copy-start | bytes 2359300
  251.0 6.4 %copy-start.12 = (f32[1,96,2048]{2,1,0:T(8,128)S(1)}, f32[1,96,2048]{2,1,0:T(8,128)}, u32[]{:S(2)}) copy-start(f32[1,96,2048]{2,1,0:T(8,128)} %param.17) | copy-start | bytes 2359300
  251.0 6.4 %copy-start.14 = (f32[1,96,2048]{2,1,0:T(8,128)S(1)}, f32[1,96,2048]{2,1,0:T(8,128)}, u32[]{:S(2)}) copy-start(f32[1,96,2048]{2,1,0:T(8,128)} %param.19) | copy-start | bytes 2359300
  251.0 25.7 %collective-permute-start.19 = (bf16[384,1536]{1,0:T(8,128)(2,1)}, bf16[384,1536]{1,0:T(8,128)(2,1)}, u32[]{:S(2)}, u32[]{:S(2)}) collective-permute-start(bf16[384,1536]{1,0:T(8,128)(2,1)} %shard_map.190.refs_0_), channel_id=1, source_target_pairs={{0,32},{16,48},{32,64},{48,80},{64,96},{80,112},{96,0},{112,16},{1... | collective-permute-start | bytes 3538952 | tf_op jit(solution)/shard_map/ppermute | solution.py:28
  251.1 25.7 %collective-permute-start.20 = (bf16[384,1536]{1,0:T(8,128)(2,1)}, bf16[384,1536]{1,0:T(8,128)(2,1)}, u32[]{:S(2)}, u32[]{:S(2)}) collective-permute-start(bf16[384,1536]{1,0:T(8,128)(2,1)} %shard_map.190.refs_0_), channel_id=1, source_target_pairs={{0,96},{16,112},{32,0},{48,16},{64,32},{80,48},{96,64},{112,80},{1... | collective-permute-start | bytes 3538952 | tf_op jit(solution)/shard_map/ppermute | solution.py:32
  254.3 23.9 %collective-permute-start.21 = (bf16[384,1536]{1,0:T(8,128)(2,1)}, bf16[384,1536]{1,0:T(8,128)(2,1)}, u32[]{:S(2)}, u32[]{:S(2)}) collective-permute-start(bf16[384,1536]{1,0:T(8,128)(2,1)} %shard_map.190.refs_0_), channel_id=1, source_target_pairs={{0,16},{16,0},{32,48},{48,32},{64,80},{80,64},{96,112},{112,96},{1... | collective-permute-start | bytes 3538952 | tf_op jit(solution)/shard_map/ppermute | solution.py:36
  257.3 2.0 copy-start.19
  257.4 2.6 copy-start.2
  257.5 3.1 copy-start.5
  257.5 3.6 %copy-start.17 = (f32[1,256,1536]{2,1,0:T(8,128)S(1)}, f32[1,256,1536]{2,1,0:T(8,128)}, u32[]{:S(2)}) copy-start(f32[1,256,1536]{2,1,0:T(8,128)} %param.16) | copy-start | bytes 4718596
  278.2 26.2 %collective-permute-start.22 = (bf16[384,1536]{1,0:T(8,128)(2,1)}, bf16[384,1536]{1,0:T(8,128)(2,1)S(1)}, u32[]{:S(2)}, u32[]{:S(2)}) collective-permute-start(bf16[384,1536]{1,0:T(8,128)(2,1)} %collective-permute-done.21.refs_1_), channel_id=1, source_target_pairs={{0,32},{16,48},{32,64},{48,80},{64,96},{80,112},{96,0},{112,16},{1... | collective-permute-start | bytes 3538952 | tf_op jit(solution)/shard_map/ppermute | solution.py:28
  278.2 26.2 %collective-permute-start.23 = (bf16[384,1536]{1,0:T(8,128)(2,1)}, bf16[384,1536]{1,0:T(8,128)(2,1)S(1)}, u32[]{:S(2)}, u32[]{:S(2)}) collective-permute-start(bf16[384,1536]{1,0:T(8,128)(2,1)} %collective-permute-done.21.refs_1_), channel_id=1, source_target_pairs={{0,96},{16,112},{32,0},{48,16},{64,32},{80,48},{96,64},{112,80},{1... | collective-permute-start | bytes 3538952 | tf_op jit(solution)/shard_map/ppermute | solution.py:32
  281.5 22.9 %collective-permute-start.24 = (bf16[256,2176]{1,0:T(8,128)(2,1)S(1)}, bf16[256,2176]{1,0:T(8,128)(2,1)S(1)}, u32[]{:S(2)}, u32[]{:S(2)}) collective-permute-start(bf16[256,2176]{1,0:T(8,128)(2,1)S(1)} %get-tuple-element.148), channel_id=1, source_target_pairs={{0,2},{1,3},{2,0},{3,1},{4,6},{5,7},{6,4},{7,5},{8,10},{9,11},{10,... | collective-permute-start | bytes 3342344 | tf_op jit(solution)/shard_map/ppermute | solution.py:58
  307.1 23.4 %collective-permute-start.25 = (bf16[384,1536]{1,0:T(8,128)(2,1)}, bf16[384,1536]{1,0:T(8,128)(2,1)S(1)}, u32[]{:S(2)}, u32[]{:S(2)}) collective-permute-start(bf16[384,1536]{1,0:T(8,128)(2,1)} %get-tuple-element.153), channel_id=1, source_target_pairs={{0,32},{16,48},{32,64},{48,80},{64,96},{80,112},{96,0},{112,16},{1... | collective-permute-start | bytes 3538952 | tf_op jit(solution)/shard_map/ppermute | solution.py:28
  307.1 23.3 %collective-permute-start.26 = (bf16[384,1536]{1,0:T(8,128)(2,1)}, bf16[384,1536]{1,0:T(8,128)(2,1)}, u32[]{:S(2)}, u32[]{:S(2)}) collective-permute-start(bf16[384,1536]{1,0:T(8,128)(2,1)} %get-tuple-element.154), channel_id=1, source_target_pairs={{0,96},{16,112},{32,0},{48,16},{64,32},{80,48},{96,64},{112,80},{1... | collective-permute-start | bytes 3538952 | tf_op jit(solution)/shard_map/ppermute | solution.py:32
  (24 other events, 27.2 us)
